TPU v7x, 256 devices: a whole 4x4x8 slice. The times are simulated.
256 devices in a mesh: row: 16 (over z_hi, y, core), col: 16 (over x, z_lo).
Axes of the slice: x: 4, y: 4, z: 8 (z_hi: 2, z_lo: 4; z = z_hi * 4 + z_lo), core: 2. Of those that a mesh axis runs over, the one named last changes fastest.
Arguments:
- amplitudes: bfloat16 [1024, 640, 640], P('col', None, 'row'), may hold values from -6 to 6
- integrals: bfloat16 [1536, 640, 640], P('col', 'row'), may hold values from -0.009765625 to 0.009765625
- owners: int32 [2], replicated, may hold values from 0 to 15
- offsets: int32 [2], replicated, may hold values from 0 to 32
Outputs:
- ladder_residual: float32 [1024, 128], P(('col', 'row'))
All inputs are finite; a program needn't handle non-finite values.
Results may differ from a plain program's by a relative error of at most 0.0003.
Values may be sent and summed in bfloat16 or wider, within the bound.
No kernel may reach another device: no remote copies, remote signals or barrier semaphores. Data moves between devices by JAX's collectives and lax.ppermute only.
A program may use at most 128 MiB of HBM per device.

v0:
```python
import jax
import jax.numpy as jnp
from jax import lax
from jax.sharding import PartitionSpec as P

PR = 64
STEPS = 2


def broadcast(array, axis, root):
    mine = lax.axis_index(axis) == root
    return lax.psum(jnp.where(mine, array, jnp.zeros_like(array)), axis)


def contract(flat, panel):
    rows = panel.reshape(panel.shape[0], -1)
    return lax.dot_general(flat, rows, (((1,), (1,)), ((), ())), preferred_element_type=jnp.float32)


def local(amplitudes, integrals, owners, offsets):
    regrouped = lax.all_to_all(amplitudes, "row", split_axis=1, concat_axis=2, tiled=True)
    flat = regrouped.reshape(regrouped.shape[0], -1)
    blocks = []
    for step in range(STEPS):
        local_panel = lax.dynamic_slice_in_dim(integrals, offsets[step], PR, 0)
        panel = broadcast(local_panel, "col", owners[step])
        block = contract(flat, panel)
        blocks.append(block)
    joined = jnp.concatenate(blocks, axis=1)
    joined = lax.psum_scatter(joined, "row", scatter_dimension=0, tiled=True)
    return joined


def solution(mesh):
    in_specs = (P("col", None, "row"), P("col", "row", None), P(), P())
    out_specs = P(("col", "row"), None)
    return jax.shard_map(local, mesh=mesh, in_specs=in_specs, out_specs=out_specs, check_vma=False)
```

profile of v0, /device:TPU:1, one launch (start us, length us, event | category | flops | bytes accessed | tf_op | source)
XLA Modules:
  0.0 491.2 jit_solution(773135430158131903)
XLA Ops:
  6.5 0.0 all-reduce.4.cloned.1.call-start
  6.5 1.4 fusion.1
  10.6 1.3 fusion
  14.5 3.5 dynamic-slice_select_fusion.1
  18.0 2.2 copy.9
  20.2 2.2 copy.10
  22.4 0.0 copy-start.1
  22.4 0.0 all-reduce.4.cloned.1.call-update
  22.4 1.9 copy-done.1
  24.3 12.2 %copy.7 = bf16[64,640,40]{0,2,1:T(8,128)(2,1)} copy(bf16[64,640,40]{1,2,0:T(8,128)(2,1)S(1)} %copy-done.1) | data formatting | bytes 6553600 | tf_op args[0]
  36.5 12.9 %reshape.14 = bf16[16,2,51200]{2,1,0:T(2,128)(2,1)} reshape(bf16[640,40,64]{2,1,0:T(8,128)(2,1)} %bitcast.26) | data formatting | bytes 6553600
  49.4 0.0 copy-start.3
  49.4 12.8 %all-to-all-start = ((bf16[16,2,51200]{2,1,0:T(2,128)(2,1)}), bf16[16,2,51200]{2,1,0:T(2,128)(2,1)S(1)}, u32[]{:S(2)}, u32[]{:S(2)}) async-start(bf16[16,2,51200]{2,1,0:T(2,128)(2,1)} %reshape.14), calls=%async_computation | async-start | bytes 6553600 | tf_op jit(solution)/shard_map/all_to_all | solution.py:21
  62.2 0.0 copy-done.3
  62.2 0.6 dynamic-slice
  63.4 95.1 %all-to-all-done = bf16[16,2,51200]{2,1,0:T(2,128)(2,1)S(1)} async-done(((bf16[16,2,51200]{2,1,0:T(2,128)(2,1)}), bf16[16,2,51200]{2,1,0:T(2,128)(2,1)S(1)}, u32[]{:S(2)}, u32[]{:S(2)}) %all-to-all-start) | async-done | bytes 3276832 | tf_op jit(solution)/shard_map/all_to_all | solution.py:21
  158.5 8.8 %reshape.15 = bf16[640,40,64]{2,1,0:T(8,128)(2,1)} reshape(bf16[16,2,51200]{2,1,0:T(2,128)(2,1)S(1)} %all-to-all-done) | data formatting | bytes 6553600
  167.4 7.5 %copy.8 = bf16[64,40,16,40]{0,3,2,1:T(8,128)(2,1)} copy(bf16[64,40,16,40]{0,3,1,2:T(8,128)(2,1)} %bitcast.25) | data formatting | bytes 6553600 | tf_op jit(solution)/shard_map/all_to_all | solution.py:21
  174.8 219.3 %all-reduce.4.cloned.1.call-done = (bf16[64,25600]{1,0:T(8,128)(2,1)}, bf16[64,25600]{1,0:T(8,128)(2,1)}) async-done(((bf16[64,25600]{1,0:T(8,128)(2,1)}, bf16[64,25600]{1,0:T(8,128)(2,1)}), (bf16[64,25600]{1,0:T(8,128)(2,1)}, bf16[64,25600]{1,0:T(8,128)(2,1)})) %all-reduce.4.cloned.1.call-update) | async-done | bytes 6553616 | tf_op jit(solution)/shard_map/psum | solution.py:12
  394.2 0.0 copy-start
  394.2 0.0 copy-start.2
  394.2 5.9 %convolution_bitcast_fusion = f32[64,64]{1,0:T(8,128)S(1)} fusion(bf16[64,25600]{1,0:T(8,128)(2,1)} %get-tuple-element.5, bf16[64,25600]{0,1:T(8,128)(2,1)} %bitcast.23), kind=kOutput, calls=%fused_computation.2 | convolution fusion | flops 209715200 | bytes 6569984 | tf_op jit(solution)/shard_map/dot_general | solution.py:17
  400.1 0.0 copy-done
  400.1 0.8 copy-done.2
  400.9 1.9 convolution_bitcast_fusion.1
  402.7 0.1 pad_maximum_fusion
  402.8 81.0 %all-reduce = f32[64,128]{1,0:T(8,128)S(1)} all-reduce(f32[64,128]{1,0:T(8,128)S(1)} %pad_maximum_fusion), channel_id=2, replica_groups=mesh['row'=16,'col'=16] {'row'}, use_global_device_ids=true, to_apply=%region_2.3.clone | all-reduce | flops 8192 | bytes 65536
  483.8 0.6 constant_dynamic-slice_fusion
Async XLA Ops:
  6.5 387.7 %all-reduce.4.cloned.1.call-start = ((), (), s32[]{:S(2)}) async-start(), calls=%async_computation.1 | async-start | bytes 13107200 | tf_op jit(solution)/shard_map/psum | solution.py:12
  22.4 1.9 copy-start.1
  49.4 12.8 %copy-start.3 = (u32[256]{0:T(256)S(1)}, u32[256]{0:T(256)}, u32[]{:S(2)}) copy-start(u32[256]{0:T(256)} %constant.14) | copy-start | bytes 3076
  49.4 109.1 %all-to-all-start = ((bf16[16,2,51200]{2,1,0:T(2,128)(2,1)}), bf16[16,2,51200]{2,1,0:T(2,128)(2,1)S(1)}, u32[]{:S(2)}, u32[]{:S(2)}) async-start(bf16[16,2,51200]{2,1,0:T(2,128)(2,1)} %reshape.14), calls=%async_computation | async-start | bytes 6553600 | tf_op jit(solution)/shard_map/all_to_all | solution.py:21
  394.2 5.9 %copy-start = (bf16[64,40,16,40]{0,3,2,1:T(8,128)(2,1)S(1)}, bf16[64,40,16,40]{0,3,2,1:T(8,128)(2,1)}, u32[]{:S(2)}) copy-start(bf16[64,40,16,40]{0,3,2,1:T(8,128)(2,1)} %copy.8) | copy-start | bytes 9830404
  394.2 6.7 %copy-start.2 = (bf16[64,25600]{1,0:T(8,128)(2,1)S(1)}, bf16[64,25600]{1,0:T(8,128)(2,1)}, u32[]{:S(2)}) copy-start(bf16[64,25600]{1,0:T(8,128)(2,1)} %get-tuple-element.6) | copy-start | bytes 9830404
Sparse Core Ops, SparseCore 0:
  22.5 371.6 all-reduce.3
where the time goes:
time: 498 us; the launch traced here: 491 us
  waiting for transfers between devices  315 us (63%)
  blocking collectives  81 us (16%)
  local copies, waits for them, and re-layouts  52.4 us (11%)
  between operations  19.3 us (4%)
  starting transfers between devices  12.8 us (3%)
  matrix products  7.72 us (2%)
    psum x1, waiting for transfers between devices, broadcast(): return lax.psum(jnp.where(mine, array, jnp.zeros_like(array)), axis)  219 us
    all_to_all x1, waiting for transfers between devices, local(): lax.all_to_all(amplitudes, 'row', split_axis=1, concat_axis=2, tiled=True)  95.1 us
    unnamed x1, blocking collectives  81 us
    unnamed x15, local copies, waits for them, and re-layouts  42.2 us
    all_to_all x1, starting transfers between devices, local(): lax.all_to_all(amplitudes, 'row', split_axis=1, concat_axis=2, tiled=True)  12.8 us
  transfers between devices with their start and end apart: 2, of which 2 were waited for; matrix products, arithmetic and copies ran while one was open for 9% of the time, Pallas kernels for 0%

commit v1 on v0

v1 whole, which is shorter than its diff:
```python
import functools

import jax
import jax.numpy as jnp
from jax import lax
from jax.experimental import pallas as pl
from jax.experimental.pallas import tpu as pltpu
from jax.sharding import PartitionSpec as P

PR = 64
STEPS = 2
X = 4
ZL = 4
COL = 16
ROW = 16
BLOCK = 40
HALF = 20
PAIRS = 64
LANES = 128


def turned(ref):
    stacked = jnp.concatenate([ref[0, 0], ref[1, 0]], axis=0)
    return stacked.T.reshape(16, BLOCK, LANES)


def panel_kernel(in_ref, *out_refs):
    tiles = turned(in_ref)
    for row in range(ROW):
        out_refs[row][0] = tiles[row]


def amplitude_kernel(place_ref, in_ref, *refs):
    out_refs, held = refs[:X], refs[X]
    held[...] = turned(in_ref)
    x, zl = place_ref[0], place_ref[1]
    for kx in range(X):
        for kz in range(ZL):
            block = lax.rem(x + kx, X) * ZL + lax.rem(zl + kz, ZL)
            out_refs[kx][kz, 0] = held[block]


def turn_panel(swapped):
    piece = jax.ShapeDtypeStruct((HALF, BLOCK, LANES), jnp.bfloat16)
    return pl.pallas_call(
        panel_kernel,
        grid=(HALF,),
        in_specs=[pl.BlockSpec((2, 1, 64, 640), lambda i: (0, i, 0, 0))],
        out_specs=[pl.BlockSpec((1, BLOCK, LANES), lambda i: (i, 0, 0))] * ROW,
        out_shape=[piece] * ROW,
        compiler_params=pltpu.CompilerParams(vmem_limit_bytes=24 * 2**20),
        cost_estimate=pl.CostEstimate(flops=0, bytes_accessed=2 * 64 * 25600 * 2, transcendentals=0),
    )(swapped.reshape(2, HALF, 64, 640))


def turn_amplitudes(swapped, place):
    piece = jax.ShapeDtypeStruct((ZL, HALF, BLOCK, LANES), jnp.bfloat16)
    return pl.pallas_call(
        amplitude_kernel,
        grid_spec=pltpu.PrefetchScalarGridSpec(
            num_scalar_prefetch=1,
            grid=(HALF,),
            in_specs=[pl.BlockSpec((2, 1, 64, 640), lambda i, place: (0, i, 0, 0))],
            out_specs=[pl.BlockSpec((ZL, 1, BLOCK, LANES), lambda i, place: (0, i, 0, 0))] * X,
            scratch_shapes=[pltpu.VMEM((16, BLOCK, LANES), jnp.bfloat16)],
        ),
        out_shape=[piece] * X,
        compiler_params=pltpu.CompilerParams(vmem_limit_bytes=24 * 2**20),
        cost_estimate=pl.CostEstimate(flops=0, bytes_accessed=2 * 64 * 25600 * 2, transcendentals=0),
    )(place, swapped.reshape(2, HALF, 64, 640))


def contract_kernel(*refs):
    left, right, out_ref = refs[:X], refs[X : X + ZL], refs[X + ZL]
    for kx in range(X):
        total = jnp.zeros((LANES, 2 * LANES), jnp.float32)
        for kz in range(ZL):
            total += lax.dot_general(
                left[kx][kz], right[kz][...], (((0,), (0,)), ((), ())), preferred_element_type=jnp.float32
            )
        out_ref[kx] = total[:PAIRS, :LANES] + total[PAIRS:, LANES:]


def contract(left, right):
    depth = HALF * BLOCK
    left = [part.reshape(ZL, depth, LANES) for part in left]
    right = [part.reshape(depth, 2 * LANES) for part in right]
    return pl.pallas_call(
        contract_kernel,
        in_specs=[pl.BlockSpec(memory_space=pltpu.VMEM)] * (X + ZL),
        out_specs=pl.BlockSpec(memory_space=pltpu.VMEM),
        out_shape=jax.ShapeDtypeStruct((X, PAIRS, LANES), jnp.float32),
        compiler_params=pltpu.CompilerParams(vmem_limit_bytes=32 * 2**20),
        cost_estimate=pl.CostEstimate(flops=2 * 512 * 3200 * 256, bytes_accessed=5 * 2**20, transcendentals=0),
    )(*left, *right)


def shift_x(array, k):
    return lax.ppermute(array, "col", [(x * ZL + z, (x + k) % X * ZL + z) for x in range(X) for z in range(ZL)])


def shift_zl(array, k):
    return lax.ppermute(array, "col", [(x * ZL + z, x * ZL + (z - k) % ZL) for x in range(X) for z in range(ZL)])


def scatter_from(owner, *pieces):
    total = None
    for row in range(ROW):
        pairs = [(source * COL + owner, row * COL + source) for source in range(ROW)]
        got = lax.ppermute(pieces[row], ("row", "col"), pairs)
        total = got if total is None else total + got
    return total


def scatter(owner, pieces):
    return lax.switch(owner, [functools.partial(scatter_from, o) for o in range(COL)], *pieces)


def local(amplitudes, integrals, owners, offsets):
    col = lax.axis_index("col")
    place = jnp.stack([col // ZL, col % ZL]).astype(jnp.int32)
    pieces = []
    for step in range(STEPS):
        panel = lax.dynamic_slice_in_dim(integrals, offsets[step], PR, 0)
        pieces.append(turn_panel(jnp.transpose(panel, (1, 0, 2))))
    left = turn_amplitudes(jnp.transpose(amplitudes, (2, 0, 1)), place)
    left = [left[0]] + [shift_x(left[k], k) for k in range(1, X)]
    got = jnp.stack([scatter(owners[step], pieces[step]) for step in range(STEPS)])
    got = got.reshape(STEPS, HALF, 2, HALF, 2, PR)
    mine = jnp.transpose(got, (3, 4, 1, 2, 0, 5)).reshape(HALF, BLOCK, 2 * LANES)
    right = [mine] + [shift_zl(mine, k) for k in range(1, ZL)]
    part = contract(left, right)
    total = part[0]
    for k in range(1, X):
        total = total + shift_x(part[k], -k)
    spread = lax.all_to_all(total.reshape(ROW, PAIRS // ROW, LANES), "row", 0, 0, tiled=True)
    return jnp.sum(spread, axis=0)


def solution(mesh):
    in_specs = (P("col", None, "row"), P("col", "row", None), P(), P())
    out_specs = P(("col", "row"), None)
    return jax.shard_map(local, mesh=mesh, in_specs=in_specs, out_specs=out_specs, check_vma=False)
```

time: 498 us -> 655 us (1.32)
  starting transfers between devices: 12.8 us -> 529 us
  waiting for transfers between devices: 315 us -> 20.5 us
  blocking collectives: 81 us -> 21.3 us
  local copies, waits for them, and re-layouts: 52.4 us -> 18.4 us
  Pallas kernels: 0 us -> 26.8 us
  loops' own time: 0 us -> 20.6 us
  between operations: 19.3 us -> 5.66 us
  matrix products: 7.72 us -> 0 us
    ppermute x0 -> x41, starting transfers between devices: none -> 529 us  [the longest x32 417 us: scatter_from(): got = lax.ppermute(pieces[row], ('row', 'col'), pairs)]
    psum x1 -> x0, waiting for transfers between devices: 219 us -> none  [broadcast(): return lax.psum(jnp.where(mine, array, jnp.zeros_like(array)), axis)]
    all_to_all x1 -> x0, waiting for transfers between devices: 95.1 us -> none  [local(): lax.all_to_all(amplitudes, 'row', split_axis=1, concat_axis=2, tiled=True)]
    unnamed x1 -> x0, blocking collectives: 81 us -> none
    unnamed x15 -> x54, local copies, waits for them, and re-layouts: 42.2 us -> 3.66 us
    pallas_call x0 -> x4, Pallas kernels: none -> 26.8 us  [the longest x2 15.9 us: turn_panel(): pl.pallas_call(panel_kernel, grid=(HALF,), in_specs=[pl.BlockSpec((2, 1,...]
    all_to_all x0 -> x1, blocking collectives: none -> 21.3 us  [local(): lax.all_to_all(total.reshape(ROW, PAIRS // ROW, LANES), 'row', 0, 0, tile...]
    another operation x0 -> x2, loops' own time: none -> 20.6 us  [scatter(): lax.switch(owner, [functools.partial(scatter_from, o) for o in range(COL)...]
  transfers between devices with their start and end apart: 2 -> 41, of which waited for: 2 -> 3; matrix products, arithmetic and copies ran while one was open for 9% -> 1% of each run, Pallas kernels for 0% -> 0%
where the time goes in v1:
time: 655 us; the launch traced here: 645 us
  starting transfers between devices  529 us (81%)
  Pallas kernels  26.8 us (4%)
  blocking collectives  21.3 us (3%)
  loops' own time  20.6 us (3%)
  waiting for transfers between devices  20.5 us (3%)
  local copies, waits for them, and re-layouts  18.4 us (3%)
    ppermute x32, starting transfers between devices, scatter_from(): got = lax.ppermute(pieces[row], ('row', 'col'), pairs)  417 us
    ppermute x6, starting transfers between devices, shift_x(): lax.ppermute(array, 'col', [(x * ZL + z, (x + k) % X * ZL + z) for x in r...  76.1 us
    ppermute x3, starting transfers between devices, shift_zl(): lax.ppermute(array, 'col', [(x * ZL + z, x * ZL + (z - k) % ZL) for x in...  35.5 us
    all_to_all x1, blocking collectives, local(): lax.all_to_all(total.reshape(ROW, PAIRS // ROW, LANES), 'row', 0, 0, tile...  21.3 us
    another operation x2, loops' own time, scatter(): lax.switch(owner, [functools.partial(scatter_from, o) for o in range(COL)...  20.6 us
    ppermute x3, waiting for transfers between devices, shift_zl(): lax.ppermute(array, 'col', [(x * ZL + z, x * ZL + (z - k) % ZL) for x in...  16.3 us
    pallas_call x2, Pallas kernels, turn_panel(): pl.pallas_call(panel_kernel, grid=(HALF,), in_specs=[pl.BlockSpec((2, 1,...  15.9 us
  transfers between devices with their start and end apart: 41, of which 3 were waited for; matrix products, arithmetic and copies ran while one was open for 1% of the time, Pallas kernels for 0%

profile of v1, /device:TPU:1, one launch (start us, length us, event | category | flops | bytes accessed | tf_op | source)
XLA Modules:
  0.0 644.9 jit_solution(17831859559761643850)
XLA Ops:
  14.3 8.0 %shard_map.47 = (bf16[20,40,128]{2,1,0:T(8,128)(2,1)}, bf16[20,40,128]{2,1,0:T(8,128)(2,1)}, bf16[20,40,128]{2,1,0:T(8,128)(2,1)}, bf16[20,40,128]{2,1,0:T(8,128...) custom-call(bf16[2,20,64,640]{3,2,1,0:T(8,128)(2,1)S(1)} %bitcast.39), custom_call_target="tpu_custom_call" | custom-call | bytes 6553600 | tf_op jit(solution)/shard_map/pallas_call | solution.py:45
  22.9 7.9 %shard_map.48 = (bf16[20,40,128]{2,1,0:T(8,128)(2,1)S(1)}, bf16[20,40,128]{2,1,0:T(8,128)(2,1)}, bf16[20,40,128]{2,1,0:T(8,128)(2,1)}, bf16[20,40,128]{2,1,0:T(8...) custom-call(bf16[2,20,64,640]{3,2,1,0:T(8,128)(2,1)S(1)} %bitcast.40), custom_call_target="tpu_custom_call" | custom-call | bytes 6553600 | tf_op jit(solution)/shard_map/pallas_call | solution.py:45
  31.1 8.3 %shard_map.46 = (bf16[4,20,40,128]{3,2,1,0:T(8,128)(2,1)S(1)}, bf16[4,20,40,128]{3,2,1,0:T(8,128)(2,1)}, bf16[4,20,40,128]{3,2,1,0:T(8,128)(2,1)S(1)}, bf16[4,20,40,128]{3,2,1,0:T(8,128)(2,1)S(1)}) custom-call(s32[2]{0:T(128)S(1)} %pad_add_fusion.place_ref, bf16[2,20,64,640]{3,2,1,0:T(8,128)(2,1)S(1)} %bitcast.38), custom_call_target="tpu_custom_call" | custom-call | bytes 6553600 | tf_op jit(solution)/shard_map/pallas_call | solution.py:58
  42.2 213.1 %conditional.2 = (bf16[1,20,2,20,2,64]{5,4,3,2,1,0:T(2,128)(2,1)S(1)}) conditional(s32[]{:T(128)} %bitcast.8, (bf16[20,40,128]{2,1,0:T(8,128)(2,1)S(1)}, bf16[20,40,128]{2,1,0:T(8,128)(2,1)S(1)}, bf16[20,40,128]{2,1,0:T(8,128)(2,1)S(1)}, bf16[20,40,128]{2,1,0:T(8,128)(2,1)S(1)}, bf16[20,40,128]{2,1,0:T(8,128)(2,1)S(1)}, ...), branch_computations={%region_0.1_spmd, %region_1.2_spmd, %region_2.3_spmd, %region_3.4_... | conditional | flops 1536000 | bytes 16999048 | solution.py:116
  52.5 14.4 %collective-permute-start.144 = (bf16[20,40,128]{2,1,0:T(8,128)(2,1)S(1)}, bf16[20,40,128]{2,1,0:T(8,128)(2,1)S(1)}, u32[]{:S(2)}, u32[]{:S(2)}) collective-permute-start(bf16[20,40,128]{2,1,0:T(8,128)(2,1)S(1)} %get-tuple-element.1209), channel_id=1, source_target_pairs={{9,0},{25,1},{41,2},{57,3},{73,4},{89,5},{105,6},{121,7},{137,8},{... | collective-permute-start | bytes 614408 | tf_op jit(solution)/shard_map/cond/branch_9_fun/ppermute | solution.py:110
  66.9 12.5 %collective-permute-start.145 = (bf16[20,40,128]{2,1,0:T(8,128)(2,1)S(1)}, bf16[20,40,128]{2,1,0:T(8,128)(2,1)S(1)}, u32[]{:S(2)}, u32[]{:S(2)}) collective-permute-start(bf16[20,40,128]{2,1,0:T(8,128)(2,1)S(1)} %get-tuple-element.1210), channel_id=1, source_target_pairs={{9,16},{25,17},{41,18},{57,19},{73,20},{89,21},{105,22},{121,23},{... | collective-permute-start | bytes 614408 | tf_op jit(solution)/shard_map/cond/branch_9_fun/ppermute | solution.py:110
  79.4 12.5 %collective-permute-start.146 = (bf16[20,40,128]{2,1,0:T(8,128)(2,1)S(1)}, bf16[20,40,128]{2,1,0:T(8,128)(2,1)S(1)}, u32[]{:S(2)}, u32[]{:S(2)}) collective-permute-start(bf16[20,40,128]{2,1,0:T(8,128)(2,1)S(1)} %get-tuple-element.1211), channel_id=1, source_target_pairs={{9,32},{25,33},{41,34},{57,35},{73,36},{89,37},{105,38},{121,39},{... | collective-permute-start | bytes 614408 | tf_op jit(solution)/shard_map/cond/branch_9_fun/ppermute | solution.py:110
  91.9 12.5 %collective-permute-start.147 = (bf16[20,40,128]{2,1,0:T(8,128)(2,1)S(1)}, bf16[20,40,128]{2,1,0:T(8,128)(2,1)S(1)}, u32[]{:S(2)}, u32[]{:S(2)}) collective-permute-start(bf16[20,40,128]{2,1,0:T(8,128)(2,1)S(1)} %get-tuple-element.1212), channel_id=1, source_target_pairs={{9,48},{25,49},{41,50},{57,51},{73,52},{89,53},{105,54},{121,55},{... | collective-permute-start | bytes 614408 | tf_op jit(solution)/shard_map/cond/branch_9_fun/ppermute | solution.py:110
  104.4 12.5 %collective-permute-start.148 = (bf16[20,40,128]{2,1,0:T(8,128)(2,1)S(1)}, bf16[20,40,128]{2,1,0:T(8,128)(2,1)S(1)}, u32[]{:S(2)}, u32[]{:S(2)}) collective-permute-start(bf16[20,40,128]{2,1,0:T(8,128)(2,1)S(1)} %get-tuple-element.1213), channel_id=1, source_target_pairs={{9,64},{25,65},{41,66},{57,67},{73,68},{89,69},{105,70},{121,71},{... | collective-permute-start | bytes 614408 | tf_op jit(solution)/shard_map/cond/branch_9_fun/ppermute | solution.py:110
  117.0 12.5 %collective-permute-start.149 = (bf16[20,40,128]{2,1,0:T(8,128)(2,1)S(1)}, bf16[20,40,128]{2,1,0:T(8,128)(2,1)S(1)}, u32[]{:S(2)}, u32[]{:S(2)}) collective-permute-start(bf16[20,40,128]{2,1,0:T(8,128)(2,1)S(1)} %get-tuple-element.1214), channel_id=1, source_target_pairs={{9,80},{25,81},{41,82},{57,83},{73,84},{89,85},{105,86},{121,87},{... | collective-permute-start | bytes 614408 | tf_op jit(solution)/shard_map/cond/branch_9_fun/ppermute | solution.py:110
  129.5 12.5 %collective-permute-start.150 = (bf16[20,40,128]{2,1,0:T(8,128)(2,1)S(1)}, bf16[20,40,128]{2,1,0:T(8,128)(2,1)S(1)}, u32[]{:S(2)}, u32[]{:S(2)}) collective-permute-start(bf16[20,40,128]{2,1,0:T(8,128)(2,1)S(1)} %get-tuple-element.1215), channel_id=1, source_target_pairs={{9,96},{25,97},{41,98},{57,99},{73,100},{89,101},{105,102},{121,10... | collective-permute-start | bytes 614408 | tf_op jit(solution)/shard_map/cond/branch_9_fun/ppermute | solution.py:110
  142.0 12.5 %collective-permute-start.151 = (bf16[20,40,128]{2,1,0:T(8,128)(2,1)S(1)}, bf16[20,40,128]{2,1,0:T(8,128)(2,1)S(1)}, u32[]{:S(2)}, u32[]{:S(2)}) collective-permute-start(bf16[20,40,128]{2,1,0:T(8,128)(2,1)S(1)} %get-tuple-element.1216), channel_id=1, source_target_pairs={{9,112},{25,113},{41,114},{57,115},{73,116},{89,117},{105,118},{12... | collective-permute-start | bytes 614408 | tf_op jit(solution)/shard_map/cond/branch_9_fun/ppermute | solution.py:110
  154.5 12.5 %collective-permute-start.152 = (bf16[20,40,128]{2,1,0:T(8,128)(2,1)S(1)}, bf16[20,40,128]{2,1,0:T(8,128)(2,1)S(1)}, u32[]{:S(2)}, u32[]{:S(2)}) collective-permute-start(bf16[20,40,128]{2,1,0:T(8,128)(2,1)S(1)} %get-tuple-element.1217), channel_id=1, source_target_pairs={{9,128},{25,129},{41,130},{57,131},{73,132},{89,133},{105,134},{12... | collective-permute-start | bytes 614408 | tf_op jit(solution)/shard_map/cond/branch_9_fun/ppermute | solution.py:110
  167.0 12.5 %collective-permute-start.153 = (bf16[20,40,128]{2,1,0:T(8,128)(2,1)S(1)}, bf16[20,40,128]{2,1,0:T(8,128)(2,1)S(1)}, u32[]{:S(2)}, u32[]{:S(2)}) collective-permute-start(bf16[20,40,128]{2,1,0:T(8,128)(2,1)S(1)} %get-tuple-element.1218), channel_id=1, source_target_pairs={{9,144},{25,145},{41,146},{57,147},{73,148},{89,149},{105,150},{12... | collective-permute-start | bytes 614408 | tf_op jit(solution)/shard_map/cond/branch_9_fun/ppermute | solution.py:110
  179.6 12.5 %collective-permute-start.154 = (bf16[20,40,128]{2,1,0:T(8,128)(2,1)S(1)}, bf16[20,40,128]{2,1,0:T(8,128)(2,1)S(1)}, u32[]{:S(2)}, u32[]{:S(2)}) collective-permute-start(bf16[20,40,128]{2,1,0:T(8,128)(2,1)S(1)} %get-tuple-element.1219), channel_id=1, source_target_pairs={{9,160},{25,161},{41,162},{57,163},{73,164},{89,165},{105,166},{12... | collective-permute-start | bytes 614408 | tf_op jit(solution)/shard_map/cond/branch_9_fun/ppermute | solution.py:110
  192.1 12.5 %collective-permute-start.155 = (bf16[20,40,128]{2,1,0:T(8,128)(2,1)S(1)}, bf16[20,40,128]{2,1,0:T(8,128)(2,1)S(1)}, u32[]{:S(2)}, u32[]{:S(2)}) collective-permute-start(bf16[20,40,128]{2,1,0:T(8,128)(2,1)S(1)} %get-tuple-element.1220), channel_id=1, source_target_pairs={{9,176},{25,177},{41,178},{57,179},{73,180},{89,181},{105,182},{12... | collective-permute-start | bytes 614408 | tf_op jit(solution)/shard_map/cond/branch_9_fun/ppermute | solution.py:110
  204.6 12.5 %collective-permute-start.156 = (bf16[20,40,128]{2,1,0:T(8,128)(2,1)S(1)}, bf16[20,40,128]{2,1,0:T(8,128)(2,1)S(1)}, u32[]{:S(2)}, u32[]{:S(2)}) collective-permute-start(bf16[20,40,128]{2,1,0:T(8,128)(2,1)S(1)} %get-tuple-element.1221), channel_id=1, source_target_pairs={{9,192},{25,193},{41,194},{57,195},{73,196},{89,197},{105,198},{12... | collective-permute-start | bytes 614408 | tf_op jit(solution)/shard_map/cond/branch_9_fun/ppermute | solution.py:110
  217.1 12.5 %collective-permute-start.157 = (bf16[20,40,128]{2,1,0:T(8,128)(2,1)S(1)}, bf16[20,40,128]{2,1,0:T(8,128)(2,1)S(1)}, u32[]{:S(2)}, u32[]{:S(2)}) collective-permute-start(bf16[20,40,128]{2,1,0:T(8,128)(2,1)S(1)} %get-tuple-element.1222), channel_id=1, source_target_pairs={{9,208},{25,209},{41,210},{57,211},{73,212},{89,213},{105,214},{12... | collective-permute-start | bytes 614408 | tf_op jit(solution)/shard_map/cond/branch_9_fun/ppermute | solution.py:110
  229.6 12.5 %collective-permute-start.158 = (bf16[20,40,128]{2,1,0:T(8,128)(2,1)S(1)}, bf16[20,40,128]{2,1,0:T(8,128)(2,1)S(1)}, u32[]{:S(2)}, u32[]{:S(2)}) collective-permute-start(bf16[20,40,128]{2,1,0:T(8,128)(2,1)S(1)} %get-tuple-element.1223), channel_id=1, source_target_pairs={{9,224},{25,225},{41,226},{57,227},{73,228},{89,229},{105,230},{12... | collective-permute-start | bytes 614408 | tf_op jit(solution)/shard_map/cond/branch_9_fun/ppermute | solution.py:110
  242.1 12.5 %collective-permute-start.159 = (bf16[20,40,128]{2,1,0:T(8,128)(2,1)S(1)}, bf16[20,40,128]{2,1,0:T(8,128)(2,1)S(1)}, u32[]{:S(2)}, u32[]{:S(2)}) collective-permute-start(bf16[20,40,128]{2,1,0:T(8,128)(2,1)S(1)} %get-tuple-element.1224), channel_id=1, source_target_pairs={{9,240},{25,241},{41,242},{57,243},{73,244},{89,245},{105,246},{12... | collective-permute-start | bytes 614408 | tf_op jit(solution)/shard_map/cond/branch_9_fun/ppermute | solution.py:110
  255.4 225.8 %conditional.3 = (bf16[1,20,2,20,2,64]{5,4,3,2,1,0:T(2,128)(2,1)S(1)}) conditional(s32[]{:T(128)} %bitcast.12, (bf16[20,40,128]{2,1,0:T(8,128)(2,1)S(1)}, bf16[20,40,128]{2,1,0:T(8,128)(2,1)S(1)}, bf16[20,40,128]{2,1,0:T(8,128)(2,1)S(1)}, bf16[20,40,128]{2,1,0:T(8,128)(2,1)S(1)}, bf16[20,40,128]{2,1,0:T(8,128)(2,1)S(1)}, ...), branch_computations={%region_16.17_spmd, %region_17.18_spmd, %region_18.19_spmd, %regio... | conditional | flops 1536000 | bytes 16999048 | solution.py:116
  265.0 18.3 %collective-permute-start.384 = (bf16[20,40,128]{2,1,0:T(8,128)(2,1)S(1)}, bf16[20,40,128]{2,1,0:T(8,128)(2,1)S(1)}, u32[]{:S(2)}, u32[]{:S(2)}) collective-permute-start(bf16[20,40,128]{2,1,0:T(8,128)(2,1)S(1)} %get-tuple-element.1449), channel_id=1, source_target_pairs={{8,0},{24,1},{40,2},{56,3},{72,4},{88,5},{104,6},{120,7},{136,8},{... | collective-permute-start | bytes 614408 | tf_op jit(solution)/shard_map/cond/branch_8_fun/ppermute | solution.py:110
  283.3 13.1 %collective-permute-start.385 = (bf16[20,40,128]{2,1,0:T(8,128)(2,1)S(1)}, bf16[20,40,128]{2,1,0:T(8,128)(2,1)S(1)}, u32[]{:S(2)}, u32[]{:S(2)}) collective-permute-start(bf16[20,40,128]{2,1,0:T(8,128)(2,1)S(1)} %get-tuple-element.1450), channel_id=1, source_target_pairs={{8,16},{24,17},{40,18},{56,19},{72,20},{88,21},{104,22},{120,23},{... | collective-permute-start | bytes 614408 | tf_op jit(solution)/shard_map/cond/branch_8_fun/ppermute | solution.py:110
  296.5 13.2 %collective-permute-start.386 = (bf16[20,40,128]{2,1,0:T(8,128)(2,1)S(1)}, bf16[20,40,128]{2,1,0:T(8,128)(2,1)S(1)}, u32[]{:S(2)}, u32[]{:S(2)}) collective-permute-start(bf16[20,40,128]{2,1,0:T(8,128)(2,1)S(1)} %get-tuple-element.1451), channel_id=1, source_target_pairs={{8,32},{24,33},{40,34},{56,35},{72,36},{88,37},{104,38},{120,39},{... | collective-permute-start | bytes 614408 | tf_op jit(solution)/shard_map/cond/branch_8_fun/ppermute | solution.py:110
  309.6 13.1 %collective-permute-start.387 = (bf16[20,40,128]{2,1,0:T(8,128)(2,1)S(1)}, bf16[20,40,128]{2,1,0:T(8,128)(2,1)S(1)}, u32[]{:S(2)}, u32[]{:S(2)}) collective-permute-start(bf16[20,40,128]{2,1,0:T(8,128)(2,1)S(1)} %get-tuple-element.1452), channel_id=1, source_target_pairs={{8,48},{24,49},{40,50},{56,51},{72,52},{88,53},{104,54},{120,55},{... | collective-permute-start | bytes 614408 | tf_op jit(solution)/shard_map/cond/branch_8_fun/ppermute | solution.py:110
  322.8 13.1 %collective-permute-start.388 = (bf16[20,40,128]{2,1,0:T(8,128)(2,1)S(1)}, bf16[20,40,128]{2,1,0:T(8,128)(2,1)S(1)}, u32[]{:S(2)}, u32[]{:S(2)}) collective-permute-start(bf16[20,40,128]{2,1,0:T(8,128)(2,1)S(1)} %get-tuple-element.1453), channel_id=1, source_target_pairs={{8,64},{24,65},{40,66},{56,67},{72,68},{88,69},{104,70},{120,71},{... | collective-permute-start | bytes 614408 | tf_op jit(solution)/shard_map/cond/branch_8_fun/ppermute | solution.py:110
  335.9 13.1 %collective-permute-start.389 = (bf16[20,40,128]{2,1,0:T(8,128)(2,1)S(1)}, bf16[20,40,128]{2,1,0:T(8,128)(2,1)S(1)}, u32[]{:S(2)}, u32[]{:S(2)}) collective-permute-start(bf16[20,40,128]{2,1,0:T(8,128)(2,1)S(1)} %get-tuple-element.1454), channel_id=1, source_target_pairs={{8,80},{24,81},{40,82},{56,83},{72,84},{88,85},{104,86},{120,87},{... | collective-permute-start | bytes 614408 | tf_op jit(solution)/shard_map/cond/branch_8_fun/ppermute | solution.py:110
  349.0 13.1 %collective-permute-start.390 = (bf16[20,40,128]{2,1,0:T(8,128)(2,1)S(1)}, bf16[20,40,128]{2,1,0:T(8,128)(2,1)S(1)}, u32[]{:S(2)}, u32[]{:S(2)}) collective-permute-start(bf16[20,40,128]{2,1,0:T(8,128)(2,1)S(1)} %get-tuple-element.1455), channel_id=1, source_target_pairs={{8,96},{24,97},{40,98},{56,99},{72,100},{88,101},{104,102},{120,10... | collective-permute-start | bytes 614408 | tf_op jit(solution)/shard_map/cond/branch_8_fun/ppermute | solution.py:110
  362.2 13.1 %collective-permute-start.391 = (bf16[20,40,128]{2,1,0:T(8,128)(2,1)}, bf16[20,40,128]{2,1,0:T(8,128)(2,1)S(1)}, u32[]{:S(2)}, u32[]{:S(2)}) collective-permute-start(bf16[20,40,128]{2,1,0:T(8,128)(2,1)} %get-tuple-element.1456), channel_id=1, source_target_pairs={{8,112},{24,113},{40,114},{56,115},{72,116},{88,117},{104,118},{12... | collective-permute-start | bytes 614408 | tf_op jit(solution)/shard_map/cond/branch_8_fun/ppermute | solution.py:110
  375.3 13.1 %collective-permute-start.392 = (bf16[20,40,128]{2,1,0:T(8,128)(2,1)}, bf16[20,40,128]{2,1,0:T(8,128)(2,1)S(1)}, u32[]{:S(2)}, u32[]{:S(2)}) collective-permute-start(bf16[20,40,128]{2,1,0:T(8,128)(2,1)} %get-tuple-element.1457), channel_id=1, source_target_pairs={{8,128},{24,129},{40,130},{56,131},{72,132},{88,133},{104,134},{12... | collective-permute-start | bytes 614408 | tf_op jit(solution)/shard_map/cond/branch_8_fun/ppermute | solution.py:110
  388.5 13.1 %collective-permute-start.393 = (bf16[20,40,128]{2,1,0:T(8,128)(2,1)}, bf16[20,40,128]{2,1,0:T(8,128)(2,1)S(1)}, u32[]{:S(2)}, u32[]{:S(2)}) collective-permute-start(bf16[20,40,128]{2,1,0:T(8,128)(2,1)} %get-tuple-element.1458), channel_id=1, source_target_pairs={{8,144},{24,145},{40,146},{56,147},{72,148},{88,149},{104,150},{12... | collective-permute-start | bytes 614408 | tf_op jit(solution)/shard_map/cond/branch_8_fun/ppermute | solution.py:110
  401.6 13.1 %collective-permute-start.394 = (bf16[20,40,128]{2,1,0:T(8,128)(2,1)}, bf16[20,40,128]{2,1,0:T(8,128)(2,1)S(1)}, u32[]{:S(2)}, u32[]{:S(2)}) collective-permute-start(bf16[20,40,128]{2,1,0:T(8,128)(2,1)} %get-tuple-element.1459), channel_id=1, source_target_pairs={{8,160},{24,161},{40,162},{56,163},{72,164},{88,165},{104,166},{12... | collective-permute-start | bytes 614408 | tf_op jit(solution)/shard_map/cond/branch_8_fun/ppermute | solution.py:110
  414.8 13.1 %collective-permute-start.395 = (bf16[20,40,128]{2,1,0:T(8,128)(2,1)}, bf16[20,40,128]{2,1,0:T(8,128)(2,1)S(1)}, u32[]{:S(2)}, u32[]{:S(2)}) collective-permute-start(bf16[20,40,128]{2,1,0:T(8,128)(2,1)} %get-tuple-element.1460), channel_id=1, source_target_pairs={{8,176},{24,177},{40,178},{56,179},{72,180},{88,181},{104,182},{12... | collective-permute-start | bytes 614408 | tf_op jit(solution)/shard_map/cond/branch_8_fun/ppermute | solution.py:110
  427.9 13.1 %collective-permute-start.396 = (bf16[20,40,128]{2,1,0:T(8,128)(2,1)}, bf16[20,40,128]{2,1,0:T(8,128)(2,1)S(1)}, u32[]{:S(2)}, u32[]{:S(2)}) collective-permute-start(bf16[20,40,128]{2,1,0:T(8,128)(2,1)} %get-tuple-element.1461), channel_id=1, source_target_pairs={{8,192},{24,193},{40,194},{56,195},{72,196},{88,197},{104,198},{12... | collective-permute-start | bytes 614408 | tf_op jit(solution)/shard_map/cond/branch_8_fun/ppermute | solution.py:110
  441.1 13.1 %collective-permute-start.397 = (bf16[20,40,128]{2,1,0:T(8,128)(2,1)}, bf16[20,40,128]{2,1,0:T(8,128)(2,1)S(1)}, u32[]{:S(2)}, u32[]{:S(2)}) collective-permute-start(bf16[20,40,128]{2,1,0:T(8,128)(2,1)} %get-tuple-element.1462), channel_id=1, source_target_pairs={{8,208},{24,209},{40,210},{56,211},{72,212},{88,213},{104,214},{12... | collective-permute-start | bytes 614408 | tf_op jit(solution)/shard_map/cond/branch_8_fun/ppermute | solution.py:110
  454.2 13.1 %collective-permute-start.398 = (bf16[20,40,128]{2,1,0:T(8,128)(2,1)}, bf16[20,40,128]{2,1,0:T(8,128)(2,1)S(1)}, u32[]{:S(2)}, u32[]{:S(2)}) collective-permute-start(bf16[20,40,128]{2,1,0:T(8,128)(2,1)} %get-tuple-element.1463), channel_id=1, source_target_pairs={{8,224},{24,225},{40,226},{56,227},{72,228},{88,229},{104,230},{12... | collective-permute-start | bytes 614408 | tf_op jit(solution)/shard_map/cond/branch_8_fun/ppermute | solution.py:110
  467.4 13.1 %collective-permute-start.399 = (bf16[20,40,128]{2,1,0:T(8,128)(2,1)}, bf16[20,40,128]{2,1,0:T(8,128)(2,1)S(1)}, u32[]{:S(2)}, u32[]{:S(2)}) collective-permute-start(bf16[20,40,128]{2,1,0:T(8,128)(2,1)} %get-tuple-element.1464), channel_id=1, source_target_pairs={{8,240},{24,241},{40,242},{56,243},{72,244},{88,245},{104,246},{12... | collective-permute-start | bytes 614408 | tf_op jit(solution)/shard_map/cond/branch_8_fun/ppermute | solution.py:110
  481.2 18.6 %collective-permute-start.512 = (bf16[4,20,40,128]{3,2,1,0:T(8,128)(2,1)}, bf16[4,20,40,128]{3,2,1,0:T(8,128)(2,1)S(1)}, u32[]{:S(2)}, u32[]{:S(2)}) collective-permute-start(bf16[4,20,40,128]{3,2,1,0:T(8,128)(2,1)} %get-tuple-element.1582), channel_id=1, source_target_pairs={{0,4},{1,5},{2,6},{3,7},{4,8},{5,9},{6,10},{7,11},{8,12},{9,13},{1... | collective-permute-start | bytes 2457608 | tf_op jit(solution)/shard_map/ppermute | solution.py:99
  504.2 11.8 %collective-permute-start.517 = (bf16[20,40,256]{2,1,0:T(8,128)(2,1)}, bf16[20,40,256]{2,1,0:T(8,128)(2,1)S(1)}, u32[]{:S(2)}, u32[]{:S(2)}) collective-permute-start(bf16[20,40,256]{2,1,0:T(8,128)(2,1)} %reshape.86), channel_id=1, source_target_pairs={{0,1},{1,2},{2,3},{3,0},{4,5},{5,6},{6,7},{7,4},{8,9},{9,10},{10,1... | collective-permute-start | bytes 1228808 | tf_op jit(solution)/shard_map/ppermute | solution.py:103
  516.0 11.8 %collective-permute-start.513 = (bf16[4,20,40,128]{3,2,1,0:T(8,128)(2,1)}, bf16[4,20,40,128]{3,2,1,0:T(8,128)(2,1)S(1)}, u32[]{:S(2)}, u32[]{:S(2)}) collective-permute-start(bf16[4,20,40,128]{3,2,1,0:T(8,128)(2,1)} %copy-done.3), channel_id=1, source_target_pairs={{0,8},{1,9},{2,10},{3,11},{4,12},{5,13},{6,14},{7,15},{8,0},{9,1},... | collective-permute-start | bytes 2457608 | tf_op jit(solution)/shard_map/ppermute | solution.py:99
  527.9 11.8 %collective-permute-start.514 = (bf16[4,20,40,128]{3,2,1,0:T(8,128)(2,1)}, bf16[4,20,40,128]{3,2,1,0:T(8,128)(2,1)}, u32[]{:S(2)}, u32[]{:S(2)}) collective-permute-start(bf16[4,20,40,128]{3,2,1,0:T(8,128)(2,1)} %copy-done.2), channel_id=1, source_target_pairs={{0,12},{1,13},{2,14},{3,15},{4,0},{5,1},{6,2},{7,3},{8,4},{9,5},{1... | collective-permute-start | bytes 2457608 | tf_op jit(solution)/shard_map/ppermute | solution.py:99
  539.7 11.8 %collective-permute-start.516 = (bf16[20,40,256]{2,1,0:T(8,128)(2,1)}, bf16[20,40,256]{2,1,0:T(8,128)(2,1)}, u32[]{:S(2)}, u32[]{:S(2)}) collective-permute-start(bf16[20,40,256]{2,1,0:T(8,128)(2,1)} %reshape.86), channel_id=1, source_target_pairs={{0,2},{1,3},{2,0},{3,1},{4,6},{5,7},{6,4},{7,5},{8,10},{9,11},{10,... | collective-permute-start | bytes 1228808 | tf_op jit(solution)/shard_map/ppermute | solution.py:103
  551.6 11.8 %collective-permute-start.515 = (bf16[20,40,256]{2,1,0:T(8,128)(2,1)}, bf16[20,40,256]{2,1,0:T(8,128)(2,1)}, u32[]{:S(2)}, u32[]{:S(2)}) collective-permute-start(bf16[20,40,256]{2,1,0:T(8,128)(2,1)} %reshape.86), channel_id=1, source_target_pairs={{0,3},{1,0},{2,1},{3,2},{4,7},{5,4},{6,5},{7,6},{8,11},{9,8},{10,9... | collective-permute-start | bytes 1228808 | tf_op jit(solution)/shard_map/ppermute | solution.py:103
  572.9 9.2 %collective-permute-done.515 = bf16[20,40,256]{2,1,0:T(8,128)(2,1)} collective-permute-done((bf16[20,40,256]{2,1,0:T(8,128)(2,1)}, bf16[20,40,256]{2,1,0:T(8,128)(2,1)}, u32[]{:S(2)}, u32[]{:S(2)}) %collective-permute-start.515) | collective-permute-done | bytes 409632 | tf_op jit(solution)/shard_map/ppermute | solution.py:103
  584.8 10.2 %collective-permute-start.518 = (f32[64,128]{1,0:T(8,128)S(1)}, f32[64,128]{1,0:T(8,128)S(1)}, u32[]{:S(2)}, u32[]{:S(2)}) collective-permute-start(f32[64,128]{1,0:T(8,128)S(1)} %get-tuple-element.1587), channel_id=1, source_target_pairs={{0,12},{1,13},{2,14},{3,15},{4,0},{5,1},{6,2},{7,3},{8,4},{9,5},{1... | collective-permute-start | bytes 98312 | tf_op jit(solution)/shard_map/ppermute | solution.py:99
  595.0 11.8 %collective-permute-start.520 = (f32[64,128]{1,0:T(8,128)S(1)}, f32[64,128]{1,0:T(8,128)S(1)}, u32[]{:S(2)}, u32[]{:S(2)}) collective-permute-start(f32[64,128]{1,0:T(8,128)S(1)} %get-tuple-element.1588), channel_id=1, source_target_pairs={{0,4},{1,5},{2,6},{3,7},{4,8},{5,9},{6,10},{7,11},{8,12},{9,13},{1... | collective-permute-start | bytes 98312 | tf_op jit(solution)/shard_map/ppermute | solution.py:99
  606.8 11.8 %collective-permute-start.519 = (f32[64,128]{1,0:T(8,128)S(1)}, f32[64,128]{1,0:T(8,128)S(1)}, u32[]{:S(2)}, u32[]{:S(2)}) collective-permute-start(f32[64,128]{1,0:T(8,128)S(1)} %get-tuple-element.1589), channel_id=1, source_target_pairs={{0,8},{1,9},{2,10},{3,11},{4,12},{5,13},{6,14},{7,15},{8,0},{9,1},... | collective-permute-start | bytes 98312 | tf_op jit(solution)/shard_map/ppermute | solution.py:99
  622.8 21.3 %all_to_all.5 = f32[16,4,128]{2,1,0:T(4,128)S(1)} all-to-all(f32[16,4,128]{2,1,0:T(4,128)S(1)} %bitcast.46), channel_id=1, replica_groups=mesh['row'=16,'col'=16] {'row'}, dimensions={0} | all-to-all | bytes 65536 | tf_op jit(solution)/shard_map/all_to_all | solution.py:136
  (113 shorter events, 35.0 us)
Async XLA Ops:
  42.2 213.2 %copy-start.5 = (bf16[20,40,128]{2,1,0:T(8,128)(2,1)S(1)}, bf16[20,40,128]{2,1,0:T(8,128)(2,1)}, u32[]{:S(2)}) copy-start(bf16[20,40,128]{2,1,0:T(8,128)(2,1)} %get-tuple-element.2136) | copy-start | bytes 614404
  42.2 213.2 %copy-start.6 = (bf16[20,40,128]{2,1,0:T(8,128)(2,1)S(1)}, bf16[20,40,128]{2,1,0:T(8,128)(2,1)}, u32[]{:S(2)}) copy-start(bf16[20,40,128]{2,1,0:T(8,128)(2,1)} %get-tuple-element.2138) | copy-start | bytes 614404
  42.2 213.2 %copy-start.7 = (bf16[20,40,128]{2,1,0:T(8,128)(2,1)S(1)}, bf16[20,40,128]{2,1,0:T(8,128)(2,1)}, u32[]{:S(2)}) copy-start(bf16[20,40,128]{2,1,0:T(8,128)(2,1)} %get-tuple-element.2139) | copy-start | bytes 614404
  42.2 213.2 %copy-start.8 = (bf16[20,40,128]{2,1,0:T(8,128)(2,1)S(1)}, bf16[20,40,128]{2,1,0:T(8,128)(2,1)}, u32[]{:S(2)}) copy-start(bf16[20,40,128]{2,1,0:T(8,128)(2,1)} %get-tuple-element.2140) | copy-start | bytes 614404
  42.2 213.2 %copy-start.9 = (bf16[20,40,128]{2,1,0:T(8,128)(2,1)S(1)}, bf16[20,40,128]{2,1,0:T(8,128)(2,1)}, u32[]{:S(2)}) copy-start(bf16[20,40,128]{2,1,0:T(8,128)(2,1)} %get-tuple-element.2141) | copy-start | bytes 614404
  42.2 213.2 %copy-start.10 = (bf16[20,40,128]{2,1,0:T(8,128)(2,1)S(1)}, bf16[20,40,128]{2,1,0:T(8,128)(2,1)}, u32[]{:S(2)}) copy-start(bf16[20,40,128]{2,1,0:T(8,128)(2,1)} %get-tuple-element.2142) | copy-start | bytes 614404
  52.5 64.5 %collective-permute-start.144 = (bf16[20,40,128]{2,1,0:T(8,128)(2,1)S(1)}, bf16[20,40,128]{2,1,0:T(8,128)(2,1)S(1)}, u32[]{:S(2)}, u32[]{:S(2)}) collective-permute-start(bf16[20,40,128]{2,1,0:T(8,128)(2,1)S(1)} %get-tuple-element.1209), channel_id=1, source_target_pairs={{9,0},{25,1},{41,2},{57,3},{73,4},{89,5},{105,6},{121,7},{137,8},{... | collective-permute-start | bytes 614408 | tf_op jit(solution)/shard_map/cond/branch_9_fun/ppermute | solution.py:110
  66.9 62.6 %collective-permute-start.145 = (bf16[20,40,128]{2,1,0:T(8,128)(2,1)S(1)}, bf16[20,40,128]{2,1,0:T(8,128)(2,1)S(1)}, u32[]{:S(2)}, u32[]{:S(2)}) collective-permute-start(bf16[20,40,128]{2,1,0:T(8,128)(2,1)S(1)} %get-tuple-element.1210), channel_id=1, source_target_pairs={{9,16},{25,17},{41,18},{57,19},{73,20},{89,21},{105,22},{121,23},{... | collective-permute-start | bytes 614408 | tf_op jit(solution)/shard_map/cond/branch_9_fun/ppermute | solution.py:110
  79.4 62.6 %collective-permute-start.146 = (bf16[20,40,128]{2,1,0:T(8,128)(2,1)S(1)}, bf16[20,40,128]{2,1,0:T(8,128)(2,1)S(1)}, u32[]{:S(2)}, u32[]{:S(2)}) collective-permute-start(bf16[20,40,128]{2,1,0:T(8,128)(2,1)S(1)} %get-tuple-element.1211), channel_id=1, source_target_pairs={{9,32},{25,33},{41,34},{57,35},{73,36},{89,37},{105,38},{121,39},{... | collective-permute-start | bytes 614408 | tf_op jit(solution)/shard_map/cond/branch_9_fun/ppermute | solution.py:110
  91.9 62.6 %collective-permute-start.147 = (bf16[20,40,128]{2,1,0:T(8,128)(2,1)S(1)}, bf16[20,40,128]{2,1,0:T(8,128)(2,1)S(1)}, u32[]{:S(2)}, u32[]{:S(2)}) collective-permute-start(bf16[20,40,128]{2,1,0:T(8,128)(2,1)S(1)} %get-tuple-element.1212), channel_id=1, source_target_pairs={{9,48},{25,49},{41,50},{57,51},{73,52},{89,53},{105,54},{121,55},{... | collective-permute-start | bytes 614408 | tf_op jit(solution)/shard_map/cond/branch_9_fun/ppermute | solution.py:110
  104.4 62.6 %collective-permute-start.148 = (bf16[20,40,128]{2,1,0:T(8,128)(2,1)S(1)}, bf16[20,40,128]{2,1,0:T(8,128)(2,1)S(1)}, u32[]{:S(2)}, u32[]{:S(2)}) collective-permute-start(bf16[20,40,128]{2,1,0:T(8,128)(2,1)S(1)} %get-tuple-element.1213), channel_id=1, source_target_pairs={{9,64},{25,65},{41,66},{57,67},{73,68},{89,69},{105,70},{121,71},{... | collective-permute-start | bytes 614408 | tf_op jit(solution)/shard_map/cond/branch_9_fun/ppermute | solution.py:110
  117.0 62.6 %collective-permute-start.149 = (bf16[20,40,128]{2,1,0:T(8,128)(2,1)S(1)}, bf16[20,40,128]{2,1,0:T(8,128)(2,1)S(1)}, u32[]{:S(2)}, u32[]{:S(2)}) collective-permute-start(bf16[20,40,128]{2,1,0:T(8,128)(2,1)S(1)} %get-tuple-element.1214), channel_id=1, source_target_pairs={{9,80},{25,81},{41,82},{57,83},{73,84},{89,85},{105,86},{121,87},{... | collective-permute-start | bytes 614408 | tf_op jit(solution)/shard_map/cond/branch_9_fun/ppermute | solution.py:110
  129.5 62.6 %collective-permute-start.150 = (bf16[20,40,128]{2,1,0:T(8,128)(2,1)S(1)}, bf16[20,40,128]{2,1,0:T(8,128)(2,1)S(1)}, u32[]{:S(2)}, u32[]{:S(2)}) collective-permute-start(bf16[20,40,128]{2,1,0:T(8,128)(2,1)S(1)} %get-tuple-element.1215), channel_id=1, source_target_pairs={{9,96},{25,97},{41,98},{57,99},{73,100},{89,101},{105,102},{121,10... | collective-permute-start | bytes 614408 | tf_op jit(solution)/shard_map/cond/branch_9_fun/ppermute | solution.py:110
  142.0 62.6 %collective-permute-start.151 = (bf16[20,40,128]{2,1,0:T(8,128)(2,1)S(1)}, bf16[20,40,128]{2,1,0:T(8,128)(2,1)S(1)}, u32[]{:S(2)}, u32[]{:S(2)}) collective-permute-start(bf16[20,40,128]{2,1,0:T(8,128)(2,1)S(1)} %get-tuple-element.1216), channel_id=1, source_target_pairs={{9,112},{25,113},{41,114},{57,115},{73,116},{89,117},{105,118},{12... | collective-permute-start | bytes 614408 | tf_op jit(solution)/shard_map/cond/branch_9_fun/ppermute | solution.py:110
  154.5 62.6 %collective-permute-start.152 = (bf16[20,40,128]{2,1,0:T(8,128)(2,1)S(1)}, bf16[20,40,128]{2,1,0:T(8,128)(2,1)S(1)}, u32[]{:S(2)}, u32[]{:S(2)}) collective-permute-start(bf16[20,40,128]{2,1,0:T(8,128)(2,1)S(1)} %get-tuple-element.1217), channel_id=1, source_target_pairs={{9,128},{25,129},{41,130},{57,131},{73,132},{89,133},{105,134},{12... | collective-permute-start | bytes 614408 | tf_op jit(solution)/shard_map/cond/branch_9_fun/ppermute | solution.py:110
  167.0 62.6 %collective-permute-start.153 = (bf16[20,40,128]{2,1,0:T(8,128)(2,1)S(1)}, bf16[20,40,128]{2,1,0:T(8,128)(2,1)S(1)}, u32[]{:S(2)}, u32[]{:S(2)}) collective-permute-start(bf16[20,40,128]{2,1,0:T(8,128)(2,1)S(1)} %get-tuple-element.1218), channel_id=1, source_target_pairs={{9,144},{25,145},{41,146},{57,147},{73,148},{89,149},{105,150},{12... | collective-permute-start | bytes 614408 | tf_op jit(solution)/shard_map/cond/branch_9_fun/ppermute | solution.py:110
  179.6 62.6 %collective-permute-start.154 = (bf16[20,40,128]{2,1,0:T(8,128)(2,1)S(1)}, bf16[20,40,128]{2,1,0:T(8,128)(2,1)S(1)}, u32[]{:S(2)}, u32[]{:S(2)}) collective-permute-start(bf16[20,40,128]{2,1,0:T(8,128)(2,1)S(1)} %get-tuple-element.1219), channel_id=1, source_target_pairs={{9,160},{25,161},{41,162},{57,163},{73,164},{89,165},{105,166},{12... | collective-permute-start | bytes 614408 | tf_op jit(solution)/shard_map/cond/branch_9_fun/ppermute | solution.py:110
  192.1 62.6 %collective-permute-start.155 = (bf16[20,40,128]{2,1,0:T(8,128)(2,1)S(1)}, bf16[20,40,128]{2,1,0:T(8,128)(2,1)S(1)}, u32[]{:S(2)}, u32[]{:S(2)}) collective-permute-start(bf16[20,40,128]{2,1,0:T(8,128)(2,1)S(1)} %get-tuple-element.1220), channel_id=1, source_target_pairs={{9,176},{25,177},{41,178},{57,179},{73,180},{89,181},{105,182},{12... | collective-permute-start | bytes 614408 | tf_op jit(solution)/shard_map/cond/branch_9_fun/ppermute | solution.py:110
  204.6 50.1 %collective-permute-start.156 = (bf16[20,40,128]{2,1,0:T(8,128)(2,1)S(1)}, bf16[20,40,128]{2,1,0:T(8,128)(2,1)S(1)}, u32[]{:S(2)}, u32[]{:S(2)}) collective-permute-start(bf16[20,40,128]{2,1,0:T(8,128)(2,1)S(1)} %get-tuple-element.1221), channel_id=1, source_target_pairs={{9,192},{25,193},{41,194},{57,195},{73,196},{89,197},{105,198},{12... | collective-permute-start | bytes 614408 | tf_op jit(solution)/shard_map/cond/branch_9_fun/ppermute | solution.py:110
  217.1 37.6 %collective-permute-start.157 = (bf16[20,40,128]{2,1,0:T(8,128)(2,1)S(1)}, bf16[20,40,128]{2,1,0:T(8,128)(2,1)S(1)}, u32[]{:S(2)}, u32[]{:S(2)}) collective-permute-start(bf16[20,40,128]{2,1,0:T(8,128)(2,1)S(1)} %get-tuple-element.1222), channel_id=1, source_target_pairs={{9,208},{25,209},{41,210},{57,211},{73,212},{89,213},{105,214},{12... | collective-permute-start | bytes 614408 | tf_op jit(solution)/shard_map/cond/branch_9_fun/ppermute | solution.py:110
  229.6 25.1 %collective-permute-start.158 = (bf16[20,40,128]{2,1,0:T(8,128)(2,1)S(1)}, bf16[20,40,128]{2,1,0:T(8,128)(2,1)S(1)}, u32[]{:S(2)}, u32[]{:S(2)}) collective-permute-start(bf16[20,40,128]{2,1,0:T(8,128)(2,1)S(1)} %get-tuple-element.1223), channel_id=1, source_target_pairs={{9,224},{25,225},{41,226},{57,227},{73,228},{89,229},{105,230},{12... | collective-permute-start | bytes 614408 | tf_op jit(solution)/shard_map/cond/branch_9_fun/ppermute | solution.py:110
  242.1 12.6 %collective-permute-start.159 = (bf16[20,40,128]{2,1,0:T(8,128)(2,1)S(1)}, bf16[20,40,128]{2,1,0:T(8,128)(2,1)S(1)}, u32[]{:S(2)}, u32[]{:S(2)}) collective-permute-start(bf16[20,40,128]{2,1,0:T(8,128)(2,1)S(1)} %get-tuple-element.1224), channel_id=1, source_target_pairs={{9,240},{25,241},{41,242},{57,243},{73,244},{89,245},{105,246},{12... | collective-permute-start | bytes 614408 | tf_op jit(solution)/shard_map/cond/branch_9_fun/ppermute | solution.py:110
  265.0 70.9 %collective-permute-start.384 = (bf16[20,40,128]{2,1,0:T(8,128)(2,1)S(1)}, bf16[20,40,128]{2,1,0:T(8,128)(2,1)S(1)}, u32[]{:S(2)}, u32[]{:S(2)}) collective-permute-start(bf16[20,40,128]{2,1,0:T(8,128)(2,1)S(1)} %get-tuple-element.1449), channel_id=1, source_target_pairs={{8,0},{24,1},{40,2},{56,3},{72,4},{88,5},{104,6},{120,7},{136,8},{... | collective-permute-start | bytes 614408 | tf_op jit(solution)/shard_map/cond/branch_8_fun/ppermute | solution.py:110
  283.3 65.7 %collective-permute-start.385 = (bf16[20,40,128]{2,1,0:T(8,128)(2,1)S(1)}, bf16[20,40,128]{2,1,0:T(8,128)(2,1)S(1)}, u32[]{:S(2)}, u32[]{:S(2)}) collective-permute-start(bf16[20,40,128]{2,1,0:T(8,128)(2,1)S(1)} %get-tuple-element.1450), channel_id=1, source_target_pairs={{8,16},{24,17},{40,18},{56,19},{72,20},{88,21},{104,22},{120,23},{... | collective-permute-start | bytes 614408 | tf_op jit(solution)/shard_map/cond/branch_8_fun/ppermute | solution.py:110
  296.5 65.7 %collective-permute-start.386 = (bf16[20,40,128]{2,1,0:T(8,128)(2,1)S(1)}, bf16[20,40,128]{2,1,0:T(8,128)(2,1)S(1)}, u32[]{:S(2)}, u32[]{:S(2)}) collective-permute-start(bf16[20,40,128]{2,1,0:T(8,128)(2,1)S(1)} %get-tuple-element.1451), channel_id=1, source_target_pairs={{8,32},{24,33},{40,34},{56,35},{72,36},{88,37},{104,38},{120,39},{... | collective-permute-start | bytes 614408 | tf_op jit(solution)/shard_map/cond/branch_8_fun/ppermute | solution.py:110
  309.6 65.7 %collective-permute-start.387 = (bf16[20,40,128]{2,1,0:T(8,128)(2,1)S(1)}, bf16[20,40,128]{2,1,0:T(8,128)(2,1)S(1)}, u32[]{:S(2)}, u32[]{:S(2)}) collective-permute-start(bf16[20,40,128]{2,1,0:T(8,128)(2,1)S(1)} %get-tuple-element.1452), channel_id=1, source_target_pairs={{8,48},{24,49},{40,50},{56,51},{72,52},{88,53},{104,54},{120,55},{... | collective-permute-start | bytes 614408 | tf_op jit(solution)/shard_map/cond/branch_8_fun/ppermute | solution.py:110
  322.8 65.7 %collective-permute-start.388 = (bf16[20,40,128]{2,1,0:T(8,128)(2,1)S(1)}, bf16[20,40,128]{2,1,0:T(8,128)(2,1)S(1)}, u32[]{:S(2)}, u32[]{:S(2)}) collective-permute-start(bf16[20,40,128]{2,1,0:T(8,128)(2,1)S(1)} %get-tuple-element.1453), channel_id=1, source_target_pairs={{8,64},{24,65},{40,66},{56,67},{72,68},{88,69},{104,70},{120,71},{... | collective-permute-start | bytes 614408 | tf_op jit(solution)/shard_map/cond/branch_8_fun/ppermute | solution.py:110
  335.9 65.7 %collective-permute-start.389 = (bf16[20,40,128]{2,1,0:T(8,128)(2,1)S(1)}, bf16[20,40,128]{2,1,0:T(8,128)(2,1)S(1)}, u32[]{:S(2)}, u32[]{:S(2)}) collective-permute-start(bf16[20,40,128]{2,1,0:T(8,128)(2,1)S(1)} %get-tuple-element.1454), channel_id=1, source_target_pairs={{8,80},{24,81},{40,82},{56,83},{72,84},{88,85},{104,86},{120,87},{... | collective-permute-start | bytes 614408 | tf_op jit(solution)/shard_map/cond/branch_8_fun/ppermute | solution.py:110
  349.0 65.7 %collective-permute-start.390 = (bf16[20,40,128]{2,1,0:T(8,128)(2,1)S(1)}, bf16[20,40,128]{2,1,0:T(8,128)(2,1)S(1)}, u32[]{:S(2)}, u32[]{:S(2)}) collective-permute-start(bf16[20,40,128]{2,1,0:T(8,128)(2,1)S(1)} %get-tuple-element.1455), channel_id=1, source_target_pairs={{8,96},{24,97},{40,98},{56,99},{72,100},{88,101},{104,102},{120,10... | collective-permute-start | bytes 614408 | tf_op jit(solution)/shard_map/cond/branch_8_fun/ppermute | solution.py:110
  362.2 65.7 %collective-permute-start.391 = (bf16[20,40,128]{2,1,0:T(8,128)(2,1)}, bf16[20,40,128]{2,1,0:T(8,128)(2,1)S(1)}, u32[]{:S(2)}, u32[]{:S(2)}) collective-permute-start(bf16[20,40,128]{2,1,0:T(8,128)(2,1)} %get-tuple-element.1456), channel_id=1, source_target_pairs={{8,112},{24,113},{40,114},{56,115},{72,116},{88,117},{104,118},{12... | collective-permute-start | bytes 614408 | tf_op jit(solution)/shard_map/cond/branch_8_fun/ppermute | solution.py:110
  375.3 65.7 %collective-permute-start.392 = (bf16[20,40,128]{2,1,0:T(8,128)(2,1)}, bf16[20,40,128]{2,1,0:T(8,128)(2,1)S(1)}, u32[]{:S(2)}, u32[]{:S(2)}) collective-permute-start(bf16[20,40,128]{2,1,0:T(8,128)(2,1)} %get-tuple-element.1457), channel_id=1, source_target_pairs={{8,128},{24,129},{40,130},{56,131},{72,132},{88,133},{104,134},{12... | collective-permute-start | bytes 614408 | tf_op jit(solution)/shard_map/cond/branch_8_fun/ppermute | solution.py:110
  388.5 65.7 %collective-permute-start.393 = (bf16[20,40,128]{2,1,0:T(8,128)(2,1)}, bf16[20,40,128]{2,1,0:T(8,128)(2,1)S(1)}, u32[]{:S(2)}, u32[]{:S(2)}) collective-permute-start(bf16[20,40,128]{2,1,0:T(8,128)(2,1)} %get-tuple-element.1458), channel_id=1, source_target_pairs={{8,144},{24,145},{40,146},{56,147},{72,148},{88,149},{104,150},{12... | collective-permute-start | bytes 614408 | tf_op jit(solution)/shard_map/cond/branch_8_fun/ppermute | solution.py:110
  401.6 65.7 %collective-permute-start.394 = (bf16[20,40,128]{2,1,0:T(8,128)(2,1)}, bf16[20,40,128]{2,1,0:T(8,128)(2,1)S(1)}, u32[]{:S(2)}, u32[]{:S(2)}) collective-permute-start(bf16[20,40,128]{2,1,0:T(8,128)(2,1)} %get-tuple-element.1459), channel_id=1, source_target_pairs={{8,160},{24,161},{40,162},{56,163},{72,164},{88,165},{104,166},{12... | collective-permute-start | bytes 614408 | tf_op jit(solution)/shard_map/cond/branch_8_fun/ppermute | solution.py:110
  414.8 65.7 %collective-permute-start.395 = (bf16[20,40,128]{2,1,0:T(8,128)(2,1)}, bf16[20,40,128]{2,1,0:T(8,128)(2,1)S(1)}, u32[]{:S(2)}, u32[]{:S(2)}) collective-permute-start(bf16[20,40,128]{2,1,0:T(8,128)(2,1)} %get-tuple-element.1460), channel_id=1, source_target_pairs={{8,176},{24,177},{40,178},{56,179},{72,180},{88,181},{104,182},{12... | collective-permute-start | bytes 614408 | tf_op jit(solution)/shard_map/cond/branch_8_fun/ppermute | solution.py:110
  427.9 52.6 %collective-permute-start.396 = (bf16[20,40,128]{2,1,0:T(8,128)(2,1)}, bf16[20,40,128]{2,1,0:T(8,128)(2,1)S(1)}, u32[]{:S(2)}, u32[]{:S(2)}) collective-permute-start(bf16[20,40,128]{2,1,0:T(8,128)(2,1)} %get-tuple-element.1461), channel_id=1, source_target_pairs={{8,192},{24,193},{40,194},{56,195},{72,196},{88,197},{104,198},{12... | collective-permute-start | bytes 614408 | tf_op jit(solution)/shard_map/cond/branch_8_fun/ppermute | solution.py:110
  441.1 39.4 %collective-permute-start.397 = (bf16[20,40,128]{2,1,0:T(8,128)(2,1)}, bf16[20,40,128]{2,1,0:T(8,128)(2,1)S(1)}, u32[]{:S(2)}, u32[]{:S(2)}) collective-permute-start(bf16[20,40,128]{2,1,0:T(8,128)(2,1)} %get-tuple-element.1462), channel_id=1, source_target_pairs={{8,208},{24,209},{40,210},{56,211},{72,212},{88,213},{104,214},{12... | collective-permute-start | bytes 614408 | tf_op jit(solution)/shard_map/cond/branch_8_fun/ppermute | solution.py:110
  454.2 26.3 %collective-permute-start.398 = (bf16[20,40,128]{2,1,0:T(8,128)(2,1)}, bf16[20,40,128]{2,1,0:T(8,128)(2,1)S(1)}, u32[]{:S(2)}, u32[]{:S(2)}) collective-permute-start(bf16[20,40,128]{2,1,0:T(8,128)(2,1)} %get-tuple-element.1463), channel_id=1, source_target_pairs={{8,224},{24,225},{40,226},{56,227},{72,228},{88,229},{104,230},{12... | collective-permute-start | bytes 614408 | tf_op jit(solution)/shard_map/cond/branch_8_fun/ppermute | solution.py:110
  467.4 13.2 %collective-permute-start.399 = (bf16[20,40,128]{2,1,0:T(8,128)(2,1)}, bf16[20,40,128]{2,1,0:T(8,128)(2,1)S(1)}, u32[]{:S(2)}, u32[]{:S(2)}) collective-permute-start(bf16[20,40,128]{2,1,0:T(8,128)(2,1)} %get-tuple-element.1464), channel_id=1, source_target_pairs={{8,240},{24,241},{40,242},{56,243},{72,244},{88,245},{104,246},{12... | collective-permute-start | bytes 614408 | tf_op jit(solution)/shard_map/cond/branch_8_fun/ppermute | solution.py:110
  481.2 100.9 %copy-start.1 = (bf16[4,20,40,128]{3,2,1,0:T(8,128)(2,1)S(1)}, bf16[4,20,40,128]{3,2,1,0:T(8,128)(2,1)}, u32[]{:S(2)}) copy-start(bf16[4,20,40,128]{3,2,1,0:T(8,128)(2,1)} %copy-done) | copy-start | bytes 2457604
  481.2 100.9 %collective-permute-start.512 = (bf16[4,20,40,128]{3,2,1,0:T(8,128)(2,1)}, bf16[4,20,40,128]{3,2,1,0:T(8,128)(2,1)S(1)}, u32[]{:S(2)}, u32[]{:S(2)}) collective-permute-start(bf16[4,20,40,128]{3,2,1,0:T(8,128)(2,1)} %get-tuple-element.1582), channel_id=1, source_target_pairs={{0,4},{1,5},{2,6},{3,7},{4,8},{5,9},{6,10},{7,11},{8,12},{9,13},{1... | collective-permute-start | bytes 2457608 | tf_op jit(solution)/shard_map/ppermute | solution.py:99
  504.2 47.4 %collective-permute-start.517 = (bf16[20,40,256]{2,1,0:T(8,128)(2,1)}, bf16[20,40,256]{2,1,0:T(8,128)(2,1)S(1)}, u32[]{:S(2)}, u32[]{:S(2)}) collective-permute-start(bf16[20,40,256]{2,1,0:T(8,128)(2,1)} %reshape.86), channel_id=1, source_target_pairs={{0,1},{1,2},{2,3},{3,0},{4,5},{5,6},{6,7},{7,4},{8,9},{9,10},{10,1... | collective-permute-start | bytes 1228808 | tf_op jit(solution)/shard_map/ppermute | solution.py:103
  516.0 66.0 %collective-permute-start.513 = (bf16[4,20,40,128]{3,2,1,0:T(8,128)(2,1)}, bf16[4,20,40,128]{3,2,1,0:T(8,128)(2,1)S(1)}, u32[]{:S(2)}, u32[]{:S(2)}) collective-permute-start(bf16[4,20,40,128]{3,2,1,0:T(8,128)(2,1)} %copy-done.3), channel_id=1, source_target_pairs={{0,8},{1,9},{2,10},{3,11},{4,12},{5,13},{6,14},{7,15},{8,0},{9,1},... | collective-permute-start | bytes 2457608 | tf_op jit(solution)/shard_map/ppermute | solution.py:99
  527.9 54.2 %collective-permute-start.514 = (bf16[4,20,40,128]{3,2,1,0:T(8,128)(2,1)}, bf16[4,20,40,128]{3,2,1,0:T(8,128)(2,1)}, u32[]{:S(2)}, u32[]{:S(2)}) collective-permute-start(bf16[4,20,40,128]{3,2,1,0:T(8,128)(2,1)} %copy-done.2), channel_id=1, source_target_pairs={{0,12},{1,13},{2,14},{3,15},{4,0},{5,1},{6,2},{7,3},{8,4},{9,5},{1... | collective-permute-start | bytes 2457608 | tf_op jit(solution)/shard_map/ppermute | solution.py:99
  539.7 33.2 %collective-permute-start.516 = (bf16[20,40,256]{2,1,0:T(8,128)(2,1)}, bf16[20,40,256]{2,1,0:T(8,128)(2,1)}, u32[]{:S(2)}, u32[]{:S(2)}) collective-permute-start(bf16[20,40,256]{2,1,0:T(8,128)(2,1)} %reshape.86), channel_id=1, source_target_pairs={{0,2},{1,3},{2,0},{3,1},{4,6},{5,7},{6,4},{7,5},{8,10},{9,11},{10,... | collective-permute-start | bytes 1228808 | tf_op jit(solution)/shard_map/ppermute | solution.py:103
  551.6 30.5 %collective-permute-start.515 = (bf16[20,40,256]{2,1,0:T(8,128)(2,1)}, bf16[20,40,256]{2,1,0:T(8,128)(2,1)}, u32[]{:S(2)}, u32[]{:S(2)}) collective-permute-start(bf16[20,40,256]{2,1,0:T(8,128)(2,1)} %reshape.86), channel_id=1, source_target_pairs={{0,3},{1,0},{2,1},{3,2},{4,7},{5,4},{6,5},{7,6},{8,11},{9,8},{10,9... | collective-permute-start | bytes 1228808 | tf_op jit(solution)/shard_map/ppermute | solution.py:103
  584.8 33.8 %collective-permute-start.518 = (f32[64,128]{1,0:T(8,128)S(1)}, f32[64,128]{1,0:T(8,128)S(1)}, u32[]{:S(2)}, u32[]{:S(2)}) collective-permute-start(f32[64,128]{1,0:T(8,128)S(1)} %get-tuple-element.1587), channel_id=1, source_target_pairs={{0,12},{1,13},{2,14},{3,15},{4,0},{5,1},{6,2},{7,3},{8,4},{9,5},{1... | collective-permute-start | bytes 98312 | tf_op jit(solution)/shard_map/ppermute | solution.py:99
  595.0 23.7 %collective-permute-start.520 = (f32[64,128]{1,0:T(8,128)S(1)}, f32[64,128]{1,0:T(8,128)S(1)}, u32[]{:S(2)}, u32[]{:S(2)}) collective-permute-start(f32[64,128]{1,0:T(8,128)S(1)} %get-tuple-element.1588), channel_id=1, source_target_pairs={{0,4},{1,5},{2,6},{3,7},{4,8},{5,9},{6,10},{7,11},{8,12},{9,13},{1... | collective-permute-start | bytes 98312 | tf_op jit(solution)/shard_map/ppermute | solution.py:99
  606.8 16.0 %collective-permute-start.519 = (f32[64,128]{1,0:T(8,128)S(1)}, f32[64,128]{1,0:T(8,128)S(1)}, u32[]{:S(2)}, u32[]{:S(2)}) collective-permute-start(f32[64,128]{1,0:T(8,128)S(1)} %get-tuple-element.1589), channel_id=1, source_target_pairs={{0,8},{1,9},{2,10},{3,11},{4,12},{5,13},{6,14},{7,15},{8,0},{9,1},... | collective-permute-start | bytes 98312 | tf_op jit(solution)/shard_map/ppermute | solution.py:99
  (20 other events, 182.6 us)

commit v2 on v0

v2 whole, which is shorter than its diff:
```python
import jax
import jax.numpy as jnp
from jax import lax
from jax.experimental import pallas as pl
from jax.experimental.pallas import tpu as pltpu
from jax.sharding import Mesh
from jax.sharding import PartitionSpec as P

PR = 64
STEPS = 2
X = 4
ZL = 4
ROW = ("zh", "y", "core")
COL = ("x", "zl")
ROWS = 16
NV = 640
BLOCK = 40
PIECE = 10
HALF = PIECE // 2
PAIRS = 64
LANES = 128
QUARTER = NV // X
DEPTH = PIECE * QUARTER
CHUNK = 16
MESSAGE = 56


def cost(flops, moved):
    return pl.CostEstimate(flops=flops, bytes_accessed=moved, transcendentals=0)


def slice_kernel(owners_ref, offsets_ref, integrals_ref, *refs):
    out_refs, (held, rows, sems) = refs[:X], refs[X:]
    i = pl.program_id(0)
    x = lax.axis_index("x")
    owns_second = jnp.logical_and(x * ZL + lax.axis_index("zl") == owners_ref[1], owners_ref[0] != owners_ref[1])
    start = jnp.where(owns_second, offsets_ref[1], offsets_ref[0])

    def copy(chunk):
        source = integrals_ref.at[pl.ds(start + chunk * CHUNK, CHUNK)]
        return pltpu.make_async_copy(source, held.at[chunk], sems.at[chunk])

    @pl.when(i == 0)
    def _():
        for chunk in range(PR // CHUNK):
            copy(chunk).start()

    for chunk in range(PR // CHUNK):

        @pl.when(i == chunk)
        def _():
            copy(chunk).wait()

    for t in range(NV // LANES):
        lanes = slice(t * LANES, (t + 1) * LANES)
        rows[...] = held[i, :, :, lanes].astype(jnp.float32).reshape(CHUNK * BLOCK, LANES)
        for k in range(X):
            first = lax.rem(x + k, X) * PIECE
            for m in range(PIECE):
                out_refs[k][m, :, lanes] = rows[pl.ds(first + m, CHUNK, stride=BLOCK), :].astype(jnp.bfloat16)


def slice_panel(integrals, owners, offsets):
    piece = jax.ShapeDtypeStruct((PIECE, PR, NV), jnp.bfloat16)
    return pl.pallas_call(
        slice_kernel,
        grid_spec=pltpu.PrefetchScalarGridSpec(
            num_scalar_prefetch=2,
            grid=(PR // CHUNK,),
            in_specs=[pl.BlockSpec(memory_space=pl.ANY)],
            out_specs=[pl.BlockSpec((PIECE, CHUNK, NV), lambda i, owners, offsets: (0, i, 0))] * X,
            scratch_shapes=[
                pltpu.VMEM((PR // CHUNK, CHUNK, BLOCK, NV), jnp.bfloat16),
                pltpu.VMEM((CHUNK * BLOCK, LANES), jnp.float32),
                pltpu.SemaphoreType.DMA((PR // CHUNK,)),
            ],
        ),
        out_shape=[piece] * X,
        compiler_params=pltpu.CompilerParams(vmem_limit_bytes=24 * 2**20),
        cost_estimate=cost(0, 4 * PR * BLOCK * NV),
    )(owners, offsets, integrals)


def turn_kernel(choice_ref, *refs):
    piece_refs, out_ref, (held, turned, message, sem) = refs[: X + 1], refs[X + 1], refs[X + 2 :]
    for k in range(X + 1):

        @pl.when(choice_ref[0] == k)
        def _():
            copy = pltpu.make_async_copy(piece_refs[k], held, sem)
            copy.start()
            copy.wait()

    for half in range(HALF):
        turned[half * NV : (half + 1) * NV, :] = held[half].T.astype(jnp.float32)
    message[...] = jnp.zeros_like(message)
    for half in range(HALF):
        for e in range(PIECE):
            rows = turned[pl.ds(half * NV + e, ROWS * ZL, stride=PIECE), :]
            message[pl.ds(half * PIECE + e, ROWS * ZL, stride=MESSAGE), :] = rows
    out_ref[...] = message[...].astype(jnp.bfloat16).reshape(ROWS * ZL, MESSAGE, LANES)


def turn_panel(choice, pieces):
    pieces = [piece.reshape(HALF, LANES, NV) for piece in pieces]
    return pl.pallas_call(
        turn_kernel,
        grid_spec=pltpu.PrefetchScalarGridSpec(
            num_scalar_prefetch=1,
            grid=(1,),
            in_specs=[pl.BlockSpec(memory_space=pl.ANY)] * (X + 1),
            out_specs=pl.BlockSpec((ROWS * ZL, MESSAGE, LANES), lambda i, choice: (0, 0, 0)),
            scratch_shapes=[
                pltpu.VMEM((HALF, LANES, NV), jnp.bfloat16),
                pltpu.VMEM((HALF * NV, LANES), jnp.float32),
                pltpu.VMEM((ROWS * ZL * MESSAGE, LANES), jnp.float32),
                pltpu.SemaphoreType.DMA,
            ],
        ),
        out_shape=jax.ShapeDtypeStruct((ROWS * ZL, MESSAGE, LANES), jnp.bfloat16),
        compiler_params=pltpu.CompilerParams(vmem_limit_bytes=24 * 2**20),
        cost_estimate=cost(0, 4 * LANES * NV * HALF),
    )(choice[None].astype(jnp.int32), *pieces)


def amplitude_kernel(place_ref, first_ref, second_ref, *refs):
    out_refs, held = refs[:-1], refs[-1]
    stacked = jnp.concatenate([first_ref[0], second_ref[0]], axis=0)
    held[...] = stacked.T.astype(jnp.float32)
    for k in range(X):
        first = lax.rem(place_ref[0] + k, X) * PIECE
        for m in range(PIECE):
            rows = held[pl.ds(first + m, ROWS, stride=BLOCK), :]
            out_ref = out_refs[k] if len(out_refs) > 1 else out_refs[0].at[k]
            out_ref[0, m % 2, m // 2 * ROWS : (m // 2 + 1) * ROWS] = rows.astype(jnp.bfloat16)


def turn_amplitudes(swapped, place, apart):
    piece = (PIECE, 2, QUARTER // 2, LANES)
    if apart:
        shapes = [jax.ShapeDtypeStruct(piece, jnp.bfloat16)] * X
        specs = [pl.BlockSpec((1, 2, QUARTER // 2, LANES), lambda i, place: (i, 0, 0, 0))] * X
    else:
        shapes = jax.ShapeDtypeStruct((X,) + piece, jnp.bfloat16)
        specs = pl.BlockSpec((X, 1, 2, QUARTER // 2, LANES), lambda i, place: (0, i, 0, 0, 0))
    return pl.pallas_call(
        amplitude_kernel,
        grid_spec=pltpu.PrefetchScalarGridSpec(
            num_scalar_prefetch=1,
            grid=(PIECE,),
            in_specs=[
                pl.BlockSpec((1, PAIRS, NV), lambda i, place: (place[1] * PIECE + i, 0, 0)),
                pl.BlockSpec((1, PAIRS, NV), lambda i, place: (place[2] * PIECE + i, 0, 0)),
            ],
            out_specs=specs,
            scratch_shapes=[pltpu.VMEM((NV, LANES), jnp.float32)],
        ),
        out_shape=shapes,
        compiler_params=pltpu.CompilerParams(vmem_limit_bytes=16 * 2**20),
        cost_estimate=cost(0, 2 * PAIRS * NV * BLOCK),
    )(place, swapped, swapped)


def join_kernel(source_ref, first_ref, second_ref, out_ref, low_held, high_held):
    first, second = first_ref[:, 0].astype(jnp.float32), second_ref[:, 0].astype(jnp.float32)
    low = lax.broadcasted_iota(jnp.int32, first.shape, 2) < PR
    low_held[...] = jnp.where(low, first, pltpu.roll(second, PR, 2)).reshape(ROWS * MESSAGE, LANES)
    high_held[...] = jnp.where(low, pltpu.roll(first, PR, 2), second).reshape(ROWS * MESSAGE, LANES)
    for e in range(PIECE):
        for side, held in enumerate((low_held, high_held)):
            for half in range(HALF):
                rows = held[pl.ds(half * PIECE + e, ROWS, stride=MESSAGE), :]
                out_ref[e, side, half * ROWS : (half + 1) * ROWS] = rows.astype(jnp.bfloat16)


def join_panels(got, sources):
    return pl.pallas_call(
        join_kernel,
        grid_spec=pltpu.PrefetchScalarGridSpec(
            num_scalar_prefetch=1,
            grid=(1,),
            in_specs=[
                pl.BlockSpec((ROWS, 1, MESSAGE, LANES), lambda i, source: (0, source[0], 0, 0)),
                pl.BlockSpec((ROWS, 1, MESSAGE, LANES), lambda i, source: (0, source[1], 0, 0)),
            ],
            out_specs=pl.BlockSpec((PIECE, 2, QUARTER // 2, LANES), lambda i, source: (0, 0, 0, 0)),
            scratch_shapes=[pltpu.VMEM((ROWS * MESSAGE, LANES), jnp.float32)] * 2,
        ),
        out_shape=jax.ShapeDtypeStruct((PIECE, 2, QUARTER // 2, LANES), jnp.bfloat16),
        compiler_params=pltpu.CompilerParams(vmem_limit_bytes=16 * 2**20),
        cost_estimate=cost(0, 3 * DEPTH * LANES * 2),
    )(sources, got, got)


def contract_kernel(*refs):
    left, (own_ref, other_ref), out_ref = refs[: 2 * X], refs[2 * X : 2 * X + 2], refs[2 * X + 2]
    both = jnp.concatenate([own_ref[...], other_ref[...]], axis=1)
    for k in range(2 * X):
        total = lax.dot_general(left[k][...], both, (((0,), (0,)), ((), ())), preferred_element_type=jnp.float32)
        out_ref[k // 2, k % 2] = total[:PAIRS, :LANES] + total[PAIRS:, LANES:]


def contract(left, right):
    left = [part.reshape(DEPTH, LANES) for part in left]
    right = [part.reshape(DEPTH, LANES) for part in right]
    return pl.pallas_call(
        contract_kernel,
        in_specs=[pl.BlockSpec(memory_space=pltpu.VMEM)] * (2 * X + 2),
        out_specs=pl.BlockSpec(memory_space=pltpu.VMEM),
        out_shape=jax.ShapeDtypeStruct((X, 2, PAIRS, LANES), jnp.float32),
        compiler_params=pltpu.CompilerParams(vmem_limit_bytes=32 * 2**20),
        cost_estimate=cost(2 * 1024 * 1600 * 256, 5 * 2**20),
    )(*left, *right)


def shift_x(array, k):
    return lax.ppermute(array, "x", [(x, (x + k) % X) for x in range(X)])


def swap_zl(array, bit):
    return lax.ppermute(array, "zl", [(z, z ^ bit) for z in range(ZL)])


def over_x(integrals, owners, offsets):
    pieces = slice_panel(integrals, owners, offsets)
    return [pieces[0]] + [shift_x(pieces[k], k) for k in range(1, X)]


def local(amplitudes, integrals, owners, offsets):
    got = over_x(integrals, owners, offsets)

    x, zl = lax.axis_index("x"), lax.axis_index("zl")
    owner_x, owner_z = lax.shift_right_logical(owners, 2), lax.bitwise_and(owners, 3)
    same_owner = owners[0] == owners[1]
    same_z = owner_z[0] == owner_z[1]
    at_z = [owner_z[0], jnp.where(same_z, lax.bitwise_xor(owner_z[1], 1), owner_z[1])]
    distance = lax.bitwise_and(x - owner_x, 3)
    choice = jnp.where(zl == at_z[1], jnp.where(same_z, X, distance[1]), distance[0])

    swapped = jnp.transpose(amplitudes, (2, 0, 1))
    places = [jnp.stack([x, lax.bitwise_xor(zl, k), lax.bitwise_xor(zl, k + 2)]).astype(jnp.int32) for k in range(2)]
    others = swap_zl(turn_amplitudes(swapped, places[1], False), 1)
    owns = turn_amplitudes(swapped, places[0], True)
    got, owns = lax.optimization_barrier((got, owns))

    def stay(*operands):
        return jnp.zeros((PIECE, PR, NV), jnp.bfloat16)

    def move(same_owner, owners, offsets, place, integrals, *got):
        def again(owners, offsets, integrals, *got):
            return over_x(integrals, owners, jnp.stack([offsets[1], offsets[1]]))

        def keep(owners, offsets, integrals, *got):
            return list(got)

        got = lax.cond(same_owner, again, keep, owners, offsets, integrals, *got)
        return swap_zl(lax.select_n(place, *got), 1)

    moved = lax.cond(same_z, move, stay, same_owner, owners, offsets, distance[1], integrals, *got)

    left = [owns[0], others[0]]
    for k in range(1, X):
        left += [shift_x(owns[k], k), shift_x(others[k], k)]

    message = turn_panel(choice, got + [moved])
    spread = lax.all_to_all(message, ROW + ("zl",), 0, 0, tiled=True)
    mine = join_panels(spread.reshape(ROWS, ZL, MESSAGE, LANES), jnp.stack(at_z).astype(jnp.int32))
    part = contract(left, [mine, swap_zl(mine, 2)])

    total = part[0]
    for k in range(1, X):
        total = total + shift_x(part[k], -k)
    total = total[0] + swap_zl(total[1], 1)
    spread = lax.all_to_all(total.reshape(ROWS, PAIRS // ROWS, LANES), ROW, 0, 0, tiled=True)
    return jnp.sum(spread, axis=0)


def solution(mesh):
    fine = Mesh(mesh.devices.reshape(2, 4, 2, X, ZL), ROW + COL)
    in_specs = (P(COL, None, ROW), P(COL, ROW, None), P(), P())
    out_specs = P(COL + ROW, None)
    return jax.shard_map(local, mesh=fine, in_specs=in_specs, out_specs=out_specs, check_vma=False)
```

time: 498 us -> 141 us (0.28); the launches traced: 491 us -> 141 us
  waiting for transfers between devices: 315 us -> 61.6 us
  blocking collectives: 81 us -> 17.9 us
  local copies, waits for them, and re-layouts: 52.4 us -> 8.2 us
  starting transfers between devices: 12.8 us -> 31.9 us
  Pallas kernels: 0 us -> 15.6 us
  between operations: 19.3 us -> 3.98 us
  matrix products: 7.72 us -> 0 us
    psum x1 -> x0, waiting for transfers between devices: 219 us -> none  [broadcast(): return lax.psum(jnp.where(mine, array, jnp.zeros_like(array)), axis)]
    unnamed x1 -> x0, blocking collectives: 81 us -> none
    all_to_all x1, waiting for transfers between devices: 95.1 us -> 16.9 us  [local(): spread = lax.all_to_all(message, ROW + ('zl',), 0, 0, tiled=True)]
    ppermute x0 -> x15, waiting for transfers between devices: none -> 44.7 us  [the longest x12 32 us: shift_x(): return lax.ppermute(array, 'x', [(x, (x + k) % X) for x in range(X)])]
    unnamed x15 -> x11, local copies, waits for them, and re-layouts: 42.2 us -> 4.14 us
    ppermute x0 -> x15, starting transfers between devices: none -> 18.7 us  [the longest x12 16.3 us: shift_x(): return lax.ppermute(array, 'x', [(x, (x + k) % X) for x in range(X)])]
    all_to_all x0 -> x1, blocking collectives: none -> 17.9 us  [local(): lax.all_to_all(total.reshape(ROWS, PAIRS // ROWS, LANES), ROW, 0, 0, tile...]
    pallas_call x0 -> x6, Pallas kernels: none -> 15.6 us  [the longest x1 5.04 us: slice_panel(): pl.pallas_call(slice_kernel, grid_spec=pltpu.PrefetchScalarGridSpec(num_s...]
  transfers between devices with their start and end apart: 2 -> 16, of which waited for: 2 -> 8; matrix products, arithmetic and copies ran while one was open for 9% -> 5% of each run, Pallas kernels for 0% -> 6%
where the time goes in v2:
time: 141 us
  waiting for transfers between devices  61.6 us (44%)
  starting transfers between devices  31.9 us (23%)
  blocking collectives  17.9 us (13%)
  Pallas kernels  15.6 us (11%)
  local copies, waits for them, and re-layouts  8.2 us (6%)
  between operations  3.98 us (3%)
  other arithmetic  1.46 us (1%)
    ppermute x12, waiting for transfers between devices, shift_x(): return lax.ppermute(array, 'x', [(x, (x + k) % X) for x in range(X)])  32 us
    all_to_all x1, blocking collectives, local(): lax.all_to_all(total.reshape(ROWS, PAIRS // ROWS, LANES), ROW, 0, 0, tile...  17.9 us
    all_to_all x1, waiting for transfers between devices, local(): spread = lax.all_to_all(message, ROW + ('zl',), 0, 0, tiled=True)  16.9 us
    ppermute x12, starting transfers between devices, shift_x(): return lax.ppermute(array, 'x', [(x, (x + k) % X) for x in range(X)])  16.3 us
    all_to_all x1, starting transfers between devices, local(): spread = lax.all_to_all(message, ROW + ('zl',), 0, 0, tiled=True)  13.2 us
    ppermute x3, waiting for transfers between devices, swap_zl(): return lax.ppermute(array, 'zl', [(z, z ^ bit) for z in range(ZL)])  12.6 us
    pallas_call x1, Pallas kernels, slice_panel(): pl.pallas_call(slice_kernel, grid_spec=pltpu.PrefetchScalarGridSpec(num_s...  5.04 us
    pallas_call x2, Pallas kernels, turn_amplitudes(): pl.pallas_call(amplitude_kernel, grid_spec=pltpu.PrefetchScalarGridSpec(n...  4.69 us
  transfers between devices with their start and end apart: 16, of which 8 were waited for; matrix products, arithmetic and copies ran while one was open for 5% of the time, Pallas kernels for 6%

profile of v2, /device:TPU:1, one launch (start us, length us, event | category | flops | bytes accessed | tf_op | source)
XLA Modules:
  0.0 140.6 jit_solution(6774856994333506222)
XLA Ops:
  0.0 5.0 %shard_map.46 = (bf16[10,64,640]{2,1,0:T(8,128)(2,1)}, bf16[10,64,640]{2,1,0:T(8,128)(2,1)}, bf16[10,64,640]{2,1,0:T(8,128)(2,1)}, bf16[10,64,640]{2,1,0:T(8,128)(2,1)S(1)}) custom-call(s32[2]{0:T(128)} %owners_ref.1, s32[2]{0:T(128)} %offsets_ref.1, bf16[96,40,640]{2,1,0:T(8,128)(2,1)} %integrals_ref.1), custom_call_target="tpu_custom_call" | custom-call | bytes 6553600 | tf_op jit(solution)/shard_map/pallas_call | solution.py:65
  5.1 2.1 %collective-permute-start.4 = (bf16[10,64,640]{2,1,0:T(8,128)(2,1)}, bf16[10,64,640]{2,1,0:T(8,128)(2,1)}, u32[]{:S(2)}, u32[]{:S(2)}) collective-permute-start(bf16[10,64,640]{2,1,0:T(8,128)(2,1)} %get-tuple-element.82), channel_id=1, source_target_pairs={{0,4},{4,8},{8,12},{12,0},{1,5},{5,9},{9,13},{13,1},{2,6},{6,10},{... | collective-permute-start | bytes 2457608 | tf_op jit(solution)/shard_map/ppermute | solution.py:217
  7.2 2.5 %collective-permute-start.5 = (bf16[10,64,640]{2,1,0:T(8,128)(2,1)}, bf16[10,64,640]{2,1,0:T(8,128)(2,1)}, u32[]{:S(2)}, u32[]{:S(2)}) collective-permute-start(bf16[10,64,640]{2,1,0:T(8,128)(2,1)} %get-tuple-element.83), channel_id=1, source_target_pairs={{0,8},{4,12},{8,0},{12,4},{1,9},{5,13},{9,1},{13,5},{2,10},{6,14},... | collective-permute-start | bytes 2457608 | tf_op jit(solution)/shard_map/ppermute | solution.py:217
  9.6 1.1 collective-permute-start.6
  10.8 2.5 %copy.7 = bf16[64,640,40]{1,0,2:T(8,128)(2,1)S(1)} copy(bf16[64,640,40]{1,2,0:T(8,128)(2,1)} %param.8) | data formatting | bytes 6553600 | tf_op args[0]
  13.3 0.1 pad_add_fusion.1
  13.4 2.4 %shard_map.48 = bf16[4,10,2,80,128]{4,3,2,1,0:T(8,128)(2,1)S(1)} custom-call(s32[3]{0:T(128)S(1)} %get-tuple-element.115.place_ref, bf16[40,64,640]{2,1,0:T(8,128)(2,1)S(1)} %bitcast.58, bf16[40,64,640]{2,1,0:T(8,128)(2,1)S(1)} %bitcast.59), custom_call_target="tpu_custom_call" | custom-call | bytes 3276800 | tf_op jit(solution)/shard_map/pallas_call | solution.py:146
  15.8 1.7 %collective-permute-start.7 = (bf16[4,10,2,80,128]{4,3,2,1,0:T(8,128)(2,1)S(1)}, bf16[4,10,2,80,128]{4,3,2,1,0:T(8,128)(2,1)}, u32[]{:S(2)}, u32[]{:S(2)}) collective-permute-start(bf16[4,10,2,80,128]{4,3,2,1,0:T(8,128)(2,1)S(1)} %shard_map.48), channel_id=1, source_target_pairs={{0,1},{1,0},{2,3},{3,2},{4,5},{5,4},{6,7},{7,6},{8,9},{9,8},{10,11... | collective-permute-start | bytes 4915208 | tf_op jit(solution)/shard_map/ppermute | solution.py:221
  17.5 2.3 %shard_map.47 = (bf16[10,2,80,128]{3,2,1,0:T(8,128)(2,1)S(1)}, bf16[10,2,80,128]{3,2,1,0:T(8,128)(2,1)S(1)}, bf16[10,2,80,128]{3,2,1,0:T(8,128)(2,1)S(1)}, bf16[10,2,80,128]{3,2,1,0:T(8,128)(2,1)S(1)}) custom-call(s32[3]{0:T(128)S(1)} %get-tuple-element.114.place_ref, bf16[40,64,640]{2,1,0:T(8,128)(2,1)S(1)} %bitcast.60, bf16[40,64,640]{2,1,0:T(8,128)(2,1)S(1)} %bitcast.61), custom_call_target="tpu_custom_call" | custom-call | bytes 3276800 | tf_op jit(solution)/shard_map/pallas_call | solution.py:146
  19.8 0.8 copy-done
  20.6 0.7 copy-done.1
  21.3 0.1 copy-done.2
  21.5 0.7 fusion.5
  26.0 0.0 collective-permute-done.4
  26.0 19.2 %collective-permute-done.5 = bf16[10,64,640]{2,1,0:T(8,128)(2,1)} collective-permute-done((bf16[10,64,640]{2,1,0:T(8,128)(2,1)}, bf16[10,64,640]{2,1,0:T(8,128)(2,1)}, u32[]{:S(2)}, u32[]{:S(2)}) %collective-permute-start.5) | collective-permute-done | bytes 819232 | tf_op jit(solution)/shard_map/ppermute | solution.py:217
  45.1 0.0 collective-permute-done.6
  45.2 1.0 conditional.2
  45.2 1.0 reshape.36
  46.1 2.7 %shard_map.49 = bf16[64,56,128]{2,1,0:T(8,128)(2,1)} custom-call(s32[1]{0:T(128)} %bitcast.24.choice_ref, bf16[5,128,640]{2,1,0:T(8,128)(2,1)} %bitcast.72, bf16[5,128,640]{2,1,0:T(8,128)(2,1)} %bitcast.26.refs_1_, bf16[5,128,640]{2,1,0:T(8,128)(2,1)} %bitcast.27.refs_2_, bf16[5,128,640]{2,1,0:T(8,128)(2,1)} %bitcast.28.refs_3_, ...), custom_call_target="tpu_custom_call" | custom-call | bytes 1638400 | tf_op jit(solution)/shard_map/pallas_call | solution.py:106
  48.8 13.2 %all-to-all-start = ((bf16[64,56,128]{2,1,0:T(8,128)(2,1)}), bf16[64,56,128]{2,1,0:T(8,128)(2,1)S(1)}, u32[]{:S(2)}, u32[]{:S(2)}) async-start(bf16[64,56,128]{2,1,0:T(8,128)(2,1)} %shard_map.49), calls=%async_computation | async-start | bytes 1835008 | tf_op jit(solution)/shard_map/all_to_all | solution.py:266
  62.0 0.9 collective-permute-start.8
  63.0 2.3 %collective-permute-start.10 = (bf16[10,2,80,128]{3,2,1,0:T(8,128)(2,1)}, bf16[10,2,80,128]{3,2,1,0:T(8,128)(2,1)}, u32[]{:S(2)}, u32[]{:S(2)}) collective-permute-start(bf16[10,2,80,128]{3,2,1,0:T(8,128)(2,1)} %copy-done.1), channel_id=1, source_target_pairs={{0,8},{4,12},{8,0},{12,4},{1,9},{5,13},{9,1},{13,5},{2,10},{6,14},... | collective-permute-start | bytes 1228808 | tf_op jit(solution)/shard_map/ppermute | solution.py:217
  65.3 0.7 pad_add_fusion.3.source_ref
  66.0 1.3 collective-permute-start.12
  67.3 2.4 %slice_bitcast_fusion = (bf16[10,2,80,128]{3,2,1,0:T(8,128)(2,1)S(1)}, bf16[10,2,80,128]{3,2,1,0:T(8,128)(2,1)}, bf16[10,2,80,128]{3,2,1,0:T(8,128)(2,1)}, bf16[1,10,2,80,128]{4,3,2,1,0:T(8,128)(2,1)S(1)}) fusion(bf16[4,10,2,80,128]{4,3,2,1,0:T(8,128)(2,1)} %collective-permute-done.7), kind=kLoop, calls=%fused_computation.3 | loop fusion | bytes 3276800 | tf_op jit(solution)/shard_map/squeeze | solution.py:263
  69.7 0.2 collective-permute-start.9
  69.9 1.0 collective-permute-start.11
  71.0 16.9 %all-to-all-done = bf16[64,56,128]{2,1,0:T(8,128)(2,1)S(1)} async-done(((bf16[64,56,128]{2,1,0:T(8,128)(2,1)}), bf16[64,56,128]{2,1,0:T(8,128)(2,1)S(1)}, u32[]{:S(2)}, u32[]{:S(2)}) %all-to-all-start) | async-done | bytes 917536 | tf_op jit(solution)/shard_map/all_to_all | solution.py:266
  87.8 0.9 shard_map.50
  88.7 0.0 collective-permute-done.8
  88.7 2.0 %collective-permute-start.13 = (bf16[10,2,80,128]{3,2,1,0:T(8,128)(2,1)S(1)}, bf16[10,2,80,128]{3,2,1,0:T(8,128)(2,1)S(1)}, u32[]{:S(2)}, u32[]{:S(2)}) collective-permute-start(bf16[10,2,80,128]{3,2,1,0:T(8,128)(2,1)S(1)} %get-tuple-element.99), channel_id=1, source_target_pairs={{0,12},{4,0},{8,4},{12,8},{1,13},{5,1},{9,5},{13,9},{2,14},{6,2},{... | collective-permute-start | bytes 1228808 | tf_op jit(solution)/shard_map/ppermute | solution.py:217
  90.8 0.0 collective-permute-done.10
  90.8 0.5 collective-permute-start.14
  91.3 0.0 collective-permute-done.12
  91.3 0.4 collective-permute-done.9
  91.7 9.3 %collective-permute-done.11 = bf16[10,2,80,128]{3,2,1,0:T(8,128)(2,1)S(1)} collective-permute-done((bf16[10,2,80,128]{3,2,1,0:T(8,128)(2,1)}, bf16[10,2,80,128]{3,2,1,0:T(8,128)(2,1)S(1)}, u32[]{:S(2)}, u32[]{:S(2)}) %collective-permute-start.11) | collective-permute-done | bytes 409632 | tf_op jit(solution)/shard_map/ppermute | solution.py:217
  101.0 0.0 collective-permute-done.13
  101.0 9.9 %collective-permute-done.14 = bf16[10,2,80,128]{3,2,1,0:T(8,128)(2,1)S(1)} collective-permute-done((bf16[10,2,80,128]{3,2,1,0:T(8,128)(2,1)S(1)}, bf16[10,2,80,128]{3,2,1,0:T(8,128)(2,1)S(1)}, u32[]{:S(2)}, u32[]{:S(2)}) %collective-permute-start.14) | collective-permute-done | bytes 409632 | tf_op jit(solution)/shard_map/ppermute | solution.py:221
  110.9 2.3 %shard_map.51 = f32[4,2,64,128]{3,2,1,0:T(8,128)S(1)} custom-call(bf16[1600,128]{1,0:T(8,128)(2,1)S(1)} %bitcast.66, bf16[1600,128]{1,0:T(8,128)(2,1)S(1)} %bitcast.64, bf16[1600,128]{1,0:T(8,128)(2,1)S(1)} %bitcast.67, bf16[1600,128]{1,0:T(8,128)(2,1)S(1)} %bitcast.68, bf16[1600,128]{1,0:T(8,128)(2,1)} %bitcast.13.refs_4_, bf16[1600,128]{1,0:T(8,128)(2,1)S(1)} %bitcast.69, ...), custom_call_target="tpu_custom_call" | custom-call | flops 838860800 | bytes 5242880 | tf_op jit(solution)/shard_map/pallas_call | solution.py:206
  113.2 0.1 collective-permute-start.17
  113.3 1.9 %collective-permute-start.16 = (f32[2,64,128]{2,1,0:T(8,128)S(1)}, f32[2,64,128]{2,1,0:T(8,128)S(1)}, u32[]{:S(2)}, u32[]{:S(2)}) collective-permute-start(f32[2,64,128]{2,1,0:T(8,128)S(1)} %get-tuple-element.105), channel_id=1, source_target_pairs={{0,8},{4,12},{8,0},{12,4},{1,9},{5,13},{9,1},{13,5},{2,10},{6,14},... | collective-permute-start | bytes 196616 | tf_op jit(solution)/shard_map/ppermute | solution.py:217
  115.1 0.9 collective-permute-start.15
  116.0 2.3 %collective-permute-done.17 = f32[2,64,128]{2,1,0:T(8,128)S(1)} collective-permute-done((f32[2,64,128]{2,1,0:T(8,128)S(1)}, f32[2,64,128]{2,1,0:T(8,128)S(1)}, u32[]{:S(2)}, u32[]{:S(2)}) %collective-permute-start.17) | collective-permute-done | bytes 65568 | tf_op jit(solution)/shard_map/ppermute | solution.py:217
  118.3 0.9 collective-permute-done.15
  119.2 0.1 collective-permute-start.18
  119.3 2.8 %collective-permute-done.18 = f32[64,128]{1,0:T(8,128)S(1)} collective-permute-done((f32[64,128]{1,0:T(8,128)S(1)}, f32[64,128]{1,0:T(8,128)S(1)}, u32[]{:S(2)}, u32[]{:S(2)}) %collective-permute-start.18) | collective-permute-done | bytes 32800 | tf_op jit(solution)/shard_map/ppermute | solution.py:221
  122.1 17.9 %all_to_all.10 = f32[16,4,128]{2,1,0:T(4,128)S(1)} all-to-all(f32[16,4,128]{2,1,0:T(4,128)S(1)} %bitcast.73), channel_id=1, replica_groups=mesh['zh'=2,'y'=4,'core'=2,'x'=4,'zl'=4] {'zh','y','core'}, dimensions={0} | all-to-all | bytes 65536 | tf_op jit(solution)/shard_map/all_to_all | solution.py:274
  140.0 0.6 reduce_sum.9
  (14 shorter events, 0.1 us)
Async XLA Ops:
  5.1 20.9 %collective-permute-start.4 = (bf16[10,64,640]{2,1,0:T(8,128)(2,1)}, bf16[10,64,640]{2,1,0:T(8,128)(2,1)}, u32[]{:S(2)}, u32[]{:S(2)}) collective-permute-start(bf16[10,64,640]{2,1,0:T(8,128)(2,1)} %get-tuple-element.82), channel_id=1, source_target_pairs={{0,4},{4,8},{8,12},{12,0},{1,5},{5,9},{9,13},{13,1},{2,6},{6,10},{... | collective-permute-start | bytes 2457608 | tf_op jit(solution)/shard_map/ppermute | solution.py:217
  7.2 38.0 %collective-permute-start.5 = (bf16[10,64,640]{2,1,0:T(8,128)(2,1)}, bf16[10,64,640]{2,1,0:T(8,128)(2,1)}, u32[]{:S(2)}, u32[]{:S(2)}) collective-permute-start(bf16[10,64,640]{2,1,0:T(8,128)(2,1)} %get-tuple-element.83), channel_id=1, source_target_pairs={{0,8},{4,12},{8,0},{12,4},{1,9},{5,13},{9,1},{13,5},{2,10},{6,14},... | collective-permute-start | bytes 2457608 | tf_op jit(solution)/shard_map/ppermute | solution.py:217
  9.6 35.5 %collective-permute-start.6 = (bf16[10,64,640]{2,1,0:T(8,128)(2,1)S(1)}, bf16[10,64,640]{2,1,0:T(8,128)(2,1)}, u32[]{:S(2)}, u32[]{:S(2)}) collective-permute-start(bf16[10,64,640]{2,1,0:T(8,128)(2,1)S(1)} %get-tuple-element.84), channel_id=1, source_target_pairs={{0,12},{4,0},{8,4},{12,8},{1,13},{5,1},{9,5},{13,9},{2,14},{6,2},{... | collective-permute-start | bytes 2457608 | tf_op jit(solution)/shard_map/ppermute | solution.py:217
  15.8 51.5 %collective-permute-start.7 = (bf16[4,10,2,80,128]{4,3,2,1,0:T(8,128)(2,1)S(1)}, bf16[4,10,2,80,128]{4,3,2,1,0:T(8,128)(2,1)}, u32[]{:S(2)}, u32[]{:S(2)}) collective-permute-start(bf16[4,10,2,80,128]{4,3,2,1,0:T(8,128)(2,1)S(1)} %shard_map.48), channel_id=1, source_target_pairs={{0,1},{1,0},{2,3},{3,2},{4,5},{5,4},{6,7},{7,6},{8,9},{9,8},{10,11... | collective-permute-start | bytes 4915208 | tf_op jit(solution)/shard_map/ppermute | solution.py:221
  17.5 3.1 %copy-start.3 = (s32[2]{0:T(128)S(1)}, s32[2]{0:T(128)}, u32[]{:S(2)}) copy-start(s32[2]{0:T(128)} %owners_ref.1) | copy-start | bytes 28
  17.5 27.6 %copy-start.4 = (s32[2]{0:T(128)S(1)}, s32[2]{0:T(128)}, u32[]{:S(2)}) copy-start(s32[2]{0:T(128)} %offsets_ref.1) | copy-start | bytes 28
  19.8 0.8 copy-start
  20.6 0.8 copy-start.1
  20.6 0.9 copy-start.2
  48.8 39.0 %all-to-all-start = ((bf16[64,56,128]{2,1,0:T(8,128)(2,1)}), bf16[64,56,128]{2,1,0:T(8,128)(2,1)S(1)}, u32[]{:S(2)}, u32[]{:S(2)}) async-start(bf16[64,56,128]{2,1,0:T(8,128)(2,1)} %shard_map.49), calls=%async_computation | async-start | bytes 1835008 | tf_op jit(solution)/shard_map/all_to_all | solution.py:266
  62.0 26.7 %collective-permute-start.8 = (bf16[10,2,80,128]{3,2,1,0:T(8,128)(2,1)}, bf16[10,2,80,128]{3,2,1,0:T(8,128)(2,1)S(1)}, u32[]{:S(2)}, u32[]{:S(2)}) collective-permute-start(bf16[10,2,80,128]{3,2,1,0:T(8,128)(2,1)} %copy-done.2), channel_id=1, source_target_pairs={{0,4},{4,8},{8,12},{12,0},{1,5},{5,9},{9,13},{13,1},{2,6},{6,10},{... | collective-permute-start | bytes 1228808 | tf_op jit(solution)/shard_map/ppermute | solution.py:217
  63.0 27.8 %collective-permute-start.10 = (bf16[10,2,80,128]{3,2,1,0:T(8,128)(2,1)}, bf16[10,2,80,128]{3,2,1,0:T(8,128)(2,1)}, u32[]{:S(2)}, u32[]{:S(2)}) collective-permute-start(bf16[10,2,80,128]{3,2,1,0:T(8,128)(2,1)} %copy-done.1), channel_id=1, source_target_pairs={{0,8},{4,12},{8,0},{12,4},{1,9},{5,13},{9,1},{13,5},{2,10},{6,14},... | collective-permute-start | bytes 1228808 | tf_op jit(solution)/shard_map/ppermute | solution.py:217
  66.0 25.3 %collective-permute-start.12 = (bf16[10,2,80,128]{3,2,1,0:T(8,128)(2,1)}, bf16[10,2,80,128]{3,2,1,0:T(8,128)(2,1)}, u32[]{:S(2)}, u32[]{:S(2)}) collective-permute-start(bf16[10,2,80,128]{3,2,1,0:T(8,128)(2,1)} %copy-done), channel_id=1, source_target_pairs={{0,12},{4,0},{8,4},{12,8},{1,13},{5,1},{9,5},{13,9},{2,14},{6,2},{... | collective-permute-start | bytes 1228808 | tf_op jit(solution)/shard_map/ppermute | solution.py:217
  69.7 21.9 %collective-permute-start.9 = (bf16[10,2,80,128]{3,2,1,0:T(8,128)(2,1)}, bf16[10,2,80,128]{3,2,1,0:T(8,128)(2,1)S(1)}, u32[]{:S(2)}, u32[]{:S(2)}) collective-permute-start(bf16[10,2,80,128]{3,2,1,0:T(8,128)(2,1)} %get-tuple-element.101), channel_id=1, source_target_pairs={{0,4},{4,8},{8,12},{12,0},{1,5},{5,9},{9,13},{13,1},{2,6},{6,10},{... | collective-permute-start | bytes 1228808 | tf_op jit(solution)/shard_map/ppermute | solution.py:217
  69.9 31.1 %collective-permute-start.11 = (bf16[10,2,80,128]{3,2,1,0:T(8,128)(2,1)}, bf16[10,2,80,128]{3,2,1,0:T(8,128)(2,1)S(1)}, u32[]{:S(2)}, u32[]{:S(2)}) collective-permute-start(bf16[10,2,80,128]{3,2,1,0:T(8,128)(2,1)} %get-tuple-element.100), channel_id=1, source_target_pairs={{0,8},{4,12},{8,0},{12,4},{1,9},{5,13},{9,1},{13,5},{2,10},{6,14},... | collective-permute-start | bytes 1228808 | tf_op jit(solution)/shard_map/ppermute | solution.py:217
  88.7 12.3 %collective-permute-start.13 = (bf16[10,2,80,128]{3,2,1,0:T(8,128)(2,1)S(1)}, bf16[10,2,80,128]{3,2,1,0:T(8,128)(2,1)S(1)}, u32[]{:S(2)}, u32[]{:S(2)}) collective-permute-start(bf16[10,2,80,128]{3,2,1,0:T(8,128)(2,1)S(1)} %get-tuple-element.99), channel_id=1, source_target_pairs={{0,12},{4,0},{8,4},{12,8},{1,13},{5,1},{9,5},{13,9},{2,14},{6,2},{... | collective-permute-start | bytes 1228808 | tf_op jit(solution)/shard_map/ppermute | solution.py:217
  90.8 20.1 %collective-permute-start.14 = (bf16[10,2,80,128]{3,2,1,0:T(8,128)(2,1)S(1)}, bf16[10,2,80,128]{3,2,1,0:T(8,128)(2,1)S(1)}, u32[]{:S(2)}, u32[]{:S(2)}) collective-permute-start(bf16[10,2,80,128]{3,2,1,0:T(8,128)(2,1)S(1)} %shard_map.50), channel_id=1, source_target_pairs={{0,2},{1,3},{2,0},{3,1},{4,6},{5,7},{6,4},{7,5},{8,10},{9,11},{10,... | collective-permute-start | bytes 1228808 | tf_op jit(solution)/shard_map/ppermute | solution.py:221
  113.2 5.1 %collective-permute-start.17 = (f32[2,64,128]{2,1,0:T(8,128)S(1)}, f32[2,64,128]{2,1,0:T(8,128)S(1)}, u32[]{:S(2)}, u32[]{:S(2)}) collective-permute-start(f32[2,64,128]{2,1,0:T(8,128)S(1)} %get-tuple-element.104), channel_id=1, source_target_pairs={{0,4},{4,8},{8,12},{12,0},{1,5},{5,9},{9,13},{13,1},{2,6},{6,10},{... | collective-permute-start | bytes 196616 | tf_op jit(solution)/shard_map/ppermute | solution.py:217
  113.3 5.0 %collective-permute-start.16 = (f32[2,64,128]{2,1,0:T(8,128)S(1)}, f32[2,64,128]{2,1,0:T(8,128)S(1)}, u32[]{:S(2)}, u32[]{:S(2)}) collective-permute-start(f32[2,64,128]{2,1,0:T(8,128)S(1)} %get-tuple-element.105), channel_id=1, source_target_pairs={{0,8},{4,12},{8,0},{12,4},{1,9},{5,13},{9,1},{13,5},{2,10},{6,14},... | collective-permute-start | bytes 196616 | tf_op jit(solution)/shard_map/ppermute | solution.py:217
  115.1 4.0 %collective-permute-start.15 = (f32[2,64,128]{2,1,0:T(8,128)S(1)}, f32[2,64,128]{2,1,0:T(8,128)S(1)}, u32[]{:S(2)}, u32[]{:S(2)}) collective-permute-start(f32[2,64,128]{2,1,0:T(8,128)S(1)} %get-tuple-element.103), channel_id=1, source_target_pairs={{0,12},{4,0},{8,4},{12,8},{1,13},{5,1},{9,5},{13,9},{2,14},{6,2},{... | collective-permute-start | bytes 196616 | tf_op jit(solution)/shard_map/ppermute | solution.py:217
  119.2 2.9 %collective-permute-start.18 = (f32[64,128]{1,0:T(8,128)S(1)}, f32[64,128]{1,0:T(8,128)S(1)}, u32[]{:S(2)}, u32[]{:S(2)}) collective-permute-start(f32[64,128]{1,0:T(8,128)S(1)} %slice_bitcast_fusion.7), channel_id=1, source_target_pairs={{0,1},{1,0},{2,3},{3,2},{4,5},{5,4},{6,7},{7,6},{8,9},{9,8},{10,11... | collective-permute-start | bytes 98312 | tf_op jit(solution)/shard_map/ppermute | solution.py:221

commit v3 on v2

--- a/solution.py
+++ b/solution.py
@@ -11,7 +11,8 @@
 X = 4
 ZL = 4
 ROW = ("zh", "y", "core")
-COL = ("x", "zl")
+Z = ("za", "zb")
+COL = ("x",) + Z
 ROWS = 16
 NV = 640
 BLOCK = 40
@@ -33,7 +34,7 @@
     out_refs, (held, rows, sems) = refs[:X], refs[X:]
     i = pl.program_id(0)
     x = lax.axis_index("x")
-    owns_second = jnp.logical_and(x * ZL + lax.axis_index("zl") == owners_ref[1], owners_ref[0] != owners_ref[1])
+    owns_second = jnp.logical_and(x * ZL + 2 * lax.axis_index("za") + lax.axis_index("zb") == owners_ref[1], owners_ref[0] != owners_ref[1])
     start = jnp.where(owns_second, offsets_ref[1], offsets_ref[0])
 
     def copy(chunk):
@@ -197,7 +198,8 @@
     both = jnp.concatenate([own_ref[...], other_ref[...]], axis=1)
     for k in range(2 * X):
         total = lax.dot_general(left[k][...], both, (((0,), (0,)), ((), ())), preferred_element_type=jnp.float32)
-        out_ref[k // 2, k % 2] = total[:PAIRS, :LANES] + total[PAIRS:, LANES:]
+        side = lax.rem(k + lax.axis_index("zb"), 2)
+        out_ref[k // 2, side] = total[:PAIRS, :LANES] + total[PAIRS:, LANES:]
 
 
 def contract(left, right):
@@ -218,7 +220,7 @@
 
 
 def swap_zl(array, bit):
-    return lax.ppermute(array, "zl", [(z, z ^ bit) for z in range(ZL)])
+    return lax.ppermute(array, Z, [(z, z ^ bit) for z in range(ZL)])
 
 
 def over_x(integrals, owners, offsets):
@@ -229,7 +231,7 @@
 def local(amplitudes, integrals, owners, offsets):
     got = over_x(integrals, owners, offsets)
 
-    x, zl = lax.axis_index("x"), lax.axis_index("zl")
+    x, zl = lax.axis_index("x"), lax.axis_index(Z)
     owner_x, owner_z = lax.shift_right_logical(owners, 2), lax.bitwise_and(owners, 3)
     same_owner = owners[0] == owners[1]
     same_z = owner_z[0] == owner_z[1]
@@ -246,37 +248,34 @@
     def stay(*operands):
         return jnp.zeros((PIECE, PR, NV), jnp.bfloat16)
 
-    def move(same_owner, owners, offsets, place, integrals, *got):
-        def again(owners, offsets, integrals, *got):
-            return over_x(integrals, owners, jnp.stack([offsets[1], offsets[1]]))
-
-        def keep(owners, offsets, integrals, *got):
-            return list(got)
-
-        got = lax.cond(same_owner, again, keep, owners, offsets, integrals, *got)
+    def move(place, owners, offsets, integrals, *got):
         return swap_zl(lax.select_n(place, *got), 1)
 
-    moved = lax.cond(same_z, move, stay, same_owner, owners, offsets, distance[1], integrals, *got)
+    def again(place, owners, offsets, integrals, *got):
+        got = over_x(integrals, owners, jnp.stack([offsets[1], offsets[1]]))
+        return swap_zl(lax.select_n(place, *got), 1)
+
+    case = jnp.where(same_owner, 2, jnp.where(same_z, 1, 0))
+    moved = lax.switch(case, [stay, move, again], distance[1], owners, offsets, integrals, *got)
 
     left = [owns[0], others[0]]
     for k in range(1, X):
         left += [shift_x(owns[k], k), shift_x(others[k], k)]
 
     message = turn_panel(choice, got + [moved])
-    spread = lax.all_to_all(message, ROW + ("zl",), 0, 0, tiled=True)
+    spread = lax.all_to_all(message, ROW + Z, 0, 0, tiled=True)
     mine = join_panels(spread.reshape(ROWS, ZL, MESSAGE, LANES), jnp.stack(at_z).astype(jnp.int32))
     part = contract(left, [mine, swap_zl(mine, 2)])
 
     total = part[0]
     for k in range(1, X):
         total = total + shift_x(part[k], -k)
-    total = total[0] + swap_zl(total[1], 1)
-    spread = lax.all_to_all(total.reshape(ROWS, PAIRS // ROWS, LANES), ROW, 0, 0, tiled=True)
+    spread = lax.all_to_all(total.reshape(2 * ROWS, PAIRS // ROWS, LANES), ("zb",) + ROW, 0, 0, tiled=True)
     return jnp.sum(spread, axis=0)
 
 
 def solution(mesh):
-    fine = Mesh(mesh.devices.reshape(2, 4, 2, X, ZL), ROW + COL)
+    fine = Mesh(mesh.devices.reshape(2, 4, 2, X, 2, 2), ROW + COL)
     in_specs = (P(COL, None, ROW), P(COL, ROW, None), P(), P())
     out_specs = P(COL + ROW, None)
     return jax.shard_map(local, mesh=fine, in_specs=in_specs, out_specs=out_specs, check_vma=False)

time: 141 us -> 160 us (1.13)
  waiting for transfers between devices: 61.6 us -> 75.5 us
  loops' own time: 0.01 us -> 2.03 us
    ppermute x3, waiting for transfers between devices: 12.6 us -> 28.2 us  [swap_zl(): return lax.ppermute(array, Z, [(z, z ^ bit) for z in range(ZL)])]
    ppermute x12, waiting for transfers between devices: 32 us -> 30 us  [shift_x(): return lax.ppermute(array, 'x', [(x, (x + k) % X) for x in range(X)])]
    another operation x1, loops' own time: 0.01 us -> 2.03 us  [local(): lax.switch(case, [stay, move, again], distance[1], owners, offsets, integ...]
    ppermute x3, starting transfers between devices: 2.36 us -> 3.99 us  [swap_zl(): return lax.ppermute(array, Z, [(z, z ^ bit) for z in range(ZL)])]
  transfers between devices with their start and end apart: 16 -> 16, of which waited for: 8 -> 10; matrix products, arithmetic and copies ran while one was open for 5% -> 5% of each run, Pallas kernels for 6% -> 5%
where the time goes in v3:
time: 160 us
  waiting for transfers between devices  75.5 us (47%)
  starting transfers between devices  33.1 us (21%)
  blocking collectives  17 us (11%)
  Pallas kernels  15.6 us (10%)
  local copies, waits for them, and re-layouts  8.48 us (5%)
  between operations  5.07 us (3%)
  other arithmetic  3.05 us (2%)
  loops' own time  2.03 us (1%)
    ppermute x12, waiting for transfers between devices, shift_x(): return lax.ppermute(array, 'x', [(x, (x + k) % X) for x in range(X)])  30 us
    ppermute x3, waiting for transfers between devices, swap_zl(): return lax.ppermute(array, Z, [(z, z ^ bit) for z in range(ZL)])  28.2 us
    all_to_all x1, waiting for transfers between devices, local(): spread = lax.all_to_all(message, ROW + Z, 0, 0, tiled=True)  17.3 us
    all_to_all x1, blocking collectives, local(): lax.all_to_all(total.reshape(2 * ROWS, PAIRS // ROWS, LANES), ('zb',) + R...  17 us
    ppermute x12, starting transfers between devices, shift_x(): return lax.ppermute(array, 'x', [(x, (x + k) % X) for x in range(X)])  15.4 us
    all_to_all x1, starting transfers between devices, local(): spread = lax.all_to_all(message, ROW + Z, 0, 0, tiled=True)  13.7 us
    pallas_call x1, Pallas kernels, slice_panel(): pl.pallas_call(slice_kernel, grid_spec=pltpu.PrefetchScalarGridSpec(num_s...  5.05 us
    unnamed x11, local copies, waits for them, and re-layouts  4.76 us
  transfers between devices with their start and end apart: 16, of which 10 were waited for; matrix products, arithmetic and copies ran while one was open for 5% of the time, Pallas kernels for 5%

profile of v3, /device:TPU:1, one launch (start us, length us, event | category | flops | bytes accessed | tf_op | source)
XLA Modules:
  0.0 159.8 jit_solution(12942775471274312215)
XLA Ops:
  0.0 5.1 %shard_map.46 = (bf16[10,64,640]{2,1,0:T(8,128)(2,1)}, bf16[10,64,640]{2,1,0:T(8,128)(2,1)}, bf16[10,64,640]{2,1,0:T(8,128)(2,1)}, bf16[10,64,640]{2,1,0:T(8,128)(2,1)S(1)}) custom-call(s32[2]{0:T(128)} %owners_ref.1, s32[2]{0:T(128)} %offsets_ref.1, bf16[96,40,640]{2,1,0:T(8,128)(2,1)} %integrals_ref.1), custom_call_target="tpu_custom_call" | custom-call | bytes 6553600 | tf_op jit(solution)/shard_map/pallas_call | solution.py:66
  5.1 2.1 %collective-permute-start.5 = (bf16[10,64,640]{2,1,0:T(8,128)(2,1)}, bf16[10,64,640]{2,1,0:T(8,128)(2,1)}, u32[]{:S(2)}, u32[]{:S(2)}) collective-permute-start(bf16[10,64,640]{2,1,0:T(8,128)(2,1)} %get-tuple-element.58), channel_id=1, source_target_pairs={{0,4},{4,8},{8,12},{12,0},{1,5},{5,9},{9,13},{13,1},{2,6},{6,10},{... | collective-permute-start | bytes 2457608 | tf_op jit(solution)/shard_map/ppermute | solution.py:219
  7.2 2.5 %collective-permute-start.6 = (bf16[10,64,640]{2,1,0:T(8,128)(2,1)}, bf16[10,64,640]{2,1,0:T(8,128)(2,1)}, u32[]{:S(2)}, u32[]{:S(2)}) collective-permute-start(bf16[10,64,640]{2,1,0:T(8,128)(2,1)} %get-tuple-element.59), channel_id=1, source_target_pairs={{0,8},{4,12},{8,0},{12,4},{1,9},{5,13},{9,1},{13,5},{2,10},{6,14},... | collective-permute-start | bytes 2457608 | tf_op jit(solution)/shard_map/ppermute | solution.py:219
  9.6 1.1 collective-permute-start.7
  10.8 2.5 %copy.7 = bf16[64,640,40]{1,0,2:T(8,128)(2,1)S(1)} copy(bf16[64,640,40]{1,2,0:T(8,128)(2,1)} %param.7) | data formatting | bytes 6553600 | tf_op args[0]
  13.3 0.1 pad_add_fusion.1
  13.4 2.4 %shard_map.48 = bf16[4,10,2,80,128]{4,3,2,1,0:T(8,128)(2,1)S(1)} custom-call(s32[3]{0:T(128)S(1)} %get-tuple-element.91.place_ref, bf16[40,64,640]{2,1,0:T(8,128)(2,1)S(1)} %bitcast.53, bf16[40,64,640]{2,1,0:T(8,128)(2,1)S(1)} %bitcast.54), custom_call_target="tpu_custom_call" | custom-call | bytes 3276800 | tf_op jit(solution)/shard_map/pallas_call | solution.py:147
  15.8 1.7 %collective-permute-start.8 = (bf16[4,10,2,80,128]{4,3,2,1,0:T(8,128)(2,1)S(1)}, bf16[4,10,2,80,128]{4,3,2,1,0:T(8,128)(2,1)}, u32[]{:S(2)}, u32[]{:S(2)}) collective-permute-start(bf16[4,10,2,80,128]{4,3,2,1,0:T(8,128)(2,1)S(1)} %shard_map.48), channel_id=1, source_target_pairs={{0,1},{1,0},{2,3},{3,2},{4,5},{5,4},{6,7},{7,6},{8,9},{9,8},{10,11... | collective-permute-start | bytes 4915208 | tf_op jit(solution)/shard_map/ppermute | solution.py:223
  17.5 2.3 %shard_map.47 = (bf16[10,2,80,128]{3,2,1,0:T(8,128)(2,1)S(1)}, bf16[10,2,80,128]{3,2,1,0:T(8,128)(2,1)S(1)}, bf16[10,2,80,128]{3,2,1,0:T(8,128)(2,1)S(1)}, bf16[10,2,80,128]{3,2,1,0:T(8,128)(2,1)S(1)}) custom-call(s32[3]{0:T(128)S(1)} %get-tuple-element.90.place_ref, bf16[40,64,640]{2,1,0:T(8,128)(2,1)S(1)} %bitcast.55, bf16[40,64,640]{2,1,0:T(8,128)(2,1)S(1)} %bitcast.56), custom_call_target="tpu_custom_call" | custom-call | bytes 3276800 | tf_op jit(solution)/shard_map/pallas_call | solution.py:147
  19.8 0.7 copy-done
  20.6 0.7 copy-done.1
  21.3 0.8 copy-done.2
  22.1 0.7 fusion.4
  25.8 0.6 fusion.3
  28.3 0.0 collective-permute-done.5
  28.3 16.9 %collective-permute-done.6 = bf16[10,64,640]{2,1,0:T(8,128)(2,1)} collective-permute-done((bf16[10,64,640]{2,1,0:T(8,128)(2,1)}, bf16[10,64,640]{2,1,0:T(8,128)(2,1)}, u32[]{:S(2)}, u32[]{:S(2)}) %collective-permute-start.6) | collective-permute-done | bytes 819232 | tf_op jit(solution)/shard_map/ppermute | solution.py:219
  45.2 0.0 collective-permute-done.7
  45.2 24.5 %conditional.1 = (bf16[5,128,640]{2,1,0:T(8,128)(2,1)}) conditional(s32[]{:T(128)} %clamp.3, () %tuple.19, (s32[]{:T(128)}, bf16[10,64,640]{2,1,0:T(8,128)(2,1)}, bf16[10,64,640]{2,1,0:T(8,128)(2,1)}, bf16[10,64,640]{2,1,0:T(8,128)(2,1)}, bf16[10,64,640]{2,1,0:T(8,128)(2,1)}) %tuple.20, (s32[]{:T(128)}, s32[2]{0:T(128)S(1)}, ...), branch_computations={%region_0.1_spmd, %region_1.2_spmd, %region_2.3_spmd} | conditional | flops 1228805 | bytes 23757018 | solution.py:259
  47.2 1.6 select_select_fusion
  48.8 1.7 %collective-permute-start = (bf16[10,64,640]{2,1,0:T(8,128)(2,1)S(1)}, bf16[10,64,640]{2,1,0:T(8,128)(2,1)}, u32[]{:S(2)}, u32[]{:S(2)}) collective-permute-start(bf16[10,64,640]{2,1,0:T(8,128)(2,1)S(1)} %select_select_fusion), channel_id=1, source_target_pairs={{0,1},{1,0},{2,3},{3,2},{4,5},{5,4},{6,7},{7,6},{8,9},{9,8},{10,11... | collective-permute-start | bytes 2457608 | tf_op jit(solution)/shard_map/cond/branch_1_fun/ppermute | solution.py:223
  50.5 19.2 %collective-permute-done = bf16[10,64,640]{2,1,0:T(8,128)(2,1)} collective-permute-done((bf16[10,64,640]{2,1,0:T(8,128)(2,1)S(1)}, bf16[10,64,640]{2,1,0:T(8,128)(2,1)}, u32[]{:S(2)}, u32[]{:S(2)}) %collective-permute-start) | collective-permute-done | bytes 819232 | tf_op jit(solution)/shard_map/cond/branch_1_fun/ppermute | solution.py:223
  69.7 2.7 %shard_map.49 = bf16[64,56,128]{2,1,0:T(8,128)(2,1)} custom-call(s32[1]{0:T(128)} %bitcast.24.choice_ref, bf16[5,128,640]{2,1,0:T(8,128)(2,1)} %bitcast.67, bf16[5,128,640]{2,1,0:T(8,128)(2,1)} %bitcast.26.refs_1_, bf16[5,128,640]{2,1,0:T(8,128)(2,1)} %bitcast.27.refs_2_, bf16[5,128,640]{2,1,0:T(8,128)(2,1)} %bitcast.28.refs_3_, ...), custom_call_target="tpu_custom_call" | custom-call | bytes 1638400 | tf_op jit(solution)/shard_map/pallas_call | solution.py:107
  72.4 13.7 %all-to-all-start = ((bf16[64,56,128]{2,1,0:T(8,128)(2,1)}), bf16[64,56,128]{2,1,0:T(8,128)(2,1)S(1)}, u32[]{:S(2)}, u32[]{:S(2)}) async-start(bf16[64,56,128]{2,1,0:T(8,128)(2,1)} %shard_map.49), calls=%async_computation | async-start | bytes 1835008 | tf_op jit(solution)/shard_map/all_to_all | solution.py:266
  86.1 0.4 collective-permute-start.9
  86.5 1.7 %collective-permute-start.11 = (bf16[10,2,80,128]{3,2,1,0:T(8,128)(2,1)}, bf16[10,2,80,128]{3,2,1,0:T(8,128)(2,1)}, u32[]{:S(2)}, u32[]{:S(2)}) collective-permute-start(bf16[10,2,80,128]{3,2,1,0:T(8,128)(2,1)} %copy-done.1), channel_id=1, source_target_pairs={{0,8},{4,12},{8,0},{12,4},{1,9},{5,13},{9,1},{13,5},{2,10},{6,14},... | collective-permute-start | bytes 1228808 | tf_op jit(solution)/shard_map/ppermute | solution.py:219
  88.3 0.8 pad_add_fusion.3.source_ref
  89.0 1.0 collective-permute-start.13
  90.0 0.0 collective-permute-done.8
  90.0 2.5 %slice_bitcast_fusion = (bf16[10,2,80,128]{3,2,1,0:T(8,128)(2,1)}, bf16[10,2,80,128]{3,2,1,0:T(8,128)(2,1)}, bf16[10,2,80,128]{3,2,1,0:T(8,128)(2,1)}, bf16[1,10,2,80,128]{4,3,2,1,0:T(8,128)(2,1)S(1)}) fusion(bf16[4,10,2,80,128]{4,3,2,1,0:T(8,128)(2,1)} %collective-permute-done.8), kind=kLoop, calls=%fused_computation.4 | loop fusion | bytes 3276800 | tf_op jit(solution)/shard_map/squeeze | solution.py:263
  92.4 0.7 collective-permute-start.10
  93.1 1.5 collective-permute-start.12
  94.7 17.3 %all-to-all-done = bf16[64,56,128]{2,1,0:T(8,128)(2,1)S(1)} async-done(((bf16[64,56,128]{2,1,0:T(8,128)(2,1)}), bf16[64,56,128]{2,1,0:T(8,128)(2,1)S(1)}, u32[]{:S(2)}, u32[]{:S(2)}) %all-to-all-start) | async-done | bytes 917536 | tf_op jit(solution)/shard_map/all_to_all | solution.py:266
  111.9 0.9 shard_map.50
  112.8 0.9 collective-permute-start.14
  113.8 0.5 collective-permute-start.15
  114.3 2.0 %collective-permute-done.10 = bf16[10,2,80,128]{3,2,1,0:T(8,128)(2,1)S(1)} collective-permute-done((bf16[10,2,80,128]{3,2,1,0:T(8,128)(2,1)}, bf16[10,2,80,128]{3,2,1,0:T(8,128)(2,1)S(1)}, u32[]{:S(2)}, u32[]{:S(2)}) %collective-permute-start.10) | collective-permute-done | bytes 409632 | tf_op jit(solution)/shard_map/ppermute | solution.py:219
  116.3 7.7 %collective-permute-done.12 = bf16[10,2,80,128]{3,2,1,0:T(8,128)(2,1)S(1)} collective-permute-done((bf16[10,2,80,128]{3,2,1,0:T(8,128)(2,1)}, bf16[10,2,80,128]{3,2,1,0:T(8,128)(2,1)S(1)}, u32[]{:S(2)}, u32[]{:S(2)}) %collective-permute-start.12) | collective-permute-done | bytes 409632 | tf_op jit(solution)/shard_map/ppermute | solution.py:219
  124.0 0.8 collective-permute-done.14
  124.8 9.0 %collective-permute-done.15 = bf16[10,2,80,128]{3,2,1,0:T(8,128)(2,1)S(1)} collective-permute-done((bf16[10,2,80,128]{3,2,1,0:T(8,128)(2,1)S(1)}, bf16[10,2,80,128]{3,2,1,0:T(8,128)(2,1)S(1)}, u32[]{:S(2)}, u32[]{:S(2)}) %collective-permute-start.15) | collective-permute-done | bytes 409632 | tf_op jit(solution)/shard_map/ppermute | solution.py:223
  133.8 2.3 %shard_map.51 = f32[4,2,64,128]{3,2,1,0:T(8,128)S(1)} custom-call(bf16[1600,128]{1,0:T(8,128)(2,1)S(1)} %bitcast.61, bf16[1600,128]{1,0:T(8,128)(2,1)S(1)} %bitcast.59, bf16[1600,128]{1,0:T(8,128)(2,1)S(1)} %bitcast.62, bf16[1600,128]{1,0:T(8,128)(2,1)S(1)} %bitcast.63, bf16[1600,128]{1,0:T(8,128)(2,1)} %bitcast.13.refs_4_, bf16[1600,128]{1,0:T(8,128)(2,1)S(1)} %bitcast.64, ...), custom_call_target="tpu_custom_call" | custom-call | flops 838860800 | bytes 5242880 | tf_op jit(solution)/shard_map/pallas_call | solution.py:208
  136.2 0.7 collective-permute-start.18
  136.8 0.7 collective-permute-start.17
  137.6 2.0 %collective-permute-start.16 = (f32[2,64,128]{2,1,0:T(8,128)S(1)}, f32[2,64,128]{2,1,0:T(8,128)S(1)}, u32[]{:S(2)}, u32[]{:S(2)}) collective-permute-start(f32[2,64,128]{2,1,0:T(8,128)S(1)} %get-tuple-element.77), channel_id=1, source_target_pairs={{0,12},{4,0},{8,4},{12,8},{1,13},{5,1},{9,5},{13,9},{2,14},{6,2},{... | collective-permute-start | bytes 196616 | tf_op jit(solution)/shard_map/ppermute | solution.py:219
  139.6 1.0 collective-permute-done.18
  140.6 1.2 collective-permute-done.17
  141.8 0.3 collective-permute-done.16
  142.2 17.0 %all_to_all.10 = f32[32,4,128]{2,1,0:T(4,128)S(1)} all-to-all(f32[32,4,128]{2,1,0:T(4,128)S(1)} %bitcast.68), channel_id=1, replica_groups=mesh['zh'=2,'y'=4,'core'=2,'x'=4,'za'=2,'zb'=2] {'zb','zh','y','core'}, dimensions={0} | all-to-all | bytes 131072 | tf_op jit(solution)/shard_map/all_to_all | solution.py:273
  159.1 0.6 reduce_sum.9
  (13 shorter events, 0.1 us)
Async XLA Ops:
  5.1 23.2 %collective-permute-start.5 = (bf16[10,64,640]{2,1,0:T(8,128)(2,1)}, bf16[10,64,640]{2,1,0:T(8,128)(2,1)}, u32[]{:S(2)}, u32[]{:S(2)}) collective-permute-start(bf16[10,64,640]{2,1,0:T(8,128)(2,1)} %get-tuple-element.58), channel_id=1, source_target_pairs={{0,4},{4,8},{8,12},{12,0},{1,5},{5,9},{9,13},{13,1},{2,6},{6,10},{... | collective-permute-start | bytes 2457608 | tf_op jit(solution)/shard_map/ppermute | solution.py:219
  7.2 38.0 %collective-permute-start.6 = (bf16[10,64,640]{2,1,0:T(8,128)(2,1)}, bf16[10,64,640]{2,1,0:T(8,128)(2,1)}, u32[]{:S(2)}, u32[]{:S(2)}) collective-permute-start(bf16[10,64,640]{2,1,0:T(8,128)(2,1)} %get-tuple-element.59), channel_id=1, source_target_pairs={{0,8},{4,12},{8,0},{12,4},{1,9},{5,13},{9,1},{13,5},{2,10},{6,14},... | collective-permute-start | bytes 2457608 | tf_op jit(solution)/shard_map/ppermute | solution.py:219
  9.6 35.5 %collective-permute-start.7 = (bf16[10,64,640]{2,1,0:T(8,128)(2,1)S(1)}, bf16[10,64,640]{2,1,0:T(8,128)(2,1)}, u32[]{:S(2)}, u32[]{:S(2)}) collective-permute-start(bf16[10,64,640]{2,1,0:T(8,128)(2,1)S(1)} %get-tuple-element.60), channel_id=1, source_target_pairs={{0,12},{4,0},{8,4},{12,8},{1,13},{5,1},{9,5},{13,9},{2,14},{6,2},{... | collective-permute-start | bytes 2457608 | tf_op jit(solution)/shard_map/ppermute | solution.py:219
  15.8 74.2 %collective-permute-start.8 = (bf16[4,10,2,80,128]{4,3,2,1,0:T(8,128)(2,1)S(1)}, bf16[4,10,2,80,128]{4,3,2,1,0:T(8,128)(2,1)}, u32[]{:S(2)}, u32[]{:S(2)}) collective-permute-start(bf16[4,10,2,80,128]{4,3,2,1,0:T(8,128)(2,1)S(1)} %shard_map.48), channel_id=1, source_target_pairs={{0,1},{1,0},{2,3},{3,2},{4,5},{5,4},{6,7},{7,6},{8,9},{9,8},{10,11... | collective-permute-start | bytes 4915208 | tf_op jit(solution)/shard_map/ppermute | solution.py:223
  17.5 4.6 %copy-start.3 = (s32[2]{0:T(128)S(1)}, s32[2]{0:T(128)}, u32[]{:S(2)}) copy-start(s32[2]{0:T(128)} %owners_ref.1) | copy-start | bytes 28
  17.5 27.6 %copy-start.4 = (s32[2]{0:T(128)S(1)}, s32[2]{0:T(128)}, u32[]{:S(2)}) copy-start(s32[2]{0:T(128)} %offsets_ref.1) | copy-start | bytes 28
  19.8 0.7 copy-start
  20.6 0.7 copy-start.1
  21.3 0.8 copy-start.2
  48.8 20.9 %collective-permute-start = (bf16[10,64,640]{2,1,0:T(8,128)(2,1)S(1)}, bf16[10,64,640]{2,1,0:T(8,128)(2,1)}, u32[]{:S(2)}, u32[]{:S(2)}) collective-permute-start(bf16[10,64,640]{2,1,0:T(8,128)(2,1)S(1)} %select_select_fusion), channel_id=1, source_target_pairs={{0,1},{1,0},{2,3},{3,2},{4,5},{5,4},{6,7},{7,6},{8,9},{9,8},{10,11... | collective-permute-start | bytes 2457608 | tf_op jit(solution)/shard_map/cond/branch_1_fun/ppermute | solution.py:223
  72.4 39.6 %all-to-all-start = ((bf16[64,56,128]{2,1,0:T(8,128)(2,1)}), bf16[64,56,128]{2,1,0:T(8,128)(2,1)S(1)}, u32[]{:S(2)}, u32[]{:S(2)}) async-start(bf16[64,56,128]{2,1,0:T(8,128)(2,1)} %shard_map.49), calls=%async_computation | async-start | bytes 1835008 | tf_op jit(solution)/shard_map/all_to_all | solution.py:266
  86.1 26.7 %collective-permute-start.9 = (bf16[10,2,80,128]{3,2,1,0:T(8,128)(2,1)}, bf16[10,2,80,128]{3,2,1,0:T(8,128)(2,1)S(1)}, u32[]{:S(2)}, u32[]{:S(2)}) collective-permute-start(bf16[10,2,80,128]{3,2,1,0:T(8,128)(2,1)} %copy-done.2), channel_id=1, source_target_pairs={{0,4},{4,8},{8,12},{12,0},{1,5},{5,9},{9,13},{13,1},{2,6},{6,10},{... | collective-permute-start | bytes 1228808 | tf_op jit(solution)/shard_map/ppermute | solution.py:219
  86.5 27.2 %collective-permute-start.11 = (bf16[10,2,80,128]{3,2,1,0:T(8,128)(2,1)}, bf16[10,2,80,128]{3,2,1,0:T(8,128)(2,1)}, u32[]{:S(2)}, u32[]{:S(2)}) collective-permute-start(bf16[10,2,80,128]{3,2,1,0:T(8,128)(2,1)} %copy-done.1), channel_id=1, source_target_pairs={{0,8},{4,12},{8,0},{12,4},{1,9},{5,13},{9,1},{13,5},{2,10},{6,14},... | collective-permute-start | bytes 1228808 | tf_op jit(solution)/shard_map/ppermute | solution.py:219
  89.0 25.3 %collective-permute-start.13 = (bf16[10,2,80,128]{3,2,1,0:T(8,128)(2,1)}, bf16[10,2,80,128]{3,2,1,0:T(8,128)(2,1)}, u32[]{:S(2)}, u32[]{:S(2)}) collective-permute-start(bf16[10,2,80,128]{3,2,1,0:T(8,128)(2,1)} %copy-done), channel_id=1, source_target_pairs={{0,12},{4,0},{8,4},{12,8},{1,13},{5,1},{9,5},{13,9},{2,14},{6,2},{... | collective-permute-start | bytes 1228808 | tf_op jit(solution)/shard_map/ppermute | solution.py:219
  92.4 23.9 %collective-permute-start.10 = (bf16[10,2,80,128]{3,2,1,0:T(8,128)(2,1)}, bf16[10,2,80,128]{3,2,1,0:T(8,128)(2,1)S(1)}, u32[]{:S(2)}, u32[]{:S(2)}) collective-permute-start(bf16[10,2,80,128]{3,2,1,0:T(8,128)(2,1)} %get-tuple-element.75), channel_id=1, source_target_pairs={{0,4},{4,8},{8,12},{12,0},{1,5},{5,9},{9,13},{13,1},{2,6},{6,10},{... | collective-permute-start | bytes 1228808 | tf_op jit(solution)/shard_map/ppermute | solution.py:219
  93.1 30.9 %collective-permute-start.12 = (bf16[10,2,80,128]{3,2,1,0:T(8,128)(2,1)}, bf16[10,2,80,128]{3,2,1,0:T(8,128)(2,1)S(1)}, u32[]{:S(2)}, u32[]{:S(2)}) collective-permute-start(bf16[10,2,80,128]{3,2,1,0:T(8,128)(2,1)} %get-tuple-element.74), channel_id=1, source_target_pairs={{0,8},{4,12},{8,0},{12,4},{1,9},{5,13},{9,1},{13,5},{2,10},{6,14},... | collective-permute-start | bytes 1228808 | tf_op jit(solution)/shard_map/ppermute | solution.py:219
  112.8 12.0 %collective-permute-start.14 = (bf16[10,2,80,128]{3,2,1,0:T(8,128)(2,1)}, bf16[10,2,80,128]{3,2,1,0:T(8,128)(2,1)S(1)}, u32[]{:S(2)}, u32[]{:S(2)}) collective-permute-start(bf16[10,2,80,128]{3,2,1,0:T(8,128)(2,1)} %get-tuple-element.73), channel_id=1, source_target_pairs={{0,12},{4,0},{8,4},{12,8},{1,13},{5,1},{9,5},{13,9},{2,14},{6,2},{... | collective-permute-start | bytes 1228808 | tf_op jit(solution)/shard_map/ppermute | solution.py:219
  113.8 20.1 %collective-permute-start.15 = (bf16[10,2,80,128]{3,2,1,0:T(8,128)(2,1)S(1)}, bf16[10,2,80,128]{3,2,1,0:T(8,128)(2,1)S(1)}, u32[]{:S(2)}, u32[]{:S(2)}) collective-permute-start(bf16[10,2,80,128]{3,2,1,0:T(8,128)(2,1)S(1)} %shard_map.50), channel_id=1, source_target_pairs={{0,2},{1,3},{2,0},{3,1},{4,6},{5,7},{6,4},{7,5},{8,10},{9,11},{10,... | collective-permute-start | bytes 1228808 | tf_op jit(solution)/shard_map/ppermute | solution.py:223
  136.2 4.4 %collective-permute-start.18 = (f32[2,64,128]{2,1,0:T(8,128)S(1)}, f32[2,64,128]{2,1,0:T(8,128)S(1)}, u32[]{:S(2)}, u32[]{:S(2)}) collective-permute-start(f32[2,64,128]{2,1,0:T(8,128)S(1)} %get-tuple-element.78), channel_id=1, source_target_pairs={{0,4},{4,8},{8,12},{12,0},{1,5},{5,9},{9,13},{13,1},{2,6},{6,10},{... | collective-permute-start | bytes 196616 | tf_op jit(solution)/shard_map/ppermute | solution.py:219
  136.8 5.0 %collective-permute-start.17 = (f32[2,64,128]{2,1,0:T(8,128)S(1)}, f32[2,64,128]{2,1,0:T(8,128)S(1)}, u32[]{:S(2)}, u32[]{:S(2)}) collective-permute-start(f32[2,64,128]{2,1,0:T(8,128)S(1)} %get-tuple-element.79), channel_id=1, source_target_pairs={{0,8},{4,12},{8,0},{12,4},{1,9},{5,13},{9,1},{13,5},{2,10},{6,14},... | collective-permute-start | bytes 196616 | tf_op jit(solution)/shard_map/ppermute | solution.py:219
  137.6 4.6 %collective-permute-start.16 = (f32[2,64,128]{2,1,0:T(8,128)S(1)}, f32[2,64,128]{2,1,0:T(8,128)S(1)}, u32[]{:S(2)}, u32[]{:S(2)}) collective-permute-start(f32[2,64,128]{2,1,0:T(8,128)S(1)} %get-tuple-element.77), channel_id=1, source_target_pairs={{0,12},{4,0},{8,4},{12,8},{1,13},{5,1},{9,5},{13,9},{2,14},{6,2},{... | collective-permute-start | bytes 196616 | tf_op jit(solution)/shard_map/ppermute | solution.py:219

commit v4 on v3

--- a/solution.py
+++ b/solution.py
@@ -1,3 +1,5 @@
+import functools
+
 import jax
 import jax.numpy as jnp
 from jax import lax
@@ -30,8 +32,8 @@
     return pl.CostEstimate(flops=flops, bytes_accessed=moved, transcendentals=0)
 
 
-def slice_kernel(owners_ref, offsets_ref, integrals_ref, *refs):
-    out_refs, (held, rows, sems) = refs[:X], refs[X:]
+def slice_kernel(steps, owners_ref, offsets_ref, integrals_ref, *refs):
+    out_refs, (held, rows, sems) = refs[: len(steps)], refs[len(steps) :]
     i = pl.program_id(0)
     x = lax.axis_index("x")
     owns_second = jnp.logical_and(x * ZL + 2 * lax.axis_index("za") + lax.axis_index("zb") == owners_ref[1], owners_ref[0] != owners_ref[1])
@@ -55,46 +57,46 @@
     for t in range(NV // LANES):
         lanes = slice(t * LANES, (t + 1) * LANES)
         rows[...] = held[i, :, :, lanes].astype(jnp.float32).reshape(CHUNK * BLOCK, LANES)
-        for k in range(X):
+        for out_ref, k in zip(out_refs, steps):
             first = lax.rem(x + k, X) * PIECE
             for m in range(PIECE):
-                out_refs[k][m, :, lanes] = rows[pl.ds(first + m, CHUNK, stride=BLOCK), :].astype(jnp.bfloat16)
-
-
-def slice_panel(integrals, owners, offsets):
+                out_ref[m, :, lanes] = rows[pl.ds(first + m, CHUNK, stride=BLOCK), :].astype(jnp.bfloat16)
+
+
+def slice_panel(steps, integrals, owners, offsets):
     piece = jax.ShapeDtypeStruct((PIECE, PR, NV), jnp.bfloat16)
     return pl.pallas_call(
-        slice_kernel,
+        functools.partial(slice_kernel, steps),
         grid_spec=pltpu.PrefetchScalarGridSpec(
             num_scalar_prefetch=2,
             grid=(PR // CHUNK,),
             in_specs=[pl.BlockSpec(memory_space=pl.ANY)],
-            out_specs=[pl.BlockSpec((PIECE, CHUNK, NV), lambda i, owners, offsets: (0, i, 0))] * X,
+            out_specs=[pl.BlockSpec((PIECE, CHUNK, NV), lambda i, owners, offsets: (0, i, 0))] * len(steps),
             scratch_shapes=[
                 pltpu.VMEM((PR // CHUNK, CHUNK, BLOCK, NV), jnp.bfloat16),
                 pltpu.VMEM((CHUNK * BLOCK, LANES), jnp.float32),
                 pltpu.SemaphoreType.DMA((PR // CHUNK,)),
             ],
         ),
-        out_shape=[piece] * X,
+        out_shape=[piece] * len(steps),
         compiler_params=pltpu.CompilerParams(vmem_limit_bytes=24 * 2**20),
         cost_estimate=cost(0, 4 * PR * BLOCK * NV),
     )(owners, offsets, integrals)
 
 
 def turn_kernel(choice_ref, *refs):
-    piece_refs, out_ref, (held, turned, message, sem) = refs[: X + 1], refs[X + 1], refs[X + 2 :]
+    piece_refs, out_ref, (held, turned, message, sems) = refs[: X + 1], refs[X + 1], refs[X + 2 :]
     for k in range(X + 1):
 
         @pl.when(choice_ref[0] == k)
         def _():
-            copy = pltpu.make_async_copy(piece_refs[k], held, sem)
-            copy.start()
-            copy.wait()
-
+            for half in range(HALF):
+                pltpu.make_async_copy(piece_refs[k].at[half], held.at[half], sems.at[half]).start()
+
+    message[...] = jnp.zeros_like(message)
     for half in range(HALF):
+        pltpu.make_async_copy(piece_refs[0].at[half], held.at[half], sems.at[half]).wait()
         turned[half * NV : (half + 1) * NV, :] = held[half].T.astype(jnp.float32)
-    message[...] = jnp.zeros_like(message)
     for half in range(HALF):
         for e in range(PIECE):
             rows = turned[pl.ds(half * NV + e, ROWS * ZL, stride=PIECE), :]
@@ -115,7 +117,7 @@
                 pltpu.VMEM((HALF, LANES, NV), jnp.bfloat16),
                 pltpu.VMEM((HALF * NV, LANES), jnp.float32),
                 pltpu.VMEM((ROWS * ZL * MESSAGE, LANES), jnp.float32),
-                pltpu.SemaphoreType.DMA,
+                pltpu.SemaphoreType.DMA((HALF,)),
             ],
         ),
         out_shape=jax.ShapeDtypeStruct((ROWS * ZL, MESSAGE, LANES), jnp.bfloat16),
@@ -224,8 +226,10 @@
 
 
 def over_x(integrals, owners, offsets):
-    pieces = slice_panel(integrals, owners, offsets)
-    return [pieces[0]] + [shift_x(pieces[k], k) for k in range(1, X)]
+    pieces = slice_panel((1, 2, 3), integrals, owners, offsets)
+    got = [shift_x(pieces[k - 1], k) for k in range(1, X)]
+    owners, _ = lax.optimization_barrier((owners, pieces[0]))
+    return list(slice_panel((0,), integrals, owners, offsets)) + got
 
 
 def local(amplitudes, integrals, owners, offsets):
@@ -246,7 +250,11 @@
     got, owns = lax.optimization_barrier((got, owns))
 
     def stay(*operands):
-        return jnp.zeros((PIECE, PR, NV), jnp.bfloat16)
+        return pl.pallas_call(
+            lambda out_ref: None,
+            out_specs=pl.BlockSpec(memory_space=pl.ANY),
+            out_shape=jax.ShapeDtypeStruct((PIECE, PR, NV), jnp.bfloat16),
+        )()
 
     def move(place, owners, offsets, integrals, *got):
         return swap_zl(lax.select_n(place, *got), 1)

time: 160 us -> 136 us (0.85)
  waiting for transfers between devices: 75.5 us -> 52.9 us
  Pallas kernels: 15.6 us -> 18.4 us
  loops' own time: 2.03 us -> 0.01 us
    ppermute x3 -> x2, waiting for transfers between devices: 28.2 us -> 9.87 us  [swap_zl(): return lax.ppermute(array, Z, [(z, z ^ bit) for z in range(ZL)])]
    ppermute x12, waiting for transfers between devices: 30 us -> 26.1 us  [shift_x(): return lax.ppermute(array, 'x', [(x, (x + k) % X) for x in range(X)])]
    pallas_call x1 -> x3, Pallas kernels: 5.05 us -> 7.77 us  [the longest x2 7.77 us: slice_panel(): pl.pallas_call(functools.partial(slice_kernel, steps), grid_spec=pltpu.Pr...]
    another operation x1, loops' own time: 2.03 us -> 0.01 us  [local(): lax.switch(case, [stay, move, again], distance[1], owners, offsets, integ...]
    ppermute x3 -> x2, starting transfers between devices: 3.99 us -> 2.26 us  [swap_zl(): return lax.ppermute(array, Z, [(z, z ^ bit) for z in range(ZL)])]
    unnamed x11 -> x15, local copies, waits for them, and re-layouts: 4.76 us -> 4.95 us
  transfers between devices with their start and end apart: 16 -> 15, of which waited for: 10 -> 7; matrix products, arithmetic and copies ran while one was open for 5% -> 5% of each run, Pallas kernels for 5% -> 8%
where the time goes in v4:
time: 136 us
  waiting for transfers between devices  52.9 us (39%)
  starting transfers between devices  31.8 us (23%)
  Pallas kernels  18.4 us (14%)
  blocking collectives  17 us (12%)
  local copies, waits for them, and re-layouts  8.64 us (6%)
  between operations  5.33 us (4%)
  other arithmetic  1.49 us (1%)
    ppermute x12, waiting for transfers between devices, shift_x(): return lax.ppermute(array, 'x', [(x, (x + k) % X) for x in range(X)])  26.1 us
    all_to_all x1, blocking collectives, local(): lax.all_to_all(total.reshape(2 * ROWS, PAIRS // ROWS, LANES), ('zb',) + R...  17 us
    all_to_all x1, waiting for transfers between devices, local(): spread = lax.all_to_all(message, ROW + Z, 0, 0, tiled=True)  16.8 us
    ppermute x12, starting transfers between devices, shift_x(): return lax.ppermute(array, 'x', [(x, (x + k) % X) for x in range(X)])  16.4 us
    all_to_all x1, starting transfers between devices, local(): spread = lax.all_to_all(message, ROW + Z, 0, 0, tiled=True)  13.2 us
    ppermute x2, waiting for transfers between devices, swap_zl(): return lax.ppermute(array, Z, [(z, z ^ bit) for z in range(ZL)])  9.87 us
    pallas_call x2, Pallas kernels, slice_panel(): pl.pallas_call(functools.partial(slice_kernel, steps), grid_spec=pltpu.Pr...  7.77 us
    unnamed x15, local copies, waits for them, and re-layouts  4.95 us
  transfers between devices with their start and end apart: 15, of which 7 were waited for; matrix products, arithmetic and copies ran while one was open for 5% of the time, Pallas kernels for 8%

profile of v4, /device:TPU:1, one launch (start us, length us, event | category | flops | bytes accessed | tf_op | source)
XLA Modules:
  0.0 135.5 jit_solution(916999480407733033)
XLA Ops:
  0.0 4.7 %shard_map.46 = (bf16[10,64,640]{2,1,0:T(8,128)(2,1)}, bf16[10,64,640]{2,1,0:T(8,128)(2,1)}, bf16[10,64,640]{2,1,0:T(8,128)(2,1)S(1)}) custom-call(s32[2]{0:T(128)} %owners_ref.2, s32[2]{0:T(128)} %offsets_ref.3, bf16[96,40,640]{2,1,0:T(8,128)(2,1)} %integrals_ref.3), custom_call_target="tpu_custom_call" | custom-call | bytes 6553600 | tf_op jit(solution)/shard_map/pallas_call | solution.py:68
  4.7 2.1 %collective-permute-start.5 = (bf16[10,64,640]{2,1,0:T(8,128)(2,1)}, bf16[10,64,640]{2,1,0:T(8,128)(2,1)}, u32[]{:S(2)}, u32[]{:S(2)}) collective-permute-start(bf16[10,64,640]{2,1,0:T(8,128)(2,1)} %get-tuple-element.57), channel_id=1, source_target_pairs={{0,4},{4,8},{8,12},{12,0},{1,5},{5,9},{9,13},{13,1},{2,6},{6,10},{... | collective-permute-start | bytes 2457608 | tf_op jit(solution)/shard_map/ppermute | solution.py:221
  6.8 2.4 %collective-permute-start.6 = (bf16[10,64,640]{2,1,0:T(8,128)(2,1)}, bf16[10,64,640]{2,1,0:T(8,128)(2,1)}, u32[]{:S(2)}, u32[]{:S(2)}) collective-permute-start(bf16[10,64,640]{2,1,0:T(8,128)(2,1)} %get-tuple-element.59), channel_id=1, source_target_pairs={{0,8},{4,12},{8,0},{12,4},{1,9},{5,13},{9,1},{13,5},{2,10},{6,14},... | collective-permute-start | bytes 2457608 | tf_op jit(solution)/shard_map/ppermute | solution.py:221
  9.3 1.2 collective-permute-start.7
  10.4 2.7 %copy.7 = bf16[64,640,40]{1,0,2:T(8,128)(2,1)S(1)} copy(bf16[64,640,40]{1,2,0:T(8,128)(2,1)} %param.7) | data formatting | bytes 6553600 | tf_op args[0]
  13.1 0.1 pad_add_fusion.1
  13.2 2.4 %shard_map.49 = bf16[4,10,2,80,128]{4,3,2,1,0:T(8,128)(2,1)S(1)} custom-call(s32[3]{0:T(128)S(1)} %get-tuple-element.91.place_ref, bf16[40,64,640]{2,1,0:T(8,128)(2,1)S(1)} %bitcast.54, bf16[40,64,640]{2,1,0:T(8,128)(2,1)S(1)} %bitcast.55), custom_call_target="tpu_custom_call" | custom-call | bytes 3276800 | tf_op jit(solution)/shard_map/pallas_call | solution.py:149
  15.6 1.7 %collective-permute-start.8 = (bf16[4,10,2,80,128]{4,3,2,1,0:T(8,128)(2,1)S(1)}, bf16[4,10,2,80,128]{4,3,2,1,0:T(8,128)(2,1)}, u32[]{:S(2)}, u32[]{:S(2)}) collective-permute-start(bf16[4,10,2,80,128]{4,3,2,1,0:T(8,128)(2,1)S(1)} %shard_map.49), channel_id=1, source_target_pairs={{0,1},{1,0},{2,3},{3,2},{4,5},{5,4},{6,7},{7,6},{8,9},{9,8},{10,11... | collective-permute-start | bytes 4915208 | tf_op jit(solution)/shard_map/ppermute | solution.py:225
  17.3 3.1 %shard_map.47 = bf16[10,64,640]{2,1,0:T(8,128)(2,1)} custom-call(s32[2]{0:T(128)S(1)} %copy-done.4, s32[2]{0:T(128)S(1)} %copy-done.5, bf16[96,40,640]{2,1,0:T(8,128)(2,1)S(1)} %bitcast.69), custom_call_target="tpu_custom_call" | custom-call | bytes 6553600 | tf_op jit(solution)/shard_map/pallas_call | solution.py:68
  20.4 2.3 %shard_map.48 = (bf16[10,2,80,128]{3,2,1,0:T(8,128)(2,1)S(1)}, bf16[10,2,80,128]{3,2,1,0:T(8,128)(2,1)S(1)}, bf16[10,2,80,128]{3,2,1,0:T(8,128)(2,1)S(1)}, bf16[10,2,80,128]{3,2,1,0:T(8,128)(2,1)S(1)}) custom-call(s32[3]{0:T(128)S(1)} %get-tuple-element.90.place_ref, bf16[40,64,640]{2,1,0:T(8,128)(2,1)S(1)} %bitcast.56, bf16[40,64,640]{2,1,0:T(8,128)(2,1)S(1)} %bitcast.57), custom_call_target="tpu_custom_call" | custom-call | bytes 3276800 | tf_op jit(solution)/shard_map/pallas_call | solution.py:149
  22.7 0.7 copy-done
  23.5 0.8 copy-done.1
  24.2 0.8 copy-done.2
  25.0 0.7 fusion.4
  28.9 0.6 fusion.3
  31.5 0.0 collective-permute-done.5
  31.5 13.3 %collective-permute-done.6 = bf16[10,64,640]{2,1,0:T(8,128)(2,1)} collective-permute-done((bf16[10,64,640]{2,1,0:T(8,128)(2,1)}, bf16[10,64,640]{2,1,0:T(8,128)(2,1)}, u32[]{:S(2)}, u32[]{:S(2)}) %collective-permute-start.6) | collective-permute-done | bytes 819232 | tf_op jit(solution)/shard_map/ppermute | solution.py:221
  44.8 0.0 collective-permute-done.7
  44.8 2.8 %shard_map.50 = bf16[64,56,128]{2,1,0:T(8,128)(2,1)} custom-call(s32[1]{0:T(128)} %bitcast.25.choice_ref, bf16[5,128,640]{2,1,0:T(8,128)(2,1)} %bitcast.70, bf16[5,128,640]{2,1,0:T(8,128)(2,1)} %bitcast.27.refs_1_, bf16[5,128,640]{2,1,0:T(8,128)(2,1)} %bitcast.28.refs_2_, bf16[5,128,640]{2,1,0:T(8,128)(2,1)} %bitcast.29.refs_3_, ...), custom_call_target="tpu_custom_call" | custom-call | bytes 1638400 | tf_op jit(solution)/shard_map/pallas_call | solution.py:109
  47.6 13.2 %all-to-all-start = ((bf16[64,56,128]{2,1,0:T(8,128)(2,1)}), bf16[64,56,128]{2,1,0:T(8,128)(2,1)S(1)}, u32[]{:S(2)}, u32[]{:S(2)}) async-start(bf16[64,56,128]{2,1,0:T(8,128)(2,1)} %shard_map.50), calls=%async_computation | async-start | bytes 1835008 | tf_op jit(solution)/shard_map/all_to_all | solution.py:274
  60.8 0.9 collective-permute-start.9
  61.7 2.3 %collective-permute-start.11 = (bf16[10,2,80,128]{3,2,1,0:T(8,128)(2,1)}, bf16[10,2,80,128]{3,2,1,0:T(8,128)(2,1)}, u32[]{:S(2)}, u32[]{:S(2)}) collective-permute-start(bf16[10,2,80,128]{3,2,1,0:T(8,128)(2,1)} %copy-done.1), channel_id=1, source_target_pairs={{0,8},{4,12},{8,0},{12,4},{1,9},{5,13},{9,1},{13,5},{2,10},{6,14},... | collective-permute-start | bytes 1228808 | tf_op jit(solution)/shard_map/ppermute | solution.py:221
  64.0 0.8 pad_add_fusion.3.source_ref
  64.8 1.3 collective-permute-start.13
  66.1 0.0 collective-permute-done.8
  66.1 2.4 %slice_bitcast_fusion = (bf16[10,2,80,128]{3,2,1,0:T(8,128)(2,1)}, bf16[10,2,80,128]{3,2,1,0:T(8,128)(2,1)}, bf16[10,2,80,128]{3,2,1,0:T(8,128)(2,1)}, bf16[1,10,2,80,128]{4,3,2,1,0:T(8,128)(2,1)S(1)}) fusion(bf16[4,10,2,80,128]{4,3,2,1,0:T(8,128)(2,1)} %collective-permute-done.8), kind=kLoop, calls=%fused_computation.4 | loop fusion | bytes 3276800 | tf_op jit(solution)/shard_map/squeeze | solution.py:271
  68.5 0.2 collective-permute-start.10
  68.7 1.0 collective-permute-start.12
  69.7 16.8 %all-to-all-done = bf16[64,56,128]{2,1,0:T(8,128)(2,1)S(1)} async-done(((bf16[64,56,128]{2,1,0:T(8,128)(2,1)}), bf16[64,56,128]{2,1,0:T(8,128)(2,1)S(1)}, u32[]{:S(2)}, u32[]{:S(2)}) %all-to-all-start) | async-done | bytes 917536 | tf_op jit(solution)/shard_map/all_to_all | solution.py:274
  86.6 0.9 shard_map.51
  87.4 0.0 collective-permute-done.9
  87.4 2.1 %collective-permute-start.14 = (bf16[10,2,80,128]{3,2,1,0:T(8,128)(2,1)}, bf16[10,2,80,128]{3,2,1,0:T(8,128)(2,1)S(1)}, u32[]{:S(2)}, u32[]{:S(2)}) collective-permute-start(bf16[10,2,80,128]{3,2,1,0:T(8,128)(2,1)} %get-tuple-element.73), channel_id=1, source_target_pairs={{0,12},{4,0},{8,4},{12,8},{1,13},{5,1},{9,5},{13,9},{2,14},{6,2},{... | collective-permute-start | bytes 1228808 | tf_op jit(solution)/shard_map/ppermute | solution.py:221
  89.5 0.0 collective-permute-done.11
  89.5 0.5 collective-permute-start.15
  90.0 0.0 collective-permute-done.13
  90.1 0.4 collective-permute-done.10
  90.4 9.3 %collective-permute-done.12 = bf16[10,2,80,128]{3,2,1,0:T(8,128)(2,1)S(1)} collective-permute-done((bf16[10,2,80,128]{3,2,1,0:T(8,128)(2,1)}, bf16[10,2,80,128]{3,2,1,0:T(8,128)(2,1)S(1)}, u32[]{:S(2)}, u32[]{:S(2)}) %collective-permute-start.12) | collective-permute-done | bytes 409632 | tf_op jit(solution)/shard_map/ppermute | solution.py:221
  99.7 0.0 collective-permute-done.14
  99.7 9.9 %collective-permute-done.15 = bf16[10,2,80,128]{3,2,1,0:T(8,128)(2,1)S(1)} collective-permute-done((bf16[10,2,80,128]{3,2,1,0:T(8,128)(2,1)S(1)}, bf16[10,2,80,128]{3,2,1,0:T(8,128)(2,1)S(1)}, u32[]{:S(2)}, u32[]{:S(2)}) %collective-permute-start.15) | collective-permute-done | bytes 409632 | tf_op jit(solution)/shard_map/ppermute | solution.py:225
  109.6 2.3 %shard_map.52 = f32[4,2,64,128]{3,2,1,0:T(8,128)S(1)} custom-call(bf16[1600,128]{1,0:T(8,128)(2,1)S(1)} %bitcast.62, bf16[1600,128]{1,0:T(8,128)(2,1)S(1)} %bitcast.60, bf16[1600,128]{1,0:T(8,128)(2,1)S(1)} %bitcast.63, bf16[1600,128]{1,0:T(8,128)(2,1)S(1)} %bitcast.64, bf16[1600,128]{1,0:T(8,128)(2,1)} %bitcast.14.refs_4_, bf16[1600,128]{1,0:T(8,128)(2,1)S(1)} %bitcast.65, ...), custom_call_target="tpu_custom_call" | custom-call | flops 838860800 | bytes 5242880 | tf_op jit(solution)/shard_map/pallas_call | solution.py:210
  111.9 0.1 collective-permute-start.18
  112.0 1.9 %collective-permute-start.17 = (f32[2,64,128]{2,1,0:T(8,128)S(1)}, f32[2,64,128]{2,1,0:T(8,128)S(1)}, u32[]{:S(2)}, u32[]{:S(2)}) collective-permute-start(f32[2,64,128]{2,1,0:T(8,128)S(1)} %get-tuple-element.79), channel_id=1, source_target_pairs={{0,8},{4,12},{8,0},{12,4},{1,9},{5,13},{9,1},{13,5},{2,10},{6,14},... | collective-permute-start | bytes 196616 | tf_op jit(solution)/shard_map/ppermute | solution.py:221
  113.9 0.8 collective-permute-start.16
  114.7 2.3 %collective-permute-done.18 = f32[2,64,128]{2,1,0:T(8,128)S(1)} collective-permute-done((f32[2,64,128]{2,1,0:T(8,128)S(1)}, f32[2,64,128]{2,1,0:T(8,128)S(1)}, u32[]{:S(2)}, u32[]{:S(2)}) %collective-permute-start.18) | collective-permute-done | bytes 65568 | tf_op jit(solution)/shard_map/ppermute | solution.py:221
  117.0 0.0 collective-permute-done.17
  117.0 0.9 collective-permute-done.16
  117.9 17.0 %all_to_all.10 = f32[32,4,128]{2,1,0:T(4,128)S(1)} all-to-all(f32[32,4,128]{2,1,0:T(4,128)S(1)} %bitcast.71), channel_id=1, replica_groups=mesh['zh'=2,'y'=4,'core'=2,'x'=4,'za'=2,'zb'=2] {'zb','zh','y','core'}, dimensions={0} | all-to-all | bytes 131072 | tf_op jit(solution)/shard_map/all_to_all | solution.py:281
  134.9 0.6 reduce_sum.9
  (17 shorter events, 0.1 us)
Async XLA Ops:
  4.7 26.8 %collective-permute-start.5 = (bf16[10,64,640]{2,1,0:T(8,128)(2,1)}, bf16[10,64,640]{2,1,0:T(8,128)(2,1)}, u32[]{:S(2)}, u32[]{:S(2)}) collective-permute-start(bf16[10,64,640]{2,1,0:T(8,128)(2,1)} %get-tuple-element.57), channel_id=1, source_target_pairs={{0,4},{4,8},{8,12},{12,0},{1,5},{5,9},{9,13},{13,1},{2,6},{6,10},{... | collective-permute-start | bytes 2457608 | tf_op jit(solution)/shard_map/ppermute | solution.py:221
  6.8 38.0 %collective-permute-start.6 = (bf16[10,64,640]{2,1,0:T(8,128)(2,1)}, bf16[10,64,640]{2,1,0:T(8,128)(2,1)}, u32[]{:S(2)}, u32[]{:S(2)}) collective-permute-start(bf16[10,64,640]{2,1,0:T(8,128)(2,1)} %get-tuple-element.59), channel_id=1, source_target_pairs={{0,8},{4,12},{8,0},{12,4},{1,9},{5,13},{9,1},{13,5},{2,10},{6,14},... | collective-permute-start | bytes 2457608 | tf_op jit(solution)/shard_map/ppermute | solution.py:221
  9.3 35.5 %collective-permute-start.7 = (bf16[10,64,640]{2,1,0:T(8,128)(2,1)S(1)}, bf16[10,64,640]{2,1,0:T(8,128)(2,1)}, u32[]{:S(2)}, u32[]{:S(2)}) collective-permute-start(bf16[10,64,640]{2,1,0:T(8,128)(2,1)S(1)} %get-tuple-element.60), channel_id=1, source_target_pairs={{0,12},{4,0},{8,4},{12,8},{1,13},{5,1},{9,5},{13,9},{2,14},{6,2},{... | collective-permute-start | bytes 2457608 | tf_op jit(solution)/shard_map/ppermute | solution.py:221
  10.4 6.9 %slice-start = ((s8[4915200]{0:T(1024)(128)(4,1)}), s8[4194304]{0:T(1024)(128)(4,1)S(1)}, s32[]{:S(2)}) async-start(s8[4915200]{0:T(1024)(128)(4,1)} %bitcast.68), calls=%async_computation.2 | async-start | bytes 8388608
  13.2 4.2 %slice-start.1 = ((s8[4915200]{0:T(1024)(128)(4,1)}), s8[720896]{0:T(1024)(128)(4,1)S(1)}, s32[]{:S(2)}) async-start(s8[4915200]{0:T(1024)(128)(4,1)} %bitcast.68), calls=%async_computation.3 | async-start | bytes 1441792
  13.2 4.2 %copy-start.4 = (s32[2]{0:T(128)S(1)}, s32[2]{0:T(128)}, u32[]{:S(2)}) copy-start(s32[2]{0:T(128)} %owners_ref.2) | copy-start | bytes 28
  13.2 4.2 %copy-start.5 = (s32[2]{0:T(128)S(1)}, s32[2]{0:T(128)}, u32[]{:S(2)}) copy-start(s32[2]{0:T(128)} %offsets_ref.3) | copy-start | bytes 28
  15.6 50.5 %collective-permute-start.8 = (bf16[4,10,2,80,128]{4,3,2,1,0:T(8,128)(2,1)S(1)}, bf16[4,10,2,80,128]{4,3,2,1,0:T(8,128)(2,1)}, u32[]{:S(2)}, u32[]{:S(2)}) collective-permute-start(bf16[4,10,2,80,128]{4,3,2,1,0:T(8,128)(2,1)S(1)} %shard_map.49), channel_id=1, source_target_pairs={{0,1},{1,0},{2,3},{3,2},{4,5},{5,4},{6,7},{7,6},{8,9},{9,8},{10,11... | collective-permute-start | bytes 4915208 | tf_op jit(solution)/shard_map/ppermute | solution.py:225
  22.7 0.8 copy-start
  23.5 0.8 copy-start.1
  24.2 0.8 copy-start.2
  47.6 39.0 %all-to-all-start = ((bf16[64,56,128]{2,1,0:T(8,128)(2,1)}), bf16[64,56,128]{2,1,0:T(8,128)(2,1)S(1)}, u32[]{:S(2)}, u32[]{:S(2)}) async-start(bf16[64,56,128]{2,1,0:T(8,128)(2,1)} %shard_map.50), calls=%async_computation | async-start | bytes 1835008 | tf_op jit(solution)/shard_map/all_to_all | solution.py:274
  60.8 26.7 %collective-permute-start.9 = (bf16[10,2,80,128]{3,2,1,0:T(8,128)(2,1)}, bf16[10,2,80,128]{3,2,1,0:T(8,128)(2,1)S(1)}, u32[]{:S(2)}, u32[]{:S(2)}) collective-permute-start(bf16[10,2,80,128]{3,2,1,0:T(8,128)(2,1)} %copy-done.2), channel_id=1, source_target_pairs={{0,4},{4,8},{8,12},{12,0},{1,5},{5,9},{9,13},{13,1},{2,6},{6,10},{... | collective-permute-start | bytes 1228808 | tf_op jit(solution)/shard_map/ppermute | solution.py:221
  61.7 27.8 %collective-permute-start.11 = (bf16[10,2,80,128]{3,2,1,0:T(8,128)(2,1)}, bf16[10,2,80,128]{3,2,1,0:T(8,128)(2,1)}, u32[]{:S(2)}, u32[]{:S(2)}) collective-permute-start(bf16[10,2,80,128]{3,2,1,0:T(8,128)(2,1)} %copy-done.1), channel_id=1, source_target_pairs={{0,8},{4,12},{8,0},{12,4},{1,9},{5,13},{9,1},{13,5},{2,10},{6,14},... | collective-permute-start | bytes 1228808 | tf_op jit(solution)/shard_map/ppermute | solution.py:221
  64.8 25.3 %collective-permute-start.13 = (bf16[10,2,80,128]{3,2,1,0:T(8,128)(2,1)}, bf16[10,2,80,128]{3,2,1,0:T(8,128)(2,1)}, u32[]{:S(2)}, u32[]{:S(2)}) collective-permute-start(bf16[10,2,80,128]{3,2,1,0:T(8,128)(2,1)} %copy-done), channel_id=1, source_target_pairs={{0,12},{4,0},{8,4},{12,8},{1,13},{5,1},{9,5},{13,9},{2,14},{6,2},{... | collective-permute-start | bytes 1228808 | tf_op jit(solution)/shard_map/ppermute | solution.py:221
  68.5 21.9 %collective-permute-start.10 = (bf16[10,2,80,128]{3,2,1,0:T(8,128)(2,1)}, bf16[10,2,80,128]{3,2,1,0:T(8,128)(2,1)S(1)}, u32[]{:S(2)}, u32[]{:S(2)}) collective-permute-start(bf16[10,2,80,128]{3,2,1,0:T(8,128)(2,1)} %get-tuple-element.75), channel_id=1, source_target_pairs={{0,4},{4,8},{8,12},{12,0},{1,5},{5,9},{9,13},{13,1},{2,6},{6,10},{... | collective-permute-start | bytes 1228808 | tf_op jit(solution)/shard_map/ppermute | solution.py:221
  68.7 31.0 %collective-permute-start.12 = (bf16[10,2,80,128]{3,2,1,0:T(8,128)(2,1)}, bf16[10,2,80,128]{3,2,1,0:T(8,128)(2,1)S(1)}, u32[]{:S(2)}, u32[]{:S(2)}) collective-permute-start(bf16[10,2,80,128]{3,2,1,0:T(8,128)(2,1)} %get-tuple-element.74), channel_id=1, source_target_pairs={{0,8},{4,12},{8,0},{12,4},{1,9},{5,13},{9,1},{13,5},{2,10},{6,14},... | collective-permute-start | bytes 1228808 | tf_op jit(solution)/shard_map/ppermute | solution.py:221
  87.4 12.3 %collective-permute-start.14 = (bf16[10,2,80,128]{3,2,1,0:T(8,128)(2,1)}, bf16[10,2,80,128]{3,2,1,0:T(8,128)(2,1)S(1)}, u32[]{:S(2)}, u32[]{:S(2)}) collective-permute-start(bf16[10,2,80,128]{3,2,1,0:T(8,128)(2,1)} %get-tuple-element.73), channel_id=1, source_target_pairs={{0,12},{4,0},{8,4},{12,8},{1,13},{5,1},{9,5},{13,9},{2,14},{6,2},{... | collective-permute-start | bytes 1228808 | tf_op jit(solution)/shard_map/ppermute | solution.py:221
  89.5 20.1 %collective-permute-start.15 = (bf16[10,2,80,128]{3,2,1,0:T(8,128)(2,1)S(1)}, bf16[10,2,80,128]{3,2,1,0:T(8,128)(2,1)S(1)}, u32[]{:S(2)}, u32[]{:S(2)}) collective-permute-start(bf16[10,2,80,128]{3,2,1,0:T(8,128)(2,1)S(1)} %shard_map.51), channel_id=1, source_target_pairs={{0,2},{1,3},{2,0},{3,1},{4,6},{5,7},{6,4},{7,5},{8,10},{9,11},{10,... | collective-permute-start | bytes 1228808 | tf_op jit(solution)/shard_map/ppermute | solution.py:225
  111.9 5.1 %collective-permute-start.18 = (f32[2,64,128]{2,1,0:T(8,128)S(1)}, f32[2,64,128]{2,1,0:T(8,128)S(1)}, u32[]{:S(2)}, u32[]{:S(2)}) collective-permute-start(f32[2,64,128]{2,1,0:T(8,128)S(1)} %get-tuple-element.78), channel_id=1, source_target_pairs={{0,4},{4,8},{8,12},{12,0},{1,5},{5,9},{9,13},{13,1},{2,6},{6,10},{... | collective-permute-start | bytes 196616 | tf_op jit(solution)/shard_map/ppermute | solution.py:221
  112.0 5.0 %collective-permute-start.17 = (f32[2,64,128]{2,1,0:T(8,128)S(1)}, f32[2,64,128]{2,1,0:T(8,128)S(1)}, u32[]{:S(2)}, u32[]{:S(2)}) collective-permute-start(f32[2,64,128]{2,1,0:T(8,128)S(1)} %get-tuple-element.79), channel_id=1, source_target_pairs={{0,8},{4,12},{8,0},{12,4},{1,9},{5,13},{9,1},{13,5},{2,10},{6,14},... | collective-permute-start | bytes 196616 | tf_op jit(solution)/shard_map/ppermute | solution.py:221
  113.9 4.0 %collective-permute-start.16 = (f32[2,64,128]{2,1,0:T(8,128)S(1)}, f32[2,64,128]{2,1,0:T(8,128)S(1)}, u32[]{:S(2)}, u32[]{:S(2)}) collective-permute-start(f32[2,64,128]{2,1,0:T(8,128)S(1)} %get-tuple-element.77), channel_id=1, source_target_pairs={{0,12},{4,0},{8,4},{12,8},{1,13},{5,1},{9,5},{13,9},{2,14},{6,2},{... | collective-permute-start | bytes 196616 | tf_op jit(solution)/shard_map/ppermute | solution.py:221

commit v5 on v4

--- a/solution.py
+++ b/solution.py
@@ -196,12 +196,12 @@
 
 
 def contract_kernel(*refs):
-    left, (own_ref, other_ref), out_ref = refs[: 2 * X], refs[2 * X : 2 * X + 2], refs[2 * X + 2]
+    left, (own_ref, other_ref), out_refs = refs[: 2 * X], refs[2 * X : 2 * X + 2], refs[2 * X + 2 :]
     both = jnp.concatenate([own_ref[...], other_ref[...]], axis=1)
     for k in range(2 * X):
         total = lax.dot_general(left[k][...], both, (((0,), (0,)), ((), ())), preferred_element_type=jnp.float32)
         side = lax.rem(k + lax.axis_index("zb"), 2)
-        out_ref[k // 2, side] = total[:PAIRS, :LANES] + total[PAIRS:, LANES:]
+        out_refs[k // 2][side] = total[:PAIRS, :LANES] + total[PAIRS:, LANES:]
 
 
 def contract(left, right):
@@ -210,8 +210,8 @@
     return pl.pallas_call(
         contract_kernel,
         in_specs=[pl.BlockSpec(memory_space=pltpu.VMEM)] * (2 * X + 2),
-        out_specs=pl.BlockSpec(memory_space=pltpu.VMEM),
-        out_shape=jax.ShapeDtypeStruct((X, 2, PAIRS, LANES), jnp.float32),
+        out_specs=[pl.BlockSpec(memory_space=pltpu.VMEM)] * X,
+        out_shape=[jax.ShapeDtypeStruct((2, PAIRS, LANES), jnp.float32)] * X,
         compiler_params=pltpu.CompilerParams(vmem_limit_bytes=32 * 2**20),
         cost_estimate=cost(2 * 1024 * 1600 * 256, 5 * 2**20),
     )(*left, *right)

time: 136 us -> 136 us (level)
  no operation moved by 1% of the time
where the time goes in v5:
time: 136 us; the launch traced here: 135 us
  waiting for transfers between devices  52.9 us (39%)
  starting transfers between devices  31.8 us (23%)
  Pallas kernels  18.4 us (14%)
  blocking collectives  17 us (12%)
  local copies, waits for them, and re-layouts  8.63 us (6%)
  between operations  5.32 us (4%)
  other arithmetic  1.49 us (1%)
    ppermute x12, waiting for transfers between devices, shift_x(): return lax.ppermute(array, 'x', [(x, (x + k) % X) for x in range(X)])  26.1 us
    all_to_all x1, blocking collectives, local(): lax.all_to_all(total.reshape(2 * ROWS, PAIRS // ROWS, LANES), ('zb',) + R...  17 us
    all_to_all x1, waiting for transfers between devices, local(): spread = lax.all_to_all(message, ROW + Z, 0, 0, tiled=True)  16.8 us
    ppermute x12, starting transfers between devices, shift_x(): return lax.ppermute(array, 'x', [(x, (x + k) % X) for x in range(X)])  16.4 us
    all_to_all x1, starting transfers between devices, local(): spread = lax.all_to_all(message, ROW + Z, 0, 0, tiled=True)  13.2 us
    ppermute x2, waiting for transfers between devices, swap_zl(): return lax.ppermute(array, Z, [(z, z ^ bit) for z in range(ZL)])  9.88 us
    pallas_call x2, Pallas kernels, slice_panel(): pl.pallas_call(functools.partial(slice_kernel, steps), grid_spec=pltpu.Pr...  7.77 us
    unnamed x15, local copies, waits for them, and re-layouts  4.95 us
  transfers between devices with their start and end apart: 15, of which 7 were waited for; matrix products, arithmetic and copies ran while one was open for 5% of the time, Pallas kernels for 8%

profile of v5, /device:TPU:1, one launch (start us, length us, event | category | flops | bytes accessed | tf_op | source)
XLA Modules:
  0.0 135.5 jit_solution(11462971796640084302)
XLA Ops:
  0.0 4.7 %shard_map.46 = (bf16[10,64,640]{2,1,0:T(8,128)(2,1)}, bf16[10,64,640]{2,1,0:T(8,128)(2,1)}, bf16[10,64,640]{2,1,0:T(8,128)(2,1)S(1)}) custom-call(s32[2]{0:T(128)} %owners_ref.2, s32[2]{0:T(128)} %offsets_ref.3, bf16[96,40,640]{2,1,0:T(8,128)(2,1)} %integrals_ref.3), custom_call_target="tpu_custom_call" | custom-call | bytes 6553600 | tf_op jit(solution)/shard_map/pallas_call | solution.py:68
  4.7 2.1 %collective-permute-start.5 = (bf16[10,64,640]{2,1,0:T(8,128)(2,1)}, bf16[10,64,640]{2,1,0:T(8,128)(2,1)}, u32[]{:S(2)}, u32[]{:S(2)}) collective-permute-start(bf16[10,64,640]{2,1,0:T(8,128)(2,1)} %get-tuple-element.61), channel_id=1, source_target_pairs={{0,4},{4,8},{8,12},{12,0},{1,5},{5,9},{9,13},{13,1},{2,6},{6,10},{... | collective-permute-start | bytes 2457608 | tf_op jit(solution)/shard_map/ppermute | solution.py:221
  6.8 2.4 %collective-permute-start.6 = (bf16[10,64,640]{2,1,0:T(8,128)(2,1)}, bf16[10,64,640]{2,1,0:T(8,128)(2,1)}, u32[]{:S(2)}, u32[]{:S(2)}) collective-permute-start(bf16[10,64,640]{2,1,0:T(8,128)(2,1)} %get-tuple-element.63), channel_id=1, source_target_pairs={{0,8},{4,12},{8,0},{12,4},{1,9},{5,13},{9,1},{13,5},{2,10},{6,14},... | collective-permute-start | bytes 2457608 | tf_op jit(solution)/shard_map/ppermute | solution.py:221
  9.3 1.2 collective-permute-start.7
  10.4 2.7 %copy.7 = bf16[64,640,40]{1,0,2:T(8,128)(2,1)S(1)} copy(bf16[64,640,40]{1,2,0:T(8,128)(2,1)} %param.7) | data formatting | bytes 6553600 | tf_op args[0]
  13.1 0.1 pad_add_fusion.1
  13.2 2.4 %shard_map.49 = bf16[4,10,2,80,128]{4,3,2,1,0:T(8,128)(2,1)S(1)} custom-call(s32[3]{0:T(128)S(1)} %get-tuple-element.96.place_ref, bf16[40,64,640]{2,1,0:T(8,128)(2,1)S(1)} %bitcast.40, bf16[40,64,640]{2,1,0:T(8,128)(2,1)S(1)} %bitcast.41), custom_call_target="tpu_custom_call" | custom-call | bytes 3276800 | tf_op jit(solution)/shard_map/pallas_call | solution.py:149
  15.6 1.7 %collective-permute-start.8 = (bf16[4,10,2,80,128]{4,3,2,1,0:T(8,128)(2,1)S(1)}, bf16[4,10,2,80,128]{4,3,2,1,0:T(8,128)(2,1)}, u32[]{:S(2)}, u32[]{:S(2)}) collective-permute-start(bf16[4,10,2,80,128]{4,3,2,1,0:T(8,128)(2,1)S(1)} %shard_map.49), channel_id=1, source_target_pairs={{0,1},{1,0},{2,3},{3,2},{4,5},{5,4},{6,7},{7,6},{8,9},{9,8},{10,11... | collective-permute-start | bytes 4915208 | tf_op jit(solution)/shard_map/ppermute | solution.py:225
  17.3 3.1 %shard_map.47 = bf16[10,64,640]{2,1,0:T(8,128)(2,1)} custom-call(s32[2]{0:T(128)S(1)} %copy-done.4, s32[2]{0:T(128)S(1)} %copy-done.5, bf16[96,40,640]{2,1,0:T(8,128)(2,1)S(1)} %bitcast.55), custom_call_target="tpu_custom_call" | custom-call | bytes 6553600 | tf_op jit(solution)/shard_map/pallas_call | solution.py:68
  20.4 2.3 %shard_map.48 = (bf16[10,2,80,128]{3,2,1,0:T(8,128)(2,1)S(1)}, bf16[10,2,80,128]{3,2,1,0:T(8,128)(2,1)S(1)}, bf16[10,2,80,128]{3,2,1,0:T(8,128)(2,1)S(1)}, bf16[10,2,80,128]{3,2,1,0:T(8,128)(2,1)S(1)}) custom-call(s32[3]{0:T(128)S(1)} %get-tuple-element.95.place_ref, bf16[40,64,640]{2,1,0:T(8,128)(2,1)S(1)} %bitcast.42, bf16[40,64,640]{2,1,0:T(8,128)(2,1)S(1)} %bitcast.43), custom_call_target="tpu_custom_call" | custom-call | bytes 3276800 | tf_op jit(solution)/shard_map/pallas_call | solution.py:149
  22.7 0.7 copy-done
  23.5 0.8 copy-done.1
  24.2 0.8 copy-done.2
  25.0 0.7 fusion.1
  28.9 0.6 fusion
  31.5 0.0 collective-permute-done.5
  31.5 13.3 %collective-permute-done.6 = bf16[10,64,640]{2,1,0:T(8,128)(2,1)} collective-permute-done((bf16[10,64,640]{2,1,0:T(8,128)(2,1)}, bf16[10,64,640]{2,1,0:T(8,128)(2,1)}, u32[]{:S(2)}, u32[]{:S(2)}) %collective-permute-start.6) | collective-permute-done | bytes 819232 | tf_op jit(solution)/shard_map/ppermute | solution.py:221
  44.8 0.0 collective-permute-done.7
  44.8 2.8 %shard_map.50 = bf16[64,56,128]{2,1,0:T(8,128)(2,1)} custom-call(s32[1]{0:T(128)} %bitcast.25.choice_ref, bf16[5,128,640]{2,1,0:T(8,128)(2,1)} %bitcast.56, bf16[5,128,640]{2,1,0:T(8,128)(2,1)} %bitcast.27.refs_1_, bf16[5,128,640]{2,1,0:T(8,128)(2,1)} %bitcast.28.refs_2_, bf16[5,128,640]{2,1,0:T(8,128)(2,1)} %bitcast.29.refs_3_, ...), custom_call_target="tpu_custom_call" | custom-call | bytes 1638400 | tf_op jit(solution)/shard_map/pallas_call | solution.py:109
  47.6 13.2 %all-to-all-start = ((bf16[64,56,128]{2,1,0:T(8,128)(2,1)}), bf16[64,56,128]{2,1,0:T(8,128)(2,1)S(1)}, u32[]{:S(2)}, u32[]{:S(2)}) async-start(bf16[64,56,128]{2,1,0:T(8,128)(2,1)} %shard_map.50), calls=%async_computation | async-start | bytes 1835008 | tf_op jit(solution)/shard_map/all_to_all | solution.py:274
  60.8 0.9 collective-permute-start.9
  61.7 2.3 %collective-permute-start.11 = (bf16[10,2,80,128]{3,2,1,0:T(8,128)(2,1)}, bf16[10,2,80,128]{3,2,1,0:T(8,128)(2,1)}, u32[]{:S(2)}, u32[]{:S(2)}) collective-permute-start(bf16[10,2,80,128]{3,2,1,0:T(8,128)(2,1)} %copy-done.1), channel_id=1, source_target_pairs={{0,8},{4,12},{8,0},{12,4},{1,9},{5,13},{9,1},{13,5},{2,10},{6,14},... | collective-permute-start | bytes 1228808 | tf_op jit(solution)/shard_map/ppermute | solution.py:221
  64.0 0.8 pad_add_fusion.3.source_ref
  64.8 1.3 collective-permute-start.13
  66.1 0.0 collective-permute-done.8
  66.1 2.4 %slice_bitcast_fusion = (bf16[10,2,80,128]{3,2,1,0:T(8,128)(2,1)}, bf16[10,2,80,128]{3,2,1,0:T(8,128)(2,1)}, bf16[10,2,80,128]{3,2,1,0:T(8,128)(2,1)}, bf16[1,10,2,80,128]{4,3,2,1,0:T(8,128)(2,1)S(1)}) fusion(bf16[4,10,2,80,128]{4,3,2,1,0:T(8,128)(2,1)} %collective-permute-done.8), kind=kLoop, calls=%fused_computation.4 | loop fusion | bytes 3276800 | tf_op jit(solution)/shard_map/squeeze | solution.py:271
  68.5 0.2 collective-permute-start.10
  68.7 1.0 collective-permute-start.12
  69.7 16.8 %all-to-all-done = bf16[64,56,128]{2,1,0:T(8,128)(2,1)S(1)} async-done(((bf16[64,56,128]{2,1,0:T(8,128)(2,1)}), bf16[64,56,128]{2,1,0:T(8,128)(2,1)S(1)}, u32[]{:S(2)}, u32[]{:S(2)}) %all-to-all-start) | async-done | bytes 917536 | tf_op jit(solution)/shard_map/all_to_all | solution.py:274
  86.6 0.9 shard_map.51
  87.4 0.0 collective-permute-done.9
  87.4 2.1 %collective-permute-start.14 = (bf16[10,2,80,128]{3,2,1,0:T(8,128)(2,1)}, bf16[10,2,80,128]{3,2,1,0:T(8,128)(2,1)S(1)}, u32[]{:S(2)}, u32[]{:S(2)}) collective-permute-start(bf16[10,2,80,128]{3,2,1,0:T(8,128)(2,1)} %get-tuple-element.81), channel_id=1, source_target_pairs={{0,12},{4,0},{8,4},{12,8},{1,13},{5,1},{9,5},{13,9},{2,14},{6,2},{... | collective-permute-start | bytes 1228808 | tf_op jit(solution)/shard_map/ppermute | solution.py:221
  89.5 0.0 collective-permute-done.11
  89.5 0.5 collective-permute-start.15
  90.1 0.0 collective-permute-done.13
  90.1 0.4 collective-permute-done.10
  90.4 9.3 %collective-permute-done.12 = bf16[10,2,80,128]{3,2,1,0:T(8,128)(2,1)S(1)} collective-permute-done((bf16[10,2,80,128]{3,2,1,0:T(8,128)(2,1)}, bf16[10,2,80,128]{3,2,1,0:T(8,128)(2,1)S(1)}, u32[]{:S(2)}, u32[]{:S(2)}) %collective-permute-start.12) | collective-permute-done | bytes 409632 | tf_op jit(solution)/shard_map/ppermute | solution.py:221
  99.7 0.0 collective-permute-done.14
  99.7 9.9 %collective-permute-done.15 = bf16[10,2,80,128]{3,2,1,0:T(8,128)(2,1)S(1)} collective-permute-done((bf16[10,2,80,128]{3,2,1,0:T(8,128)(2,1)S(1)}, bf16[10,2,80,128]{3,2,1,0:T(8,128)(2,1)S(1)}, u32[]{:S(2)}, u32[]{:S(2)}) %collective-permute-start.15) | collective-permute-done | bytes 409632 | tf_op jit(solution)/shard_map/ppermute | solution.py:225
  109.6 2.3 %shard_map.52 = (f32[2,64,128]{2,1,0:T(8,128)S(1)}, f32[2,64,128]{2,1,0:T(8,128)S(1)}, f32[2,64,128]{2,1,0:T(8,128)S(1)}, f32[2,64,128]{2,1,0:T(8,128)S(1)}) custom-call(bf16[1600,128]{1,0:T(8,128)(2,1)S(1)} %bitcast.48, bf16[1600,128]{1,0:T(8,128)(2,1)S(1)} %bitcast.46, bf16[1600,128]{1,0:T(8,128)(2,1)S(1)} %bitcast.49, bf16[1600,128]{1,0:T(8,128)(2,1)S(1)} %bitcast.50, ...), custom_call_target="tpu_custom_call" | custom-call | flops 838860800 | bytes 5242880 | tf_op jit(solution)/shard_map/pallas_call | solution.py:210
  111.9 0.1 collective-permute-start.18
  112.0 1.9 %collective-permute-start.17 = (f32[2,64,128]{2,1,0:T(8,128)S(1)}, f32[2,64,128]{2,1,0:T(8,128)S(1)}, u32[]{:S(2)}, u32[]{:S(2)}) collective-permute-start(f32[2,64,128]{2,1,0:T(8,128)S(1)} %get-tuple-element.79), channel_id=1, source_target_pairs={{0,8},{4,12},{8,0},{12,4},{1,9},{5,13},{9,1},{13,5},{2,10},{6,14},... | collective-permute-start | bytes 196616 | tf_op jit(solution)/shard_map/ppermute | solution.py:221
  113.9 0.8 collective-permute-start.16
  114.7 2.3 %collective-permute-done.18 = f32[2,64,128]{2,1,0:T(8,128)S(1)} collective-permute-done((f32[2,64,128]{2,1,0:T(8,128)S(1)}, f32[2,64,128]{2,1,0:T(8,128)S(1)}, u32[]{:S(2)}, u32[]{:S(2)}) %collective-permute-start.18) | collective-permute-done | bytes 65568 | tf_op jit(solution)/shard_map/ppermute | solution.py:221
  117.0 0.0 collective-permute-done.17
  117.0 0.9 collective-permute-done.16
  117.9 17.0 %all_to_all.10 = f32[32,4,128]{2,1,0:T(4,128)S(1)} all-to-all(f32[32,4,128]{2,1,0:T(4,128)S(1)} %bitcast.57), channel_id=1, replica_groups=mesh['zh'=2,'y'=4,'core'=2,'x'=4,'za'=2,'zb'=2] {'zb','zh','y','core'}, dimensions={0} | all-to-all | bytes 131072 | tf_op jit(solution)/shard_map/all_to_all | solution.py:281
  134.9 0.6 reduce_sum.9
  (16 shorter events, 0.0 us)
Async XLA Ops:
  4.7 26.8 %collective-permute-start.5 = (bf16[10,64,640]{2,1,0:T(8,128)(2,1)}, bf16[10,64,640]{2,1,0:T(8,128)(2,1)}, u32[]{:S(2)}, u32[]{:S(2)}) collective-permute-start(bf16[10,64,640]{2,1,0:T(8,128)(2,1)} %get-tuple-element.61), channel_id=1, source_target_pairs={{0,4},{4,8},{8,12},{12,0},{1,5},{5,9},{9,13},{13,1},{2,6},{6,10},{... | collective-permute-start | bytes 2457608 | tf_op jit(solution)/shard_map/ppermute | solution.py:221
  6.8 38.0 %collective-permute-start.6 = (bf16[10,64,640]{2,1,0:T(8,128)(2,1)}, bf16[10,64,640]{2,1,0:T(8,128)(2,1)}, u32[]{:S(2)}, u32[]{:S(2)}) collective-permute-start(bf16[10,64,640]{2,1,0:T(8,128)(2,1)} %get-tuple-element.63), channel_id=1, source_target_pairs={{0,8},{4,12},{8,0},{12,4},{1,9},{5,13},{9,1},{13,5},{2,10},{6,14},... | collective-permute-start | bytes 2457608 | tf_op jit(solution)/shard_map/ppermute | solution.py:221
  9.3 35.5 %collective-permute-start.7 = (bf16[10,64,640]{2,1,0:T(8,128)(2,1)S(1)}, bf16[10,64,640]{2,1,0:T(8,128)(2,1)}, u32[]{:S(2)}, u32[]{:S(2)}) collective-permute-start(bf16[10,64,640]{2,1,0:T(8,128)(2,1)S(1)} %get-tuple-element.64), channel_id=1, source_target_pairs={{0,12},{4,0},{8,4},{12,8},{1,13},{5,1},{9,5},{13,9},{2,14},{6,2},{... | collective-permute-start | bytes 2457608 | tf_op jit(solution)/shard_map/ppermute | solution.py:221
  10.4 6.9 %slice-start = ((s8[4915200]{0:T(1024)(128)(4,1)}), s8[4194304]{0:T(1024)(128)(4,1)S(1)}, s32[]{:S(2)}) async-start(s8[4915200]{0:T(1024)(128)(4,1)} %bitcast.54), calls=%async_computation.2 | async-start | bytes 8388608
  13.2 4.2 %slice-start.1 = ((s8[4915200]{0:T(1024)(128)(4,1)}), s8[720896]{0:T(1024)(128)(4,1)S(1)}, s32[]{:S(2)}) async-start(s8[4915200]{0:T(1024)(128)(4,1)} %bitcast.54), calls=%async_computation.3 | async-start | bytes 1441792
  13.2 4.2 %copy-start.4 = (s32[2]{0:T(128)S(1)}, s32[2]{0:T(128)}, u32[]{:S(2)}) copy-start(s32[2]{0:T(128)} %owners_ref.2) | copy-start | bytes 28
  13.2 4.2 %copy-start.5 = (s32[2]{0:T(128)S(1)}, s32[2]{0:T(128)}, u32[]{:S(2)}) copy-start(s32[2]{0:T(128)} %offsets_ref.3) | copy-start | bytes 28
  15.6 50.5 %collective-permute-start.8 = (bf16[4,10,2,80,128]{4,3,2,1,0:T(8,128)(2,1)S(1)}, bf16[4,10,2,80,128]{4,3,2,1,0:T(8,128)(2,1)}, u32[]{:S(2)}, u32[]{:S(2)}) collective-permute-start(bf16[4,10,2,80,128]{4,3,2,1,0:T(8,128)(2,1)S(1)} %shard_map.49), channel_id=1, source_target_pairs={{0,1},{1,0},{2,3},{3,2},{4,5},{5,4},{6,7},{7,6},{8,9},{9,8},{10,11... | collective-permute-start | bytes 4915208 | tf_op jit(solution)/shard_map/ppermute | solution.py:225
  22.7 0.8 copy-start
  23.5 0.8 copy-start.1
  24.2 0.8 copy-start.2
  47.6 39.0 %all-to-all-start = ((bf16[64,56,128]{2,1,0:T(8,128)(2,1)}), bf16[64,56,128]{2,1,0:T(8,128)(2,1)S(1)}, u32[]{:S(2)}, u32[]{:S(2)}) async-start(bf16[64,56,128]{2,1,0:T(8,128)(2,1)} %shard_map.50), calls=%async_computation | async-start | bytes 1835008 | tf_op jit(solution)/shard_map/all_to_all | solution.py:274
  60.8 26.7 %collective-permute-start.9 = (bf16[10,2,80,128]{3,2,1,0:T(8,128)(2,1)}, bf16[10,2,80,128]{3,2,1,0:T(8,128)(2,1)S(1)}, u32[]{:S(2)}, u32[]{:S(2)}) collective-permute-start(bf16[10,2,80,128]{3,2,1,0:T(8,128)(2,1)} %copy-done.2), channel_id=1, source_target_pairs={{0,4},{4,8},{8,12},{12,0},{1,5},{5,9},{9,13},{13,1},{2,6},{6,10},{... | collective-permute-start | bytes 1228808 | tf_op jit(solution)/shard_map/ppermute | solution.py:221
  61.7 27.8 %collective-permute-start.11 = (bf16[10,2,80,128]{3,2,1,0:T(8,128)(2,1)}, bf16[10,2,80,128]{3,2,1,0:T(8,128)(2,1)}, u32[]{:S(2)}, u32[]{:S(2)}) collective-permute-start(bf16[10,2,80,128]{3,2,1,0:T(8,128)(2,1)} %copy-done.1), channel_id=1, source_target_pairs={{0,8},{4,12},{8,0},{12,4},{1,9},{5,13},{9,1},{13,5},{2,10},{6,14},... | collective-permute-start | bytes 1228808 | tf_op jit(solution)/shard_map/ppermute | solution.py:221
  64.8 25.3 %collective-permute-start.13 = (bf16[10,2,80,128]{3,2,1,0:T(8,128)(2,1)}, bf16[10,2,80,128]{3,2,1,0:T(8,128)(2,1)}, u32[]{:S(2)}, u32[]{:S(2)}) collective-permute-start(bf16[10,2,80,128]{3,2,1,0:T(8,128)(2,1)} %copy-done), channel_id=1, source_target_pairs={{0,12},{4,0},{8,4},{12,8},{1,13},{5,1},{9,5},{13,9},{2,14},{6,2},{... | collective-permute-start | bytes 1228808 | tf_op jit(solution)/shard_map/ppermute | solution.py:221
  68.5 21.9 %collective-permute-start.10 = (bf16[10,2,80,128]{3,2,1,0:T(8,128)(2,1)}, bf16[10,2,80,128]{3,2,1,0:T(8,128)(2,1)S(1)}, u32[]{:S(2)}, u32[]{:S(2)}) collective-permute-start(bf16[10,2,80,128]{3,2,1,0:T(8,128)(2,1)} %get-tuple-element.83), channel_id=1, source_target_pairs={{0,4},{4,8},{8,12},{12,0},{1,5},{5,9},{9,13},{13,1},{2,6},{6,10},{... | collective-permute-start | bytes 1228808 | tf_op jit(solution)/shard_map/ppermute | solution.py:221
  68.7 31.0 %collective-permute-start.12 = (bf16[10,2,80,128]{3,2,1,0:T(8,128)(2,1)}, bf16[10,2,80,128]{3,2,1,0:T(8,128)(2,1)S(1)}, u32[]{:S(2)}, u32[]{:S(2)}) collective-permute-start(bf16[10,2,80,128]{3,2,1,0:T(8,128)(2,1)} %get-tuple-element.82), channel_id=1, source_target_pairs={{0,8},{4,12},{8,0},{12,4},{1,9},{5,13},{9,1},{13,5},{2,10},{6,14},... | collective-permute-start | bytes 1228808 | tf_op jit(solution)/shard_map/ppermute | solution.py:221
  87.4 12.3 %collective-permute-start.14 = (bf16[10,2,80,128]{3,2,1,0:T(8,128)(2,1)}, bf16[10,2,80,128]{3,2,1,0:T(8,128)(2,1)S(1)}, u32[]{:S(2)}, u32[]{:S(2)}) collective-permute-start(bf16[10,2,80,128]{3,2,1,0:T(8,128)(2,1)} %get-tuple-element.81), channel_id=1, source_target_pairs={{0,12},{4,0},{8,4},{12,8},{1,13},{5,1},{9,5},{13,9},{2,14},{6,2},{... | collective-permute-start | bytes 1228808 | tf_op jit(solution)/shard_map/ppermute | solution.py:221
  89.5 20.1 %collective-permute-start.15 = (bf16[10,2,80,128]{3,2,1,0:T(8,128)(2,1)S(1)}, bf16[10,2,80,128]{3,2,1,0:T(8,128)(2,1)S(1)}, u32[]{:S(2)}, u32[]{:S(2)}) collective-permute-start(bf16[10,2,80,128]{3,2,1,0:T(8,128)(2,1)S(1)} %shard_map.51), channel_id=1, source_target_pairs={{0,2},{1,3},{2,0},{3,1},{4,6},{5,7},{6,4},{7,5},{8,10},{9,11},{10,... | collective-permute-start | bytes 1228808 | tf_op jit(solution)/shard_map/ppermute | solution.py:225
  111.9 5.1 %collective-permute-start.18 = (f32[2,64,128]{2,1,0:T(8,128)S(1)}, f32[2,64,128]{2,1,0:T(8,128)S(1)}, u32[]{:S(2)}, u32[]{:S(2)}) collective-permute-start(f32[2,64,128]{2,1,0:T(8,128)S(1)} %get-tuple-element.80), channel_id=1, source_target_pairs={{0,4},{4,8},{8,12},{12,0},{1,5},{5,9},{9,13},{13,1},{2,6},{6,10},{... | collective-permute-start | bytes 196616 | tf_op jit(solution)/shard_map/ppermute | solution.py:221
  112.0 5.0 %collective-permute-start.17 = (f32[2,64,128]{2,1,0:T(8,128)S(1)}, f32[2,64,128]{2,1,0:T(8,128)S(1)}, u32[]{:S(2)}, u32[]{:S(2)}) collective-permute-start(f32[2,64,128]{2,1,0:T(8,128)S(1)} %get-tuple-element.79), channel_id=1, source_target_pairs={{0,8},{4,12},{8,0},{12,4},{1,9},{5,13},{9,1},{13,5},{2,10},{6,14},... | collective-permute-start | bytes 196616 | tf_op jit(solution)/shard_map/ppermute | solution.py:221
  113.9 4.0 %collective-permute-start.16 = (f32[2,64,128]{2,1,0:T(8,128)S(1)}, f32[2,64,128]{2,1,0:T(8,128)S(1)}, u32[]{:S(2)}, u32[]{:S(2)}) collective-permute-start(f32[2,64,128]{2,1,0:T(8,128)S(1)} %get-tuple-element.78), channel_id=1, source_target_pairs={{0,12},{4,0},{8,4},{12,8},{1,13},{5,1},{9,5},{13,9},{2,14},{6,2},{... | collective-permute-start | bytes 196616 | tf_op jit(solution)/shard_map/ppermute | solution.py:221
